TPU v7x, 32 devices: a whole 2x2x4 slice. The times are simulated.
32 devices in a mesh: fsdp: 2 (over x), ctx: 4 (over z), head: 4 (over y, core).
Axes of the slice: x: 2, y: 2, z: 4, core: 2. Of those that a mesh axis runs over, the one named last changes fastest.
Arguments:
- tokens: bfloat16 [4096, 2304], P(('fsdp', 'ctx', 'head')), may hold values from -6 to 6
- positions: int32 [4096], P('fsdp'), may hold values from 0 to 2047, as said below
- cotangent: bfloat16 [4096, 2304], P(('fsdp', 'ctx', 'head')), may hold values from -6 to 6
- qkv_weight: float32 [2304, 4096], P(('fsdp', 'ctx', 'head')), may hold values from -0.125 to 0.125
- qkv_first: float32 [2304, 4096], P(('fsdp', 'ctx', 'head'))
- qkv_second: float32 [2304, 4096], P(('fsdp', 'ctx', 'head')), as said below
- out_weight: float32 [2048, 2304], P(('fsdp', 'ctx', 'head')), may hold values from -0.125 to 0.125
- out_first: float32 [2048, 2304], P(('fsdp', 'ctx', 'head'))
- out_second: float32 [2048, 2304], P(('fsdp', 'ctx', 'head')), as said below
- gate_up: float32 [2, 2304, 9216], P(None, ('fsdp', 'ctx'), 'head'), may hold values from -0.125 to 0.125
- gate_up_first: float32 [2, 2304, 9216], P(None, ('fsdp', 'ctx'), 'head')
- gate_up_second: float32 [2, 2304, 9216], P(None, ('fsdp', 'ctx'), 'head'), as said below
- down_weight: float32 [9216, 2304], P('head', ('fsdp', 'ctx')), may hold values from -0.0625 to 0.0625
- down_first: float32 [9216, 2304], P('head', ('fsdp', 'ctx'))
- down_second: float32 [9216, 2304], P('head', ('fsdp', 'ctx')), as said below
- gains: float32 [2304, 4], P(('fsdp', 'ctx', 'head')), may hold values from -0.6 to 0.6
- gains_first: float32 [2304, 4], P(('fsdp', 'ctx', 'head'))
- gains_second: float32 [2304, 4], P(('fsdp', 'ctx', 'head')), as said below
Outputs:
- mixed_out: bfloat16 [4096, 2304], P(('fsdp', 'ctx', 'head'))
- tokens_grad: bfloat16 [4096, 2304], P(('fsdp', 'ctx', 'head'))
- qkv_grad: float32 [2304, 4096], P(('fsdp', 'ctx', 'head'))
- qkv_first_new: float32 [2304, 4096], P(('fsdp', 'ctx', 'head'))
- qkv_second_new: float32 [2304, 4096], P(('fsdp', 'ctx', 'head'))
- qkv_new: float32 [2304, 4096], P(('fsdp', 'ctx', 'head'))
- out_grad: float32 [2048, 2304], P(('fsdp', 'ctx', 'head'))
- out_first_new: float32 [2048, 2304], P(('fsdp', 'ctx', 'head'))
- out_second_new: float32 [2048, 2304], P(('fsdp', 'ctx', 'head'))
- out_new: float32 [2048, 2304], P(('fsdp', 'ctx', 'head'))
- gate_up_grad: float32 [2, 2304, 9216], P(None, ('fsdp', 'ctx'), 'head')
- gate_up_first_new: float32 [2, 2304, 9216], P(None, ('fsdp', 'ctx'), 'head')
- gate_up_second_new: float32 [2, 2304, 9216], P(None, ('fsdp', 'ctx'), 'head')
- gate_up_new: float32 [2, 2304, 9216], P(None, ('fsdp', 'ctx'), 'head')
- down_grad: float32 [9216, 2304], P('head', ('fsdp', 'ctx'))
- down_first_new: float32 [9216, 2304], P('head', ('fsdp', 'ctx'))
- down_second_new: float32 [9216, 2304], P('head', ('fsdp', 'ctx'))
- down_new: float32 [9216, 2304], P('head', ('fsdp', 'ctx'))
- gains_grad: float32 [2304, 4], P(('fsdp', 'ctx', 'head'))
- gains_first_new: float32 [2304, 4], P(('fsdp', 'ctx', 'head'))
- gains_second_new: float32 [2304, 4], P(('fsdp', 'ctx', 'head'))
- gains_new: float32 [2304, 4], P(('fsdp', 'ctx', 'head'))
Inputs may be any that keep to these rules, and one draw needn't show every extreme that they name: Rows s * 2048 to (s + 1) * 2048 - 1 are sequence s and hold each position 0 to 2047 once; each aligned block of 512 rows holds either one run of consecutive rising positions or two such runs of 256. `qkv_second`: positive. `out_second`: positive. `gate_up_second`: positive. `down_second`: positive. `gains_second`: positive.
All inputs are finite; a program needn't handle non-finite values.
Results may differ from a plain program's by a relative error of at most 0.023.
Values may be sent and summed in bfloat16 or wider, within the bound.
No kernel may reach another device: no remote copies, remote signals or barrier semaphores. Data moves between devices by JAX's collectives and lax.ppermute only.
A program may use at most 384 MiB of HBM per device.

v0:
```python
import math

import jax
import jax.numpy as jnp
from jax import lax
from jax.sharding import PartitionSpec as P

QH = 8
KVH = 4
HD = 256
STEP = 10


SOFT_CAP = 50.0
EPS_NORM = 1e-06
ROPE_BASE = 10000.0
BETA_ONE = 0.9
BETA_TWO = 0.95
EPS_ADAM = 1e-08
RATE_MATRIX = 0.05
RATE_DOWN = 0.025
RATE_GAIN = 0.5
WEIGHT_DECAY = 0.1


def fetch_params(qkv_weight, out_weight, gains, gate_up, down_weight):
    attn_set = (
        lax.all_gather(
            qkv_weight.astype(jnp.bfloat16), ("fsdp", "ctx", "head"), axis=0, tiled=True
        ),
        lax.all_gather(
            out_weight.astype(jnp.bfloat16), ("fsdp", "ctx", "head"), axis=0, tiled=True
        ),
        lax.all_gather(gains.astype(jnp.bfloat16), ("fsdp", "ctx", "head"), axis=0, tiled=True),
    )
    ffn_set = (
        lax.all_gather(gate_up.astype(jnp.bfloat16), ("fsdp", "ctx"), axis=1, tiled=True),
        lax.all_gather(down_weight.astype(jnp.bfloat16), ("fsdp", "ctx"), axis=1, tiled=True),
    )
    return (attn_set, ffn_set)


def rms_norm(values, gain_col):
    inv_scale = lax.rsqrt(jnp.mean(values * values, axis=-1, keepdims=True) + EPS_NORM)
    return values * inv_scale * (1.0 + gain_col)


def norm_back(values, gain_col, upstream):
    inv_scale = lax.rsqrt(jnp.mean(values * values, axis=-1, keepdims=True) + EPS_NORM)
    unit_rows = values * inv_scale
    scaled = upstream * (1.0 + gain_col)
    result = inv_scale * (scaled - unit_rows * jnp.mean(scaled * unit_rows, axis=-1, keepdims=True))
    return (result, upstream * unit_rows)


def rope_tables(position, half_dim):
    freq_table = ROPE_BASE ** (-(jnp.arange(half_dim, dtype=jnp.float32) * 2.0 / (2 * half_dim)))
    angle_table = position.astype(jnp.float32)[:, None] * freq_table[None, :]
    return (jnp.cos(angle_table)[:, None, :], jnp.sin(angle_table)[:, None, :])


def rope_turn(values, cosine, sine_table):
    half_dim = values.shape[-1] // 2
    lead_half = values[..., :half_dim]
    tail_half = values[..., half_dim:]
    return jnp.concatenate(
        [lead_half * cosine - tail_half * sine_table, tail_half * cosine + lead_half * sine_table],
        axis=-1,
    )


def rope_back(grad_rows, cosine, sine_table):
    half_dim = grad_rows.shape[-1] // 2
    lead_half = grad_rows[..., :half_dim]
    tail_half = grad_rows[..., half_dim:]
    return jnp.concatenate(
        [lead_half * cosine + tail_half * sine_table, tail_half * cosine - lead_half * sine_table],
        axis=-1,
    )


def capped_scores(query_grouped, key_block, query_pos, key_pos):
    scores = jnp.einsum(
        "qkgd,rkd->kgqr", query_grouped, key_block, preferred_element_type=jnp.float32
    )
    capped = SOFT_CAP * jnp.tanh(scores / SOFT_CAP)
    allowed = key_pos[None, None, None, :] <= query_pos[None, None, :, None]
    return (capped, jnp.where(allowed, jnp.exp(capped), 0.0))


def gated_unit(gate_in, up_in):
    return jax.nn.gelu(gate_in, approximate=True) * up_in


def adam_step(weight, first_old, second_old, gradient, step_rate, decay_rate):
    first_new = BETA_ONE * first_old + (1.0 - BETA_ONE) * gradient
    second_new = BETA_TWO * second_old + (1.0 - BETA_TWO) * gradient * gradient
    first_hat = first_new / (1.0 - BETA_ONE**STEP)
    second_hat = second_new / (1.0 - BETA_TWO**STEP)
    weight_new = weight - step_rate * (
        first_hat / (jnp.sqrt(second_hat) + EPS_ADAM) + decay_rate * weight
    )
    return (first_new, second_new, weight_new)


def shards(
    tokens,
    positions,
    cotangent,
    qkv_weight,
    qkv_first,
    qkv_second,
    out_weight,
    out_first,
    out_second,
    gate_up,
    gate_up_first,
    gate_up_second,
    down_weight,
    down_first,
    down_second,
    gains,
    gains_first,
    gains_second,
):
    head_count = lax.axis_size("head")
    tok_rows = tokens.shape[0]
    block_rows = tok_rows * head_count
    seq_len = positions.shape[0]
    ctx_index = lax.axis_index("ctx")
    head_index = lax.axis_index("head")
    block_pos = lax.dynamic_slice_in_dim(positions, ctx_index * block_rows, block_rows)
    own_pos = lax.dynamic_slice_in_dim(block_pos, head_index * tok_rows, tok_rows)
    copies = max(1, head_count // KVH)
    query_scale = 1.0 / math.sqrt(HD)
    attn_set, ffn_set = fetch_params(qkv_weight, out_weight, gains, gate_up, down_weight)
    qkv_low, out_low, gains_low = attn_set
    gate_up_low, down_low = ffn_set
    gain_cols = gains_low.astype(jnp.float32)
    inputs = tokens.astype(jnp.float32)
    first_normed = rms_norm(inputs, gain_cols[:, 0]).astype(jnp.bfloat16)
    projected = jnp.dot(first_normed, qkv_low, preferred_element_type=jnp.float32)
    cosine, sine_table = rope_tables(own_pos, HD // 2)
    queries = (
        rope_turn(projected[:, : QH * HD].reshape(tok_rows, QH, HD), cosine, sine_table)
        * query_scale
    )
    key_rot = rope_turn(
        projected[:, QH * HD : (QH + KVH) * HD].reshape(tok_rows, KVH, HD), cosine, sine_table
    )
    values = projected[:, (QH + KVH) * HD :].reshape(tok_rows, KVH, HD)
    key_copies = jnp.repeat(key_rot.astype(jnp.bfloat16), copies, axis=1)
    value_copies = jnp.repeat(values.astype(jnp.bfloat16), copies, axis=1)
    query_heads, key_heads, value_heads = (
        lax.all_to_all(
            queries.astype(jnp.bfloat16), "head", split_axis=1, concat_axis=0, tiled=True
        ),
        lax.all_to_all(key_copies, "head", split_axis=1, concat_axis=0, tiled=True),
        lax.all_to_all(value_copies, "head", split_axis=1, concat_axis=0, tiled=True),
    )
    kv_local = key_heads.shape[1]
    query_local = query_heads.shape[1]
    group_size = query_local // kv_local
    query_grouped = query_heads.reshape(block_rows, kv_local, group_size, HD)
    fold_init = (
        jnp.zeros((kv_local, group_size, block_rows), jnp.float32),
        jnp.zeros((block_rows, kv_local, group_size, HD), jnp.float32),
    )
    fold_state = fold_init
    key_piece = lax.all_gather(key_heads, "ctx", axis=0, tiled=True)
    value_piece = lax.all_gather(value_heads, "ctx", axis=0, tiled=True)
    piece_rows = key_piece.shape[0]
    block_size = math.gcd(piece_rows, block_rows)
    block_count = piece_rows // block_size
    key_blocks = key_piece.reshape((block_count, block_size) + key_piece.shape[1:])
    value_blocks = value_piece.reshape((block_count, block_size) + value_piece.shape[1:])
    pos_blocks = positions.reshape(block_count, block_size)

    def fold_block_step(scan_state, block_item):
        exp_total, summed = scan_state
        key_block, value_block, key_pos = block_item
        capped, exp_scores = capped_scores(query_grouped, key_block, block_pos, key_pos)
        exp_total = exp_total + jnp.sum(exp_scores, axis=-1)
        summed = summed + jnp.einsum(
            "kgqr,rkd->qkgd",
            exp_scores.astype(jnp.bfloat16),
            value_block,
            preferred_element_type=jnp.float32,
        )
        return ((exp_total, summed), None)

    fold_state, unused = lax.scan(
        fold_block_step, fold_state, (key_blocks, value_blocks, pos_blocks)
    )
    exp_total, summed = fold_state
    total_rows = jnp.transpose(exp_total, (2, 0, 1))[..., None]
    attended = summed / total_rows
    attended_low = attended.astype(jnp.bfloat16).reshape(block_rows, query_local, HD)
    gathered_heads = lax.all_to_all(attended_low, "head", split_axis=0, concat_axis=1, tiled=True)
    flat_heads = gathered_heads.reshape(tok_rows, QH * HD)
    attn_out = jnp.dot(flat_heads, out_low, preferred_element_type=jnp.float32)
    middle = inputs + rms_norm(attn_out, gain_cols[:, 1])
    second_normed = rms_norm(middle, gain_cols[:, 2]).astype(jnp.bfloat16)
    block_normed, block_cotangent = (
        lax.all_gather(second_normed, "head", axis=0, tiled=True),
        lax.all_gather(cotangent, "head", axis=0, tiled=True),
    )
    gate_up_act = jnp.einsum(
        "md,kdf->kmf", block_normed, gate_up_low, preferred_element_type=jnp.float32
    )
    gate_act = gate_up_act[0]
    up_act = gate_up_act[1]
    hidden_low = gated_unit(gate_act, up_act).astype(jnp.bfloat16)
    ffn_part = jnp.dot(hidden_low, down_low, preferred_element_type=jnp.float32)
    ffn_out = lax.psum(ffn_part.astype(jnp.bfloat16), "head").astype(jnp.float32)
    own_ffn = lax.dynamic_slice_in_dim(ffn_out, head_index * tok_rows, tok_rows)
    mixed_out = (middle + rms_norm(own_ffn, gain_cols[:, 3])).astype(jnp.bfloat16)
    attn_set, ffn_set = fetch_params(qkv_weight, out_weight, gains, gate_up, down_weight)
    qkv_low, out_low, gains_low = attn_set
    gate_up_low, down_low = ffn_set
    upstream_block = block_cotangent.astype(jnp.float32)
    grad_ffn, ffn_gain_rows = norm_back(ffn_out, gain_cols[:, 3], upstream_block)
    ffn_gain_term = jnp.sum(
        lax.dynamic_slice_in_dim(ffn_gain_rows, head_index * tok_rows, tok_rows), axis=0
    )
    grad_ffn_low = grad_ffn.astype(jnp.bfloat16)
    down_term = jnp.einsum(
        "mf,md->fd", hidden_low, grad_ffn_low, preferred_element_type=jnp.float32
    )
    grad_hidden = jnp.einsum(
        "md,fd->mf", grad_ffn_low, down_low, preferred_element_type=jnp.float32
    )
    unit_out, unit_back = jax.vjp(gated_unit, gate_act, up_act)
    grad_gate, grad_up = unit_back(grad_hidden)
    grad_gate_up = jnp.stack([grad_gate, grad_up]).astype(jnp.bfloat16)
    gate_up_term = jnp.einsum(
        "md,kmf->kdf", block_normed, grad_gate_up, preferred_element_type=jnp.float32
    )
    grad_second_part = jnp.einsum(
        "kmf,kdf->md", grad_gate_up, gate_up_low, preferred_element_type=jnp.float32
    )
    grad_second = lax.psum_scatter(
        grad_second_part.astype(jnp.bfloat16), "head", scatter_dimension=0, tiled=True
    ).astype(jnp.float32)
    upstream = cotangent.astype(jnp.float32)
    grad_middle_part, mid_gain_rows = norm_back(middle, gain_cols[:, 2], grad_second)
    grad_middle = upstream + grad_middle_part
    grad_attn, attn_gain_rows = norm_back(attn_out, gain_cols[:, 1], grad_middle)
    grad_attn_low = grad_attn.astype(jnp.bfloat16)
    grad_flat = jnp.einsum("td,id->ti", grad_attn_low, out_low, preferred_element_type=jnp.float32)
    grad_flat = grad_flat.astype(jnp.bfloat16).reshape(tok_rows, QH, HD)
    grad_heads = lax.all_to_all(grad_flat, "head", split_axis=1, concat_axis=0, tiled=True)
    grad_grouped = grad_heads.astype(jnp.float32).reshape(block_rows, kv_local, group_size, HD)
    row_delta = jnp.sum(grad_grouped * attended, axis=-1)
    delta_scaled = jnp.transpose(row_delta, (1, 2, 0)) / exp_total
    grad_summed = (grad_grouped / total_rows).astype(jnp.bfloat16)
    back_init = (
        jnp.zeros((block_rows, kv_local, group_size, HD), jnp.float32),
        jnp.zeros((seq_len, kv_local, HD), jnp.float32),
        jnp.zeros((seq_len, kv_local, HD), jnp.float32),
    )
    fold_state = back_init
    key_piece = lax.all_gather(key_heads, "ctx", axis=0, tiled=True)
    value_piece = lax.all_gather(value_heads, "ctx", axis=0, tiled=True)
    piece_rows = key_piece.shape[0]
    block_size = math.gcd(piece_rows, block_rows)
    block_count = piece_rows // block_size
    key_blocks = key_piece.reshape((block_count, block_size) + key_piece.shape[1:])
    value_blocks = value_piece.reshape((block_count, block_size) + value_piece.shape[1:])
    pos_blocks = positions.reshape(block_count, block_size)
    row_starts = jnp.arange(block_count, dtype=jnp.int32) * block_size

    def back_block_step(scan_state, block_item):
        grad_query_acc, grad_key_all, grad_value_all = scan_state
        key_block, value_block, key_pos, offset_row = block_item
        capped, exp_scores = capped_scores(query_grouped, key_block, block_pos, key_pos)
        grad_weights = jnp.einsum(
            "qkgd,rkd->kgqr", grad_summed, value_block, preferred_element_type=jnp.float32
        )
        grad_scores = (
            exp_scores * (grad_weights - delta_scaled[..., None]) * (1.0 - (capped / SOFT_CAP) ** 2)
        ).astype(jnp.bfloat16)
        grad_query_acc = grad_query_acc + jnp.einsum(
            "kgqr,rkd->qkgd", grad_scores, key_block, preferred_element_type=jnp.float32
        )
        key_part = jnp.einsum(
            "kgqr,qkgd->rkd", grad_scores, query_grouped, preferred_element_type=jnp.float32
        )
        value_part = jnp.einsum(
            "kgqr,qkgd->rkd",
            exp_scores.astype(jnp.bfloat16),
            grad_summed,
            preferred_element_type=jnp.float32,
        )
        grad_key_all = lax.dynamic_update_slice_in_dim(
            grad_key_all,
            lax.dynamic_slice_in_dim(grad_key_all, offset_row, block_size) + key_part,
            offset_row,
            0,
        )
        grad_value_all = lax.dynamic_update_slice_in_dim(
            grad_value_all,
            lax.dynamic_slice_in_dim(grad_value_all, offset_row, block_size) + value_part,
            offset_row,
            0,
        )
        return ((grad_query_acc, grad_key_all, grad_value_all), None)

    fold_state, unused = lax.scan(
        back_block_step, fold_state, (key_blocks, value_blocks, pos_blocks, row_starts)
    )
    grad_query_acc, grad_key_all, grad_value_all = fold_state
    grad_keys_block, grad_values_block = (
        lax.psum_scatter(
            grad_key_all.astype(jnp.bfloat16), "ctx", scatter_dimension=0, tiled=True
        ).astype(jnp.float32),
        lax.psum_scatter(
            grad_value_all.astype(jnp.bfloat16), "ctx", scatter_dimension=0, tiled=True
        ).astype(jnp.float32),
    )
    grad_query_low = grad_query_acc.reshape(block_rows, query_local, HD).astype(jnp.bfloat16)
    grad_query_tok, grad_key_tok, grad_value_tok = (
        lax.all_to_all(grad_query_low, "head", split_axis=0, concat_axis=1, tiled=True),
        lax.all_to_all(
            grad_keys_block.astype(jnp.bfloat16), "head", split_axis=0, concat_axis=1, tiled=True
        ),
        lax.all_to_all(
            grad_values_block.astype(jnp.bfloat16), "head", split_axis=0, concat_axis=1, tiled=True
        ),
    )
    grad_key_sum = jnp.sum(
        grad_key_tok.astype(jnp.float32).reshape(tok_rows, KVH, copies, HD), axis=2
    )
    grad_value_sum = jnp.sum(
        grad_value_tok.astype(jnp.float32).reshape(tok_rows, KVH, copies, HD), axis=2
    )
    grad_query_in = rope_back(grad_query_tok.astype(jnp.float32), cosine, sine_table) * query_scale
    grad_key_in = rope_back(grad_key_sum, cosine, sine_table)
    grad_proj = jnp.concatenate(
        [
            grad_query_in.reshape(tok_rows, QH * HD),
            grad_key_in.reshape(tok_rows, KVH * HD),
            grad_value_sum.reshape(tok_rows, KVH * HD),
        ],
        axis=1,
    ).astype(jnp.bfloat16)
    grad_first = jnp.einsum("tc,dc->td", grad_proj, qkv_low, preferred_element_type=jnp.float32)
    grad_input_part, input_gain_rows = norm_back(inputs, gain_cols[:, 0], grad_first)
    tokens_grad = (grad_middle + grad_input_part).astype(jnp.bfloat16)
    gain_term = jnp.stack(
        [
            jnp.sum(input_gain_rows, axis=0),
            jnp.sum(attn_gain_rows, axis=0),
            jnp.sum(mid_gain_rows, axis=0),
            ffn_gain_term,
        ],
        axis=1,
    )
    qkv_term = jnp.einsum("td,tc->dc", first_normed, grad_proj, preferred_element_type=jnp.float32)
    out_term = jnp.einsum(
        "ti,td->id", flat_heads, grad_attn_low, preferred_element_type=jnp.float32
    )
    qkv_grad, out_grad, gains_grad = (
        lax.psum_scatter(qkv_term, ("fsdp", "ctx", "head"), scatter_dimension=0, tiled=True),
        lax.psum_scatter(out_term, ("fsdp", "ctx", "head"), scatter_dimension=0, tiled=True),
        lax.psum_scatter(gain_term, ("fsdp", "ctx", "head"), scatter_dimension=0, tiled=True),
    )
    gate_up_grad, down_grad = (
        lax.psum_scatter(
            gate_up_term.astype(jnp.bfloat16), ("fsdp", "ctx"), scatter_dimension=1, tiled=True
        ).astype(jnp.float32),
        lax.psum_scatter(
            down_term.astype(jnp.bfloat16), ("fsdp", "ctx"), scatter_dimension=1, tiled=True
        ).astype(jnp.float32),
    )
    qkv_first_new, qkv_second_new, qkv_new = adam_step(
        qkv_weight, qkv_first, qkv_second, qkv_grad, RATE_MATRIX, WEIGHT_DECAY
    )
    out_first_new, out_second_new, out_new = adam_step(
        out_weight, out_first, out_second, out_grad, RATE_MATRIX, WEIGHT_DECAY
    )
    gate_up_first_new, gate_up_second_new, gate_up_new = adam_step(
        gate_up, gate_up_first, gate_up_second, gate_up_grad, RATE_MATRIX, WEIGHT_DECAY
    )
    down_first_new, down_second_new, down_new = adam_step(
        down_weight, down_first, down_second, down_grad, RATE_DOWN, WEIGHT_DECAY
    )
    gains_first_new, gains_second_new, gains_new = adam_step(
        gains, gains_first, gains_second, gains_grad, RATE_GAIN, 0.0
    )
    return (
        mixed_out,
        tokens_grad,
        qkv_grad,
        qkv_first_new,
        qkv_second_new,
        qkv_new,
        out_grad,
        out_first_new,
        out_second_new,
        out_new,
        gate_up_grad,
        gate_up_first_new,
        gate_up_second_new,
        gate_up_new,
        down_grad,
        down_first_new,
        down_second_new,
        down_new,
        gains_grad,
        gains_first_new,
        gains_second_new,
        gains_new,
    )


def solution(mesh):
    in_specs = (
        P(("fsdp", "ctx", "head"), None),
        P("fsdp"),
        P(("fsdp", "ctx", "head"), None),
        P(("fsdp", "ctx", "head"), None),
        P(("fsdp", "ctx", "head"), None),
        P(("fsdp", "ctx", "head"), None),
        P(("fsdp", "ctx", "head"), None),
        P(("fsdp", "ctx", "head"), None),
        P(("fsdp", "ctx", "head"), None),
        P(None, ("fsdp", "ctx"), "head"),
        P(None, ("fsdp", "ctx"), "head"),
        P(None, ("fsdp", "ctx"), "head"),
        P("head", ("fsdp", "ctx")),
        P("head", ("fsdp", "ctx")),
        P("head", ("fsdp", "ctx")),
        P(("fsdp", "ctx", "head"), None),
        P(("fsdp", "ctx", "head"), None),
        P(("fsdp", "ctx", "head"), None),
    )
    out_specs = (
        P(("fsdp", "ctx", "head"), None),
        P(("fsdp", "ctx", "head"), None),
        P(("fsdp", "ctx", "head"), None),
        P(("fsdp", "ctx", "head"), None),
        P(("fsdp", "ctx", "head"), None),
        P(("fsdp", "ctx", "head"), None),
        P(("fsdp", "ctx", "head"), None),
        P(("fsdp", "ctx", "head"), None),
        P(("fsdp", "ctx", "head"), None),
        P(("fsdp", "ctx", "head"), None),
        P(None, ("fsdp", "ctx"), "head"),
        P(None, ("fsdp", "ctx"), "head"),
        P(None, ("fsdp", "ctx"), "head"),
        P(None, ("fsdp", "ctx"), "head"),
        P("head", ("fsdp", "ctx")),
        P("head", ("fsdp", "ctx")),
        P("head", ("fsdp", "ctx")),
        P("head", ("fsdp", "ctx")),
        P(("fsdp", "ctx", "head"), None),
        P(("fsdp", "ctx", "head"), None),
        P(("fsdp", "ctx", "head"), None),
        P(("fsdp", "ctx", "head"), None),
    )
    return jax.shard_map(shards, mesh=mesh, in_specs=in_specs, out_specs=out_specs, check_vma=False)
```

profile of v0, /device:TPU:0, one launch (start us, length us, event | category | flops | bytes accessed | tf_op | source)
XLA Modules:
  0.0 2729.6 jit_solution(9910453606472588548)
XLA Ops:
  9.6 43.4 %all-gather = bf16[32,72,4]{1,2,0:T(4,128)(2,1)S(1)} all-gather(bf16[1,72,4]{1,2,0:T(4,128)(2,1)S(1)} %convert_bitcast_fusion.1), channel_id=1, replica_groups=mesh['fsdp'=2,'ctx'=4,'head'=4] {'fsdp','ctx','head'}, dimensions={0}, use_global_device_ids=true | all-gather | bytes 19008 | tf_op jit(solution)/shard_map/all_gather | solution.py:34
  53.9 85.0 %all-gather.10.cloned.1.call-done = bf16[2304,4096]{1,0:T(8,128)(2,1)} async-done(((bf16[72,4096]{1,0:T(8,128)(2,1)}), bf16[2304,4096]{1,0:T(8,128)(2,1)}) %all-gather.10.cloned.1.call-update) | async-done | bytes 18874384 | tf_op jit(solution)/shard_map/all_gather | solution.py:28
  139.0 7.8 fusion.83
  149.1 9.1 all_to_all.102
  158.4 9.1 all_to_all.103
  169.5 4.3 convert_element_type.207
  181.5 8.6 all-to-all-done.1
  190.2 23.3 all-gather.14.cloned.1.call-done
  213.5 14.6 while.30
  230.4 11.4 all_to_all.104
  242.2 56.2 %all-gather.16.cloned.1.call-done = bf16[2048,2304]{1,0:T(8,128)(2,1)} async-done(((bf16[64,2304]{1,0:T(8,128)(2,1)}), bf16[2048,2304]{1,0:T(8,128)(2,1)}) %all-gather.16.cloned.1.call-update) | async-done | bytes 9437200 | tf_op jit(solution)/shard_map/all_gather | solution.py:31
  298.4 5.2 multiply_reduce_fusion.6
  310.4 395.2 %all-gather.20.cloned.1.call-done = bf16[2,2304,2304]{2,1,0:T(8,128)(2,1)} async-done(((bf16[2,288,2304]{2,1,0:T(8,128)(2,1)}), bf16[2,2304,2304]{2,1,0:T(8,128)(2,1)}) %all-gather.20.cloned.1.call-update) | async-done | bytes 21233680 | tf_op jit(solution)/shard_map/all_gather | solution.py:37
  705.7 27.3 %all-gather.18.cloned.1.call-done = bf16[512,2304]{1,0:T(8,128)(2,1)} async-done(((bf16[128,2304]{1,0:T(8,128)(2,1)}), bf16[512,2304]{1,0:T(8,128)(2,1)}) %all-gather.18.cloned.1.call-update) | async-done | bytes 2359312 | tf_op jit(solution)/shard_map/all_gather | solution.py:205
  733.0 15.2 convolution_bitcast_fusion.4
  748.2 3.6 copy-done.13
  753.5 134.6 %all-gather.22.cloned.1.call-done = bf16[2304,2304]{0,1:T(8,128)(2,1)} async-done(((bf16[2304,288]{0,1:T(8,128)(2,1)}), bf16[2304,2304]{0,1:T(8,128)(2,1)}) %all-gather.22.cloned.1.call-update) | async-done | bytes 10616848 | tf_op jit(solution)/shard_map/all_gather | solution.py:38
  888.1 10.9 convolution_convert_fusion.2
  899.9 53.2 %all-reduce.9.cloned.1.call-done = bf16[512,2304]{1,0:T(8,128)(2,1)} async-done(((bf16[512,2304]{1,0:T(8,128)(2,1)}), bf16[512,2304]{1,0:T(8,128)(2,1)}) %all-reduce.9.cloned.1.call-update) | async-done | bytes 2359312 | tf_op jit(solution)/shard_map/psum | solution.py:215
  955.5 23.4 all-gather.24.cloned.1.call-done
  978.9 5.1 broadcast_multiply_fusion
  984.7 13.8 fusion.54
  1000.7 15.5 fusion.49
  1023.4 26.1 reduce-scatter.6.cloned.1.call-done
  1051.0 3.7 multiply_reduce_fusion.2
  1056.1 7.0 convolution_convert_fusion.3
  1068.4 7.9 all-to-all-done.4
  1082.2 70.6 %while.31 = (s32[]{:T(128)}, f32[512,1,2,256]{0,3,2,1:T(8,128)S(1)}, f32[2048,1,256]{2,0,1:T(8,128)}, f32[2048,1,256]{2,0,1:T(8,128)}, bf16[4,512,1,256]{3,1,2,0...) while((s32[]{:T(128)}, ...), condition=%wide.region_15.16_spmd.clone, body=%wide.region_14.15_spmd.clone.sunk | while | flops 1350041600 | bytes 31994176 | solution.py:309
  1154.5 12.9 copy.261
  1167.5 12.9 copy.263
  1180.5 18.0 fusion.40
  1198.6 52.4 %copy.266 = bf16[2,2304,2304]{2,0,1:T(2,128)(2,1)} copy(bf16[2,2304,2304]{1,2,0:T(8,128)(2,1)} %fusion.40) | data formatting | bytes 42467328 | tf_op jit(solution)/shard_map/convert_element_type | solution.py:370
  1251.7 11.1 convolution_convert_fusion.1
  1264.1 7.9 fusion.103
  1273.2 3.7 all-to-all-start.5
  1278.2 57.8 %all-reduce.13.cloned.1.call-done = (bf16[2048,1,256]{2,1,0:T(2,128)(2,1)}, bf16[2048,1,256]{2,1,0:T(2,128)(2,1)}) async-done(((bf16[2048,1,256]{2,1,0:T(2,128)(2,1)}, bf16[2048,1,256]{2,1,0:T(2,128)(2,1)}), (bf16[2048,1,256]{2,1,0:T(2,128)(2,1)}, bf16[2048,1,256]{2,1,0:T(2,128)(2,1)})) %all-reduce.13.cloned.1.call-update) | async-done | bytes 2097168
  1354.8 5.1 all-to-all-done.6
  1360.6 16.0 fusion.80
  1378.6 10.8 fusion.71
  1389.4 42.6 %all-reduce.3 = f32[2304,4]{0,1:T(4,128)S(1)} all-reduce(f32[2304,4]{0,1:T(4,128)S(1)} %pad_maximum_fusion.8), channel_id=9, replica_groups=mesh['fsdp'=2,'ctx'=4,'head'=4] {'fsdp','ctx','head'}, use_global_device_ids=true, to_apply=%region_27.28.clone | all-reduce | flops 9216 | bytes 73728
  1435.3 536.4 %all-reduce.11.cloned.1.call-done = bf16[2,2304,2304]{2,0,1:T(2,128)(2,1)} async-done(((bf16[2,2304,2304]{2,0,1:T(2,128)(2,1)}), bf16[2,2304,2304]{2,0,1:T(2,128)(2,1)}) %all-reduce.11.cloned.1.call-update) | async-done | bytes 21233680
  1971.7 5.1 constant_dynamic-slice_fusion.3
  1976.8 178.0 %reduce-scatter.12.cloned.1.call-done = bf16[2304,288]{0,1:T(8,128)(2,1)} async-done(((bf16[2304,2304]{0,1:T(8,128)(2,1)}), bf16[2304,288]{0,1:T(8,128)(2,1)}) %reduce-scatter.12.cloned.1.call-update) | async-done | bytes 1327120 | tf_op jit(solution)/shard_map/reduce_scatter | solution.py:372
  2154.7 7.6 multiply_subtract_fusion.1
  2162.4 14.0 multiply_subtract_fusion
  2176.4 189.3 %reduce-scatter.10.cloned.1.call-done = f32[64,2304]{1,0:T(8,128)} async-done(((f32[2048,2304]{1,0:T(8,128)}), f32[64,2304]{1,0:T(8,128)}) %reduce-scatter.10.cloned.1.call-update) | async-done | bytes 589840 | tf_op jit(solution)/shard_map/reduce_scatter | solution.py:365
  2368.5 350.2 %reduce-scatter.8.cloned.1.call-done = f32[72,4096]{1,0:T(8,128)} async-done(((f32[2304,4096]{1,0:T(8,128)}), f32[72,4096]{1,0:T(8,128)}) %reduce-scatter.8.cloned.1.call-update) | async-done | bytes 1179664 | tf_op jit(solution)/shard_map/reduce_scatter | solution.py:364
  2718.7 4.0 multiply_subtract_fusion.2
  (328 shorter events, 162.4 us)
Async XLA Ops:
  7.2 46.0 %copy-start.47 = (s32[2048]{0:T(1024)S(1)}, s32[2048]{0:T(1024)}, u32[]{:S(2)}) copy-start(s32[2048]{0:T(1024)} %param.23) | copy-start | bytes 24580
  7.2 46.2 %copy-start.6 = (bf16[128,2304]{1,0:T(8,128)(2,1)S(1)}, bf16[128,2304]{1,0:T(8,128)(2,1)}, u32[]{:S(2)}) copy-start(bf16[128,2304]{1,0:T(8,128)(2,1)} %param.22) | copy-start | bytes 1769476
  7.2 131.7 %all-gather.10.cloned.1.call-start = ((), (), s32[]{:S(2)}) async-start(), calls=%async_computation.12 | async-start | bytes 19464192 | tf_op jit(solution)/shard_map/all_gather | solution.py:28
  9.5 180.7 %all-gather.12.cloned.1.call-start = ((), (), s32[]{:S(2)}) async-start(), calls=%async_computation.13 | async-start | bytes 1310720 | tf_op jit(solution)/shard_map/all_gather | solution.py:170
  53.4 93.4 %copy-start.42 = (f32[2304]{0:T(1024)}, f32[2304]{0:T(1024)S(1)}, u32[]{:S(2)}) copy-start(f32[2304]{0:T(1024)S(1)} %get-tuple-element.556) | copy-start | bytes 27652
  53.6 93.2 %copy-start.45 = (f32[128]{0:T(128)}, f32[128]{0:T(128)S(1)}, u32[]{:S(2)}) copy-start(f32[128]{0:T(128)S(1)} %add_rsqrt_fusion.4) | copy-start | bytes 1540
  53.9 119.9 %copy-start.32 = (f32[128,128]{1,0:T(8,128)}, f32[128,128]{1,0:T(8,128)S(1)}, u32[]{:S(2)}) copy-start(f32[128,128]{1,0:T(8,128)S(1)} %get-tuple-element.642) | copy-start | bytes 196612
  53.9 120.0 %copy-start.30 = (f32[128,128]{1,0:T(8,128)}, f32[128,128]{1,0:T(8,128)S(1)}, u32[]{:S(2)}) copy-start(f32[128,128]{1,0:T(8,128)S(1)} %get-tuple-element.641) | copy-start | bytes 196612
  158.3 55.3 %all-gather.14.cloned.1.call-start = ((), (), s32[]{:S(2)}) async-start(), calls=%async_computation.14 | async-start | bytes 1310720 | tf_op jit(solution)/shard_map/all_gather | solution.py:171
  167.5 130.9 %all-gather.16.cloned.1.call-start = ((), (), s32[]{:S(2)}) async-start(), calls=%async_computation.15 | async-start | bytes 9732096 | tf_op jit(solution)/shard_map/all_gather | solution.py:31
  169.4 536.3 %all-gather.20.cloned.1.call-start = ((), (), s32[]{:S(2)}) async-start(), calls=%async_computation.17 | async-start | bytes 23887872 | tf_op jit(solution)/shard_map/all_gather | solution.py:37
  177.9 12.3 all-to-all-start.1
  181.4 551.6 %all-gather.18.cloned.1.call-start = ((), (), s32[]{:S(2)}) async-start(), calls=%async_computation.16 | async-start | bytes 2949120 | tf_op jit(solution)/shard_map/all_gather | solution.py:205
  228.8 13.1 copy-start.25
  242.2 61.4 %copy-start.16 = (bf16[128,4,2,256]{0,3,2,1:T(8,128)(2,1)}, bf16[128,4,2,256]{0,3,2,1:T(8,128)(2,1)S(1)}, u32[]{:S(2)}) copy-start(bf16[128,4,2,256]{0,3,2,1:T(8,128)(2,1)S(1)} %copy.251) | copy-start | bytes 1572868
  307.0 581.1 %all-gather.22.cloned.1.call-start = ((), (), s32[]{:S(2)}) async-start(), calls=%async_computation.18 | async-start | bytes 11943936 | tf_op jit(solution)/shard_map/all_gather | solution.py:38
  310.2 642.9 %all-reduce.9.cloned.1.call-start = ((), (), s32[]{:S(2)}) async-start(), calls=%async_computation.19 | async-start | bytes 4718592 | tf_op jit(solution)/shard_map/psum | solution.py:215
  753.5 145.6 %copy-start.24 = (bf16[512,2304]{1,0:T(8,128)(2,1)}, bf16[512,2304]{1,0:T(8,128)(2,1)S(1)}, u32[]{:S(2)}) copy-start(bf16[512,2304]{1,0:T(8,128)(2,1)S(1)} %multiply_convert_fusion.2) | copy-start | bytes 7077892
  899.1 79.8 %all-gather.24.cloned.1.call-start = ((), (), s32[]{:S(2)}) async-start(), calls=%async_computation.20 | async-start | bytes 2949120 | tf_op jit(solution)/shard_map/all_gather | solution.py:206
  899.8 149.7 %reduce-scatter.6.cloned.1.call-start = ((), (), s32[]{:S(2)}) async-start(), calls=%async_computation.21 | async-start | bytes 2949120 | tf_op jit(solution)/shard_map/reduce_scatter | solution.py:242
  953.1 25.8 copy-start.1
  984.7 13.8 copy-start.53
  1018.6 30.9 %copy-start.5 = (f32[128,2304]{1,0:T(8,128)S(1)}, f32[128,2304]{1,0:T(8,128)}, u32[]{:S(2)}) copy-start(f32[128,2304]{1,0:T(8,128)} %copy-done.4) | copy-start | bytes 3538948
  1020.8 30.2 %copy-start.3 = (f32[128,2304]{1,0:T(8,128)S(1)}, f32[128,2304]{1,0:T(8,128)}, u32[]{:S(2)}) copy-start(f32[128,2304]{1,0:T(8,128)} %copy-done.2) | copy-start | bytes 3538948
  1020.8 30.2 %copy-start.22 = (bf16[128,2304]{1,0:T(8,128)(2,1)S(1)}, bf16[128,2304]{1,0:T(8,128)(2,1)}, u32[]{:S(2)}) copy-start(bf16[128,2304]{1,0:T(8,128)(2,1)} %param.24) | copy-start | bytes 1769476
  1063.2 13.7 copy-start.21
  1063.2 13.7 copy-start.26
  1064.0 12.3 all-to-all-start.4
  1067.5 268.5 %all-reduce.13.cloned.1.call-start = ((), (), s32[]{:S(2)}) async-start(), calls=%async_computation.26 | async-start | bytes 8388608
  1154.5 12.9 copy-start.15
  1180.5 791.2 %all-reduce.11.cloned.1.call-start = ((), (), s32[]{:S(2)}) async-start(), calls=%async_computation.25 | async-start | bytes 42467328
  1251.0 903.7 %reduce-scatter.12.cloned.1.call-start = ((), (), s32[]{:S(2)}) async-start(), calls=%async_computation.24 | async-start | bytes 11943936 | tf_op jit(solution)/shard_map/reduce_scatter | solution.py:372
  1262.8 1102.9 %reduce-scatter.10.cloned.1.call-start = ((), (), s32[]{:S(2)}) async-start(), calls=%async_computation.23 | async-start | bytes 19464192 | tf_op jit(solution)/shard_map/reduce_scatter | solution.py:365
  1273.2 67.8 %all-to-all-start.5 = ((bf16[512,2,256]{2,1,0:T(2,128)(2,1)}), bf16[512,2,256]{2,1,0:T(2,128)(2,1)S(1)}, u32[]{:S(2)}, u32[]{:S(2)}) async-start(bf16[512,2,256]{2,1,0:T(2,128)(2,1)} %bitcast.34), calls=%async_computation.6 | async-start | bytes 1048576 | tf_op jit(solution)/shard_map/all_to_all | solution.py:323
  1341.0 9.4 all-to-all-start.7
  1344.5 9.5 copy-start.36
  1344.5 9.5 copy-start.38
  1350.5 9.4 all-to-all-start.6
  1353.9 1364.8 %reduce-scatter.8.cloned.1.call-start = ((), (), s32[]{:S(2)}) async-start(), calls=%async_computation.22 | async-start | bytes 38928384 | tf_op jit(solution)/shard_map/reduce_scatter | solution.py:364
  1354.8 21.8 copy-start.28
  1360.5 16.1 copy-start.29
  1378.5 54.1 %copy-start.49 = (f32[72,4]{0,1:T(4,128)S(1)}, f32[72,4]{0,1:T(4,128)}, u32[]{:S(2)}) copy-start(f32[72,4]{0,1:T(4,128)} %param.37) | copy-start | bytes 3460
  1378.6 55.5 %copy-start.10 = (f32[128,2304]{1,0:T(8,128)S(1)}, f32[128,2304]{1,0:T(8,128)}, u32[]{:S(2)}) copy-start(f32[128,2304]{1,0:T(8,128)} %copy-done.9) | copy-start | bytes 3538948
  1435.3 719.5 %copy-start.11 = (f32[2304,288]{0,1:T(8,128)S(1)}, f32[2304,288]{0,1:T(8,128)}, u32[]{:S(2)}) copy-start(f32[2304,288]{0,1:T(8,128)} %param.34) | copy-start | bytes 7962628
  2162.4 203.4 %copy-start.23 = (f32[64,2304]{1,0:T(8,128)S(1)}, f32[64,2304]{1,0:T(8,128)}, u32[]{:S(2)}) copy-start(f32[64,2304]{1,0:T(8,128)} %param.28) | copy-start | bytes 1769476
  2162.4 203.4 %copy-start.39 = (f32[64,2304]{1,0:T(8,128)S(1)}, f32[64,2304]{1,0:T(8,128)}, u32[]{:S(2)}) copy-start(f32[64,2304]{1,0:T(8,128)} %param.30) | copy-start | bytes 1769476
  2176.4 542.2 %copy-start.20 = (f32[72,4096]{1,0:T(8,128)S(1)}, f32[72,4096]{1,0:T(8,128)}, u32[]{:S(2)}) copy-start(f32[72,4096]{1,0:T(8,128)} %param.25) | copy-start | bytes 3538948
  2176.4 542.2 %copy-start.27 = (f32[72,4096]{1,0:T(8,128)S(1)}, f32[72,4096]{1,0:T(8,128)}, u32[]{:S(2)}) copy-start(f32[72,4096]{1,0:T(8,128)} %param.27) | copy-start | bytes 3538948
  (40 other events, 144.9 us)
Sparse Core Ops, SparseCore 0:
  11.5 127.3 all-gather.9
  158.4 26.0 all-gather.11
  186.1 27.4 all-gather.13
  216.9 81.5 all-gather.15
  300.4 405.2 all-gather.19
  707.7 25.2 all-gather.17
  735.7 152.4 all-gather.21
  899.2 53.8 all-reduce.8
  954.7 24.1 all-gather.23
  1016.4 33.0 reduce-scatter.5
  1180.6 155.3 all-reduce.12
  1339.9 631.7 all-reduce.10
  1975.7 178.9 reduce-scatter.11
  2161.6 204.1 reduce-scatter.9
  2372.6 345.9 reduce-scatter.7
where the time goes:
time: 2740 us; the launch traced here: 2730 us
  waiting for transfers between devices  2160 us (79%)
  matrix products  191 us (7%)
  local copies, waits for them, and re-layouts  143 us (5%)
  blocking collectives  116 us (4%)
  other arithmetic  77.3 us (3%)
    unnamed x17, waiting for transfers between devices  595 us
    all_gather x1, waiting for transfers between devices, fetch_params(): lax.all_gather(gate_up.astype(jnp.bfloat16), ('fsdp', 'ctx'), axis=1, til...  395 us
    reduce_scatter x1, waiting for transfers between devices, shards(): lax.psum_scatter(qkv_term, ('fsdp', 'ctx', 'head'), scatter_dimension=0,...  350 us
    reduce_scatter x1, waiting for transfers between devices, shards(): lax.psum_scatter(out_term, ('fsdp', 'ctx', 'head'), scatter_dimension=0,...  189 us
    reduce_scatter x1, waiting for transfers between devices, shards(): lax.psum_scatter(down_term.astype(jnp.bfloat16), ('fsdp', 'ctx'), scatter...  178 us
    all_gather x1, waiting for transfers between devices, fetch_params(): lax.all_gather(down_weight.astype(jnp.bfloat16), ('fsdp', 'ctx'), axis=1,...  135 us
    all_gather x1, waiting for transfers between devices, fetch_params(): lax.all_gather(qkv_weight.astype(jnp.bfloat16), ('fsdp', 'ctx', 'head'),...  85 us
    all_gather x1, waiting for transfers between devices, fetch_params(): lax.all_gather(out_weight.astype(jnp.bfloat16), ('fsdp', 'ctx', 'head'),...  56.2 us
  transfers between devices with their start and end apart: 20, of which 18 were waited for; matrix products, arithmetic and copies ran while one was open for 8% of the time, Pallas kernels for 0%

commit v1 on v0

v1 whole, which is shorter than its diff:
```python
import math

import jax
import jax.numpy as jnp
from jax import lax
from jax.sharding import PartitionSpec as P

QH = 8
KVH = 4
HD = 256
STEP = 10


SOFT_CAP = 50.0
EPS_NORM = 1e-06
ROPE_BASE = 10000.0
BETA_ONE = 0.9
BETA_TWO = 0.95
EPS_ADAM = 1e-08
RATE_MATRIX = 0.05
RATE_DOWN = 0.025
RATE_GAIN = 0.5
WEIGHT_DECAY = 0.1

BF16 = jnp.bfloat16
F32 = jnp.float32


def send_by(values, axis, step):
    size = lax.axis_size(axis)
    return lax.ppermute(values, axis, [(i, (i + step) % size) for i in range(size)])


def swap_bit(values, axis, bit):
    size = lax.axis_size(axis)
    return lax.ppermute(values, axis, [(i, i ^ bit) for i in range(size)])


def head_bits():
    bits = []
    bit = lax.axis_size("head") // 2
    while bit:
        bits.append(bit)
        bit //= 2
    return bits


def head_order():
    order = [0]
    for bit in head_bits():
        order = order + [one ^ bit for one in order]
    return order


def head_gather(rows):
    for bit in head_bits():
        rows = jnp.concatenate([rows, swap_bit(rows, "head", bit)], axis=0)
    return rows


def head_reduce(part):
    for bit in reversed(head_bits()):
        half = part.shape[0] // 2
        came = swap_bit(part[half:].astype(BF16), "head", bit)
        part = part[:half].astype(F32) + came.astype(F32)
    return part


def head_exchange(pieces):
    size = lax.axis_size("head")
    own = lax.axis_index("head")
    result = pieces
    for other in range(1, size):
        came = swap_bit(lax.dynamic_index_in_dim(pieces, own ^ other, 0, keepdims=True), "head", other)
        result = lax.dynamic_update_slice_in_dim(result, came, own ^ other, 0)
    return result


def gather_pieces(piece_for):
    size_x, size_z = lax.axis_size("fsdp"), lax.axis_size("ctx")
    x, z = lax.axis_index("fsdp"), lax.axis_index("ctx")
    own = piece_for(0)
    result = jnp.zeros((size_x, size_z) + own.shape, own.dtype)
    for k in range(size_z):
        came = own if k == 0 else send_by(piece_for(k), "ctx", k)
        place = lax.rem(z - k + size_z, size_z)
        result = lax.dynamic_update_slice(result, came[None, None], (x, place) + (0,) * own.ndim)
        for step in range(1, size_x):
            other = send_by(came, "fsdp", step)
            place_x = lax.rem(x - step + size_x, size_x)
            result = lax.dynamic_update_slice(
                result, other[None, None], (place_x, place) + (0,) * own.ndim
            )
    return result


def scatter_pieces(pieces):
    size_x, size_z = lax.axis_size("fsdp"), lax.axis_size("ctx")
    x, z = lax.axis_index("fsdp"), lax.axis_index("ctx")
    rest = pieces.shape[2:]

    def pick(at_x, at_z):
        return lax.dynamic_slice(
            pieces, (at_x, at_z) + (0,) * len(rest), (1, 1) + rest
        ).reshape(rest)

    came_by = [None] * size_z
    for k in sorted(range(size_z), key=lambda k: -min(k, size_z - k)):
        at_z = lax.rem(z + k, size_z)
        total = pick(x, at_z).astype(F32)
        for step in range(1, size_x):
            at_x = lax.rem(x + step, size_x)
            total = total + send_by(pick(at_x, at_z).astype(BF16), "fsdp", step).astype(F32)
        came_by[k] = total if k == 0 else send_by(total.astype(BF16), "ctx", k).astype(F32)
    return came_by


def gather_gains(gains):
    rows = gains.astype(BF16).T
    for axis in ("head", "ctx", "fsdp"):
        size, bit = lax.axis_size(axis), 1
        own = lax.axis_index(axis)
        while bit < size:
            other = swap_bit(rows, axis, bit)
            rows = jnp.where(
                (own & bit) == 0,
                jnp.concatenate([rows, other], axis=1),
                jnp.concatenate([other, rows], axis=1),
            )
            bit *= 2
    return rows.astype(F32)


def scatter_gains(rows):
    for axis in ("fsdp", "ctx", "head"):
        own = lax.axis_index(axis)
        bit = lax.axis_size(axis) // 2
        while bit:
            half = rows.shape[1] // 2
            low_part, high_part = rows[:, :half], rows[:, half:]
            is_low = (own & bit) == 0
            keep = jnp.where(is_low, low_part, high_part)
            rows = keep + swap_bit(jnp.where(is_low, high_part, low_part), axis, bit)
            bit //= 2
    return rows.T


def matmul(left, right):
    return jnp.dot(left, right, preferred_element_type=F32)


def matmul_nt(left, right):
    return lax.dot_general(left, right, (((1,), (1,)), ((), ())), preferred_element_type=F32)


def matmul_tn(left, right):
    return lax.dot_general(left, right, (((0,), (0,)), ((), ())), preferred_element_type=F32)


def rms_norm(values, gain_row):
    inv_scale = lax.rsqrt(jnp.mean(values * values, axis=-1, keepdims=True) + EPS_NORM)
    return values * inv_scale * (1.0 + gain_row)


def norm_back(values, gain_row, upstream):
    inv_scale = lax.rsqrt(jnp.mean(values * values, axis=-1, keepdims=True) + EPS_NORM)
    unit_rows = values * inv_scale
    scaled = upstream * (1.0 + gain_row)
    result = inv_scale * (scaled - unit_rows * jnp.mean(scaled * unit_rows, axis=-1, keepdims=True))
    return (result, jnp.sum(upstream * unit_rows, axis=0))


def rope_tables(position, half_dim):
    freq_table = ROPE_BASE ** (-(jnp.arange(half_dim, dtype=F32) * 2.0 / (2 * half_dim)))
    angle_table = position.astype(F32)[:, None] * freq_table[None, :]
    return (jnp.cos(angle_table), jnp.sin(angle_table))


def rope_turn(values, cosine, sine_table):
    half_dim = values.shape[-1] // 2
    lead_half = values[..., :half_dim]
    tail_half = values[..., half_dim:]
    return jnp.concatenate(
        [lead_half * cosine - tail_half * sine_table, tail_half * cosine + lead_half * sine_table],
        axis=-1,
    )


def rope_back(grad_rows, cosine, sine_table):
    return rope_turn(grad_rows, cosine, -sine_table)


def gated_unit(gate_in, up_in):
    return jax.nn.gelu(gate_in, approximate=True) * up_in


def adam_step(weight, first_old, second_old, gradient, step_rate, decay_rate):
    first_new = BETA_ONE * first_old + (1.0 - BETA_ONE) * gradient
    second_new = BETA_TWO * second_old + (1.0 - BETA_TWO) * gradient * gradient
    first_hat = first_new / (1.0 - BETA_ONE**STEP)
    second_hat = second_new / (1.0 - BETA_TWO**STEP)
    weight_new = weight - step_rate * (
        first_hat / (jnp.sqrt(second_hat) + EPS_ADAM) + decay_rate * weight
    )
    return (first_new, second_new, weight_new)


def block_weights(queries, keys, query_pos, key_pos):
    scores = jnp.einsum("kqd,krd->kqr", queries, keys, preferred_element_type=F32)
    unit = jnp.tanh(scores / SOFT_CAP)
    allowed = key_pos[None, None, :] <= query_pos[None, :, None]
    return (unit, jnp.where(allowed, jnp.exp(SOFT_CAP * unit), 0.0))


def block_forward(queries, keys, values, query_pos, key_pos):
    unused, weights = block_weights(queries, keys, query_pos, key_pos)
    return (
        jnp.sum(weights, axis=-1, keepdims=True),
        jnp.einsum("kqr,krd->kqd", weights.astype(BF16), values, preferred_element_type=F32),
    )


def block_backward(queries, keys, values, query_pos, key_pos, grad_summed, delta):
    unit, weights = block_weights(queries, keys, query_pos, key_pos)
    grad_weights = jnp.einsum("kqd,krd->kqr", grad_summed, values, preferred_element_type=F32)
    grad_scores = (weights * (grad_weights - delta) * (1.0 - unit * unit)).astype(BF16)
    return (
        jnp.einsum("kqr,krd->kqd", grad_scores, keys, preferred_element_type=F32),
        jnp.einsum("kqr,kqd->krd", grad_scores, queries, preferred_element_type=F32),
        jnp.einsum("kqr,kqd->krd", weights.astype(BF16), grad_summed, preferred_element_type=F32),
    )


def shards(
    tokens,
    positions,
    cotangent,
    qkv_weight,
    qkv_first,
    qkv_second,
    out_weight,
    out_first,
    out_second,
    gate_up,
    gate_up_first,
    gate_up_second,
    down_weight,
    down_first,
    down_second,
    gains,
    gains_first,
    gains_second,
):
    size_x, size_z, size_h = lax.axis_size("fsdp"), lax.axis_size("ctx"), lax.axis_size("head")
    z, own_h = lax.axis_index("ctx"), lax.axis_index("head")
    tok_rows, width = tokens.shape
    block_rows = tok_rows * size_h
    order = head_order()
    copies = max(1, size_h // KVH)
    kv_local = KVH * copies // size_h
    query_local = QH // size_h
    group = query_local // kv_local
    query_scale = 1.0 / math.sqrt(HD)
    query_cols, kv_cols = query_local * HD, kv_local * HD

    def positions_of(block):
        rows = lax.dynamic_slice_in_dim(positions, block * block_rows, block_rows)
        return jnp.concatenate(
            [lax.dynamic_slice_in_dim(rows, (own_h ^ one) * tok_rows, tok_rows) for one in order]
        )

    qkv_rows = qkv_weight.shape[0]
    qkv_low = qkv_weight.astype(BF16)

    def head_columns(part, heads, repeat):
        part = jnp.repeat(part.reshape(qkv_rows, heads, HD), repeat, axis=1)
        return part.reshape(qkv_rows, size_h, heads * repeat // size_h * HD)

    by_head = jnp.concatenate(
        [
            head_columns(qkv_low[:, : QH * HD], QH, 1),
            head_columns(qkv_low[:, QH * HD : (QH + KVH) * HD], KVH, copies),
            head_columns(qkv_low[:, (QH + KVH) * HD :], KVH, copies),
        ],
        axis=2,
    )
    local_cols = by_head.shape[2]
    qkv_piece = head_exchange(jnp.transpose(by_head, (1, 0, 2))).reshape(
        size_h * qkv_rows, local_cols
    )
    qkv_full = gather_pieces(lambda k: qkv_piece).reshape(width, local_cols)

    out_rows = out_weight.shape[0]
    strip = width // size_h
    out_low = jnp.transpose(out_weight.astype(BF16).reshape(out_rows, size_h, strip), (1, 0, 2))
    out_piece = head_exchange(out_low).reshape(size_h * out_rows, strip)
    out_strip = gather_pieces(lambda k: out_piece).reshape(size_h, query_cols, strip)
    out_full = jnp.transpose(head_exchange(out_strip), (1, 0, 2)).reshape(query_cols, width)

    gain_rows = gather_gains(gains)

    ff_rows = gate_up.shape[1]
    ff_cols = gate_up.shape[2] // size_z
    gate_up_low = jnp.transpose(
        gate_up.astype(BF16).reshape(2, ff_rows, size_z, ff_cols), (2, 1, 0, 3)
    ).reshape(size_z, ff_rows, 2 * ff_cols)
    down_low = jnp.transpose(
        down_weight.astype(BF16).reshape(size_z, ff_cols, ff_rows), (0, 2, 1)
    )
    gate_up_full = gather_pieces(
        lambda k: lax.dynamic_index_in_dim(gate_up_low, lax.rem(z + k, size_z), 0, keepdims=False)
    ).reshape(width, 2 * ff_cols)
    down_full = gather_pieces(
        lambda k: lax.dynamic_index_in_dim(down_low, lax.rem(z + k, size_z), 0, keepdims=False)
    ).reshape(width, ff_cols)

    block_tokens = head_gather(tokens).astype(F32)
    inputs = tokens.astype(F32)
    first_normed = rms_norm(block_tokens, gain_rows[0]).astype(BF16)
    projected = matmul(first_normed, qkv_full)
    block_pos = positions_of(z)
    cosine, sine_table = rope_tables(block_pos, HD // 2)

    def heads_of(values, count):
        return jnp.transpose(values.reshape(block_rows, count, HD), (1, 0, 2))

    queries = heads_of(projected[:, :query_cols], query_local)
    queries = (rope_turn(queries, cosine, sine_table) * query_scale).astype(BF16)
    queries = queries.reshape(kv_local, group * block_rows, HD)
    own_keys = heads_of(projected[:, query_cols : query_cols + kv_cols], kv_local)
    own_keys = rope_turn(own_keys, cosine, sine_table).astype(BF16)
    own_values = heads_of(projected[:, query_cols + kv_cols :], kv_local).astype(BF16)
    query_pos = jnp.tile(block_pos, group)
    own_kv = jnp.stack([own_keys, own_values])
    kv_slots = [own_kv] + [send_by(own_kv, "ctx", k) for k in range(1, size_z)]
    pos_slots = [positions_of(lax.rem(z - k + size_z, size_z)) for k in range(size_z)]
    exp_total = 0.0
    summed = 0.0
    for kv_slot, key_pos in zip(kv_slots, pos_slots):
        total_part, summed_part = block_forward(
            queries, kv_slot[0], kv_slot[1], query_pos, key_pos
        )
        exp_total = exp_total + total_part
        summed = summed + summed_part
    attended = summed / exp_total

    def rows_of(heads):
        heads = heads.reshape(-1, block_rows, HD)
        return jnp.transpose(heads, (1, 0, 2)).reshape(block_rows, -1)

    attended_low = rows_of(attended.astype(BF16))
    attn_out = head_reduce(matmul(attended_low, out_full).astype(BF16))
    middle = inputs + rms_norm(attn_out, gain_rows[1])
    second_normed = rms_norm(middle, gain_rows[2]).astype(BF16)

    def all_slots(rows):
        return [head_gather(rows)] + [
            head_gather(send_by(rows, "ctx", k)) for k in range(1, size_z)
        ]

    def sum_slots(parts):
        total = head_reduce(parts[0])
        for k in range(1, size_z):
            back = send_by(head_reduce(parts[k]).astype(BF16), "ctx", size_z - k)
            total = total + back.astype(F32)
        return total

    normed_slots = all_slots(second_normed)
    act_slots = [matmul(rows, gate_up_full) for rows in normed_slots]
    hidden_slots = [
        gated_unit(act[:, :ff_cols], act[:, ff_cols:]).astype(BF16) for act in act_slots
    ]
    ffn_out = sum_slots([matmul_nt(hidden, down_full).astype(BF16) for hidden in hidden_slots])
    mixed_out = (middle + rms_norm(ffn_out, gain_rows[3])).astype(BF16)

    upstream = cotangent.astype(F32)
    grad_ffn, gain_grad_ffn = norm_back(ffn_out, gain_rows[3], upstream)
    grad_slots = all_slots(grad_ffn.astype(BF16))
    grad_act_slots = []
    for rows, act in zip(grad_slots, act_slots):
        grad_hidden = matmul(rows, down_full)
        unit_out, unit_back = jax.vjp(gated_unit, act[:, :ff_cols], act[:, ff_cols:])
        grad_act_slots.append(jnp.concatenate(unit_back(grad_hidden), axis=1).astype(BF16))
    grad_second = sum_slots([matmul_nt(rows, gate_up_full).astype(BF16) for rows in grad_act_slots])
    down_term = matmul_tn(jnp.concatenate(grad_slots), jnp.concatenate(hidden_slots))
    gate_up_term = matmul_tn(jnp.concatenate(normed_slots), jnp.concatenate(grad_act_slots))
    down_came = scatter_pieces(down_term.reshape(size_x, size_z, ff_rows, ff_cols))
    gate_up_came = scatter_pieces(gate_up_term.reshape(size_x, size_z, ff_rows, 2 * ff_cols))

    def in_order(came):
        result = jnp.zeros((size_z,) + came[0].shape, F32)
        for k, part in enumerate(came):
            result = lax.dynamic_update_slice_in_dim(
                result, part[None], lax.rem(z - k + size_z, size_z), 0
            )
        return result

    down_grad = jnp.transpose(in_order(down_came), (0, 2, 1)).reshape(down_weight.shape)
    gate_up_grad = jnp.transpose(
        in_order(gate_up_came).reshape(size_z, ff_rows, 2, ff_cols), (2, 1, 0, 3)
    ).reshape(gate_up.shape)

    grad_middle_part, gain_grad_middle = norm_back(middle, gain_rows[2], grad_second)
    grad_middle = upstream + grad_middle_part
    grad_attn, gain_grad_attn = norm_back(attn_out, gain_rows[1], grad_middle)
    block_grad_attn = head_gather(grad_attn.astype(BF16))
    out_term = matmul_tn(attended_low, block_grad_attn).astype(BF16)
    out_term = head_exchange(
        jnp.transpose(out_term.reshape(query_cols, size_h, strip), (1, 0, 2))
    )
    out_came = sum(scatter_pieces(out_term.reshape(size_x, size_z, size_h * out_rows, strip)))
    out_grad = head_exchange(out_came.reshape(size_h, out_rows, strip).astype(BF16)).astype(F32)
    out_grad = jnp.transpose(out_grad, (1, 0, 2)).reshape(out_weight.shape)

    grad_attended = matmul_nt(block_grad_attn, out_full).astype(BF16)
    grad_attended = heads_of(grad_attended, query_local).astype(F32)
    grad_attended = grad_attended.reshape(kv_local, group * block_rows, HD)
    row_delta = jnp.sum(grad_attended * attended, axis=-1, keepdims=True)
    delta = row_delta / exp_total
    grad_summed = (grad_attended / exp_total).astype(BF16)
    grad_query = 0.0
    grad_kv = 0.0
    for k in sorted(range(size_z), key=lambda k: -min(k, size_z - k)):
        query_part, key_part, value_part = block_backward(
            queries, kv_slots[k][0], kv_slots[k][1], query_pos, pos_slots[k], grad_summed, delta
        )
        grad_query = grad_query + query_part
        kv_part = jnp.stack([key_part, value_part])
        if k:
            kv_part = send_by(kv_part.astype(BF16), "ctx", size_z - k).astype(F32)
        grad_kv = grad_kv + kv_part
    grad_query = grad_query.astype(BF16).astype(F32).reshape(query_local, block_rows, HD)
    grad_kv = grad_kv.astype(BF16).astype(F32)
    grad_proj = jnp.concatenate(
        [
            rows_of(rope_back(grad_query, cosine, sine_table) * query_scale),
            rows_of(rope_back(grad_kv[0], cosine, sine_table)),
            rows_of(grad_kv[1]),
        ],
        axis=1,
    ).astype(BF16)
    grad_first = head_reduce(matmul_nt(grad_proj, qkv_full).astype(BF16))
    grad_input_part, gain_grad_input = norm_back(inputs, gain_rows[0], grad_first)
    tokens_grad = (grad_middle + grad_input_part).astype(BF16)

    qkv_term = matmul_tn(first_normed, grad_proj)
    qkv_came = sum(scatter_pieces(qkv_term.reshape(size_x, size_z, size_h * qkv_rows, local_cols)))
    qkv_grad = head_exchange(qkv_came.reshape(size_h, qkv_rows, local_cols).astype(BF16))
    qkv_grad = jnp.transpose(qkv_grad.astype(F32), (1, 0, 2))

    def whole_columns(part, heads, repeat):
        part = part.reshape(qkv_rows, heads, repeat, HD)
        return jnp.sum(part, axis=2).reshape(qkv_rows, heads * HD)

    qkv_grad = jnp.concatenate(
        [
            whole_columns(qkv_grad[:, :, :query_cols], QH, 1),
            whole_columns(qkv_grad[:, :, query_cols : query_cols + kv_cols], KVH, copies),
            whole_columns(qkv_grad[:, :, query_cols + kv_cols :], KVH, copies),
        ],
        axis=1,
    )
    gains_grad = scatter_gains(
        jnp.stack([gain_grad_input, gain_grad_attn, gain_grad_middle, gain_grad_ffn])
    )

    qkv_first_new, qkv_second_new, qkv_new = adam_step(
        qkv_weight, qkv_first, qkv_second, qkv_grad, RATE_MATRIX, WEIGHT_DECAY
    )
    out_first_new, out_second_new, out_new = adam_step(
        out_weight, out_first, out_second, out_grad, RATE_MATRIX, WEIGHT_DECAY
    )
    gate_up_first_new, gate_up_second_new, gate_up_new = adam_step(
        gate_up, gate_up_first, gate_up_second, gate_up_grad, RATE_MATRIX, WEIGHT_DECAY
    )
    down_first_new, down_second_new, down_new = adam_step(
        down_weight, down_first, down_second, down_grad, RATE_DOWN, WEIGHT_DECAY
    )
    gains_first_new, gains_second_new, gains_new = adam_step(
        gains, gains_first, gains_second, gains_grad, RATE_GAIN, 0.0
    )
    return (
        mixed_out,
        tokens_grad,
        qkv_grad,
        qkv_first_new,
        qkv_second_new,
        qkv_new,
        out_grad,
        out_first_new,
        out_second_new,
        out_new,
        gate_up_grad,
        gate_up_first_new,
        gate_up_second_new,
        gate_up_new,
        down_grad,
        down_first_new,
        down_second_new,
        down_new,
        gains_grad,
        gains_first_new,
        gains_second_new,
        gains_new,
    )


TOKEN_SPEC = P(("fsdp", "ctx", "head"), None)
GATE_UP_SPEC = P(None, ("fsdp", "ctx"), "head")
DOWN_SPEC = P("head", ("fsdp", "ctx"))


def solution(mesh):
    in_specs = (
        (TOKEN_SPEC, P("fsdp"))
        + (TOKEN_SPEC,) * 7
        + (GATE_UP_SPEC,) * 3
        + (DOWN_SPEC,) * 3
        + (TOKEN_SPEC,) * 3
    )
    out_specs = (
        (TOKEN_SPEC,) * 10 + (GATE_UP_SPEC,) * 4 + (DOWN_SPEC,) * 4 + (TOKEN_SPEC,) * 4
    )
    return jax.shard_map(shards, mesh=mesh, in_specs=in_specs, out_specs=out_specs, check_vma=False)
```

time: 2740 us -> 1500 us (0.55)
  waiting for transfers between devices: 2160 us -> 509 us
  local copies, waits for them, and re-layouts: 143 us -> 483 us
  starting transfers between devices: 18.2 us -> 222 us
  blocking collectives: 116 us -> 0 us
  matrix products: 191 us -> 153 us
  other arithmetic: 77.3 us -> 109 us
    all_gather x8 -> x0, waiting for transfers between devices: 745 us -> none  [the longest x1 395 us: fetch_params(): lax.all_gather(gate_up.astype(jnp.bfloat16), ('fsdp', 'ctx'), axis=1, til...]
    reduce_scatter x4 -> x0, waiting for transfers between devices: 744 us -> none  [the longest x1 350 us: shards(): lax.psum_scatter(qkv_term, ('fsdp', 'ctx', 'head'), scatter_dimension=0,...]
    unnamed x17 -> x0, waiting for transfers between devices: 595 us -> none
    ppermute x0 -> x142, waiting for transfers between devices: none -> 509 us  [the longest x74 346 us: send_by(): lax.ppermute(values, axis, [(i, (i + step) % size) for i in range(size)])]
    dynamic_update_slice x8 -> x56, local copies, waits for them, and re-layouts: 21.4 us -> 301 us  [the longest x20 102 us: head_exchange(): result = lax.dynamic_update_slice_in_dim(result, came, own ^ other, 0)]
    ppermute x0 -> x142, starting transfers between devices: none -> 222 us  [the longest x74 177 us: send_by(): lax.ppermute(values, axis, [(i, (i + step) % size) for i in range(size)])]
    convert_element_type x9 -> x7, local copies, waits for them, and re-layouts: 80.5 us -> 6.76 us  [the longest x1 2.99 us: shards(): out_term = matmul_tn(attended_low, block_grad_attn).astype(BF16)]
    psum x1 -> x0, waiting for transfers between devices: 53.2 us -> none  [shards(): lax.psum(ffn_part.astype(jnp.bfloat16), 'head').astype(jnp.float32)]
  transfers between devices with their start and end apart: 20 -> 142, of which waited for: 18 -> 54; matrix products, arithmetic and copies ran while one was open for 8% -> 47% of each run, Pallas kernels for 0% -> 0%
where the time goes in v1:
time: 1500 us; the launch traced here: 1480 us
  waiting for transfers between devices  509 us (34%)
  local copies, waits for them, and re-layouts  483 us (32%)
  starting transfers between devices  222 us (15%)
  matrix products  153 us (10%)
  other arithmetic  109 us (7%)
    ppermute x74, waiting for transfers between devices, send_by(): lax.ppermute(values, axis, [(i, (i + step) % size) for i in range(size)])  346 us
    ppermute x74, starting transfers between devices, send_by(): lax.ppermute(values, axis, [(i, (i + step) % size) for i in range(size)])  177 us
    ppermute x68, waiting for transfers between devices, swap_bit(): return lax.ppermute(values, axis, [(i, i ^ bit) for i in range(size)])  163 us
    dynamic_update_slice x20, local copies, waits for them, and re-layouts, head_exchange(): result = lax.dynamic_update_slice_in_dim(result, came, own ^ other, 0)  102 us
    dynamic_update_slice x16, local copies, waits for them, and re-layouts, gather_pieces(): lax.dynamic_update_slice(result, other[None, None], (place_x, place) + (0...  69.8 us
    dynamic_update_slice x16, local copies, waits for them, and re-layouts, gather_pieces(): lax.dynamic_update_slice(result, came[None, None], (x, place) + (0,) * ow...  68.8 us
    dynamic_update_slice x4, local copies, waits for them, and re-layouts, in_order(): lax.dynamic_update_slice_in_dim(result, part[None], lax.rem(z - k + size_...  60.2 us
    dot_general x10, matrix products, matmul_nt(): lax.dot_general(left, right, (((1,), (1,)), ((), ())), preferred_element_...  51.7 us
  transfers between devices with their start and end apart: 142, of which 54 were waited for; matrix products, arithmetic and copies ran while one was open for 47% of the time, Pallas kernels for 0%

profile of v1, /device:TPU:0, one launch (start us, length us, event | category | flops | bytes accessed | tf_op | source)
XLA Modules:
  0.0 1480.5 jit_solution(780944235210293449)
XLA Ops:
  94.0 12.5 dynamic_update_slice.188
  138.8 12.5 collective-permute-start.38
  158.6 12.5 dynamic_update_slice.189
  171.1 12.5 dynamic_update_slice.190
  196.8 26.5 %collective-permute-start.11 = (bf16[288,1024]{1,0:T(8,128)(2,1)S(1)}, bf16[288,1024]{1,0:T(8,128)(2,1)}, u32[]{:S(2)}, u32[]{:S(2)}) collective-permute-start(bf16[288,1024]{1,0:T(8,128)(2,1)S(1)} %bitcast.452), channel_id=1, source_target_pairs={{0,4},{4,8},{8,12},{12,0},{1,5},{5,9},{9,13},{13,1},{2,6},{6,10},{... | collective-permute-start | bytes 1769480 | tf_op jit(solution)/shard_map/ppermute | solution.py:31
  239.3 12.5 dynamic_update_slice.191
  251.9 12.6 dynamic_update_slice.192
  264.5 12.5 dynamic_update_slice.193
  277.0 12.5 dynamic_update_slice.194
  289.5 12.5 dynamic_update_slice.195
  331.9 18.6 %dynamic_update_slice.196 = bf16[4,512,576]{1,0,2:T(4,128)(2,1)S(1)} dynamic-update-slice(bf16[4,512,576]{1,0,2:T(4,128)(2,1)S(1)} %reshape.1022, bf16[1,512,576]{1,0,2:T(2,128)(2,1)} %copy.220, s32[]{:T(128)S(6)} %select_n.228, s32[]{:T(128)} %constant.277.clone.1, s32[]{:T(128)} %constant.277.clone.1) | dynamic-update-slice | bytes 1179652 | tf_op jit(solution)/shard_map/dynamic_update_slice | solution.py:75
  355.0 18.6 %dynamic_update_slice.197 = bf16[4,512,576]{1,0,2:T(4,128)(2,1)S(1)} dynamic-update-slice(bf16[4,512,576]{1,0,2:T(4,128)(2,1)S(1)} %dynamic_update_slice.196, bf16[1,512,576]{1,0,2:T(2,128)(2,1)} %copy.222, s32[]{:T(128)S(6)} %select_n.410, s32[]{:T(128)} %constant.277.clone.1, s32[]{:T(128)} %constant.277.clone.1) | dynamic-update-slice | bytes 1179652 | tf_op jit(solution)/shard_map/dynamic_update_slice | solution.py:75
  377.8 19.0 %dynamic_update_slice.198 = bf16[4,512,576]{1,0,2:T(4,128)(2,1)S(1)} dynamic-update-slice(bf16[4,512,576]{1,0,2:T(4,128)(2,1)S(1)} %dynamic_update_slice.197, bf16[1,512,576]{1,0,2:T(2,128)(2,1)} %copy.224, s32[]{:T(128)S(6)} %select_n.411, s32[]{:T(128)} %constant.277.clone.1, s32[]{:T(128)} %constant.277.clone.1) | dynamic-update-slice | bytes 1179652 | tf_op jit(solution)/shard_map/dynamic_update_slice | solution.py:75
  429.3 10.4 collective-permute-done.19
  439.8 23.8 %collective-permute-start.17 = (bf16[2,1,512,256]{3,2,1,0:T(8,128)(2,1)S(1)}, bf16[2,1,512,256]{3,2,1,0:T(8,128)(2,1)S(1)}, u32[]{:S(2)}, u32[]{:S(2)}) collective-permute-start(bf16[2,1,512,256]{3,2,1,0:T(8,128)(2,1)S(1)} %pad_maximum_fusion.19), channel_id=1, source_target_pairs={{0,4},{4,8},{8,12},{12,0},{1,5},{5,9},{9,13},{13,1},{2,6},{6,10},{... | collective-permute-start | bytes 1572872 | tf_op jit(solution)/shard_map/ppermute | solution.py:31
  493.4 10.9 collective-permute-done.34
  522.5 36.4 %collective-permute-done.59 = bf16[128,2304]{1,0:T(8,128)(2,1)S(1)} collective-permute-done((bf16[128,2304]{1,0:T(8,128)(2,1)S(1)}, bf16[128,2304]{1,0:T(8,128)(2,1)S(1)}, u32[]{:S(2)}, u32[]{:S(2)}) %collective-permute-start.59) | collective-permute-done | bytes 589856 | tf_op jit(solution)/shard_map/ppermute | solution.py:31
  562.0 13.2 collective-permute-done.60
  575.3 10.6 collective-permute-done.54
  641.7 23.6 %collective-permute-done.69 = bf16[128,2304]{1,0:T(8,128)(2,1)S(1)} collective-permute-done((bf16[128,2304]{1,0:T(8,128)(2,1)S(1)}, bf16[128,2304]{1,0:T(8,128)(2,1)S(1)}, u32[]{:S(2)}, u32[]{:S(2)}) %collective-permute-start.69) | collective-permute-done | bytes 589856 | tf_op jit(solution)/shard_map/ppermute | solution.py:36
  665.4 12.5 collective-permute-done.63
  678.1 12.0 collective-permute-done.57
  692.3 14.8 %collective-permute-done.64 = bf16[128,2304]{1,0:T(8,128)(2,1)S(1)} collective-permute-done((bf16[128,2304]{1,0:T(8,128)(2,1)S(1)}, bf16[128,2304]{1,0:T(8,128)(2,1)S(1)}, u32[]{:S(2)}, u32[]{:S(2)}) %collective-permute-start.64) | collective-permute-done | bytes 589856 | tf_op jit(solution)/shard_map/ppermute | solution.py:31
  707.1 10.6 collective-permute-done.58
  728.0 8.7 collective-permute-done.87
  737.4 38.4 %collective-permute-done.81 = bf16[128,2304]{1,0:T(8,128)(2,1)S(1)} collective-permute-done((bf16[128,2304]{1,0:T(8,128)(2,1)S(1)}, bf16[128,2304]{1,0:T(8,128)(2,1)S(1)}, u32[]{:S(2)}, u32[]{:S(2)}) %collective-permute-start.81) | collective-permute-done | bytes 589856 | tf_op jit(solution)/shard_map/ppermute | solution.py:31
  778.9 13.2 collective-permute-done.82
  792.2 10.6 collective-permute-done.76
  850.7 10.3 fusion.13
  867.4 15.4 %fusion.4 = f32[2304,1152]{1,0:T(8,128)S(1)} fusion(bf16[2048,2304]{1,0:T(8,128)(2,1)} %constant_dynamic-update-slice_fusion.6, bf16[512,1152]{1,0:T(8,128)(2,1)S(1)} %copy-done.65, bf16[512,1152]{1,0:T(8,128)(2,1)S(1)} %copy-done.67, bf16[512,1152]{1,0:T(8,128)(2,1)S(1)} %pad_maximum_fusion.10, bf16[512,1152]{1,0:T(8,128)(2,1)S(1)} %copy-done.63), kind=kOutput, calls=%fused_computation.9 | convolution fusion | flops 10890510336 | bytes 24772608 | tf_op jit(solution)/shard_map/dot_general | solution.py:157
  882.8 9.8 convolution_convert_fusion.2
  933.5 15.0 %dynamic_update_slice.228 = f32[4,288,576]{2,0,1:T(4,128)} dynamic-update-slice(f32[4,288,576]{2,0,1:T(4,128)} %broadcast_in_dim.255, f32[1,288,576]{2,0,1:T(1,128)S(1)} %copy.258, s32[]{:T(128)S(6)} %select_n.413, s32[]{:T(128)} %constant.277.clone.1, s32[]{:T(128)} %constant.277.clone.1) | dynamic-update-slice | bytes 1327108 | tf_op jit(solution)/shard_map/dynamic_update_slice | solution.py:393
  957.9 10.4 collective-permute-done.134
  973.7 15.1 %dynamic_update_slice.229 = f32[4,288,576]{2,0,1:T(4,128)} dynamic-update-slice(f32[4,288,576]{2,0,1:T(4,128)} %dynamic_update_slice.228, f32[1,288,576]{2,0,1:T(1,128)} %copy.259, s32[]{:T(128)S(6)} %select_n.415, s32[]{:T(128)} %constant.277.clone.1, s32[]{:T(128)} %constant.277.clone.1) | dynamic-update-slice | bytes 1327108 | tf_op jit(solution)/shard_map/dynamic_update_slice | solution.py:393
  988.8 15.1 %dynamic_update_slice.230 = f32[4,288,576]{2,0,1:T(4,128)} dynamic-update-slice(f32[4,288,576]{2,0,1:T(4,128)} %dynamic_update_slice.229, f32[1,288,576]{2,0,1:T(1,128)} %copy.260, s32[]{:T(128)S(6)} %select_n.416, s32[]{:T(128)} %constant.277.clone.1, s32[]{:T(128)} %constant.277.clone.1) | dynamic-update-slice | bytes 1327108 | tf_op jit(solution)/shard_map/dynamic_update_slice | solution.py:393
  1003.9 15.1 %dynamic_update_slice.231 = f32[4,288,576]{2,0,1:T(4,128)} dynamic-update-slice(f32[4,288,576]{2,0,1:T(4,128)} %dynamic_update_slice.230, f32[1,288,576]{2,0,1:T(1,128)} %copy.261, s32[]{:T(128)S(6)} %select_n.417, s32[]{:T(128)} %constant.277.clone.1, s32[]{:T(128)} %constant.277.clone.1) | dynamic-update-slice | bytes 1327108 | tf_op jit(solution)/shard_map/dynamic_update_slice | solution.py:393
  1023.5 8.7 multiply_subtract_fusion.1
  1047.6 14.0 collective-permute-done.91
  1062.3 12.0 collective-permute-done.85
  1104.0 17.1 %collective-permute-done.86 = bf16[128,2304]{1,0:T(8,128)(2,1)S(1)} collective-permute-done((bf16[128,2304]{1,0:T(8,128)(2,1)S(1)}, bf16[128,2304]{1,0:T(8,128)(2,1)S(1)}, u32[]{:S(2)}, u32[]{:S(2)}) %collective-permute-start.86) | collective-permute-done | bytes 589856 | tf_op jit(solution)/shard_map/ppermute | solution.py:31
  1124.2 36.6 %collective-permute-done.127 = bf16[288,1152]{1,0:T(8,128)(2,1)S(1)} collective-permute-done((bf16[288,1152]{1,0:T(8,128)(2,1)S(1)}, bf16[288,1152]{1,0:T(8,128)(2,1)S(1)}, u32[]{:S(2)}, u32[]{:S(2)}) %collective-permute-start.127) | collective-permute-done | bytes 663584 | tf_op jit(solution)/shard_map/ppermute | solution.py:31
  1171.4 9.0 copy.256
  1188.3 15.0 %multiply_subtract_fusion = (f32[2,288,2304]{2,1,0:T(8,128)}, f32[2,288,2304]{2,1,0:T(8,128)}, f32[2,288,2304]{2,1,0:T(8,128)}) fusion(f32[2,288,2304]{2,1,0:T(8,128)} %param.27, f32[2,288,2304]{2,1,0:T(8,128)} %reshape.1055, f32[2,288,2304]{2,1,0:T(8,128)} %param.29, f32[2,288,2304]{2,1,0:T(8,128)} %param.28), kind=kLoop, calls=%fused_computation.4 | loop fusion | flops 19906560 | bytes 37158912 | tf_op jit(solution)/shard_map/sub | solution.py:202
  1219.5 13.5 collective-permute-start.97
  1258.6 22.5 %collective-permute-done.95 = bf16[2,1,512,256]{3,2,1,0:T(8,128)(2,1)} collective-permute-done((bf16[2,1,512,256]{3,2,1,0:T(8,128)(2,1)}, bf16[2,1,512,256]{3,2,1,0:T(8,128)(2,1)}, u32[]{:S(2)}, u32[]{:S(2)}) %collective-permute-start.95) | collective-permute-done | bytes 524320 | tf_op jit(solution)/shard_map/ppermute | solution.py:31
  1348.5 12.1 collective-permute-done.105
  1360.6 12.6 collective-permute-done.103
  1395.2 29.3 %collective-permute-done.104 = bf16[288,1024]{1,0:T(8,128)(2,1)} collective-permute-done((bf16[288,1024]{1,0:T(8,128)(2,1)}, bf16[288,1024]{1,0:T(8,128)(2,1)}, u32[]{:S(2)}, u32[]{:S(2)}) %collective-permute-start.104) | collective-permute-done | bytes 589856 | tf_op jit(solution)/shard_map/ppermute | solution.py:31
  (902 shorter events, 722.4 us)
Async XLA Ops:
  1.3 52.9 %collective-permute-start.2 = (bf16[4,72]{1,0:T(4,128)(2,1)S(1)}, bf16[4,72]{1,0:T(4,128)(2,1)S(1)}, u32[]{:S(2)}, u32[]{:S(2)}) collective-permute-start(bf16[4,72]{1,0:T(4,128)(2,1)S(1)} %convert_bitcast_fusion.2), channel_id=1, source_target_pairs={{0,1},{1,0},{2,3},{3,2},{4,5},{5,4},{6,7},{7,6},{8,9},{9,8},{10,11... | collective-permute-start | bytes 1736 | tf_op jit(solution)/shard_map/ppermute | solution.py:36
  5.7 82.4 %collective-permute-start.7 = (bf16[1,72,1024]{2,0,1:T(2,128)(2,1)}, bf16[1,72,1024]{2,0,1:T(2,128)(2,1)}, u32[]{:S(2)}, u32[]{:S(2)}) collective-permute-start(bf16[1,72,1024]{2,0,1:T(2,128)(2,1)} %get-tuple-element.129), channel_id=1, source_target_pairs={{0,1},{1,0},{2,3},{3,2},{4,5},{5,4},{6,7},{7,6},{8,9},{9,8},{10,11... | collective-permute-start | bytes 442376 | tf_op jit(solution)/shard_map/ppermute | solution.py:36
  7.5 64.8 %collective-permute-start.20 = (bf16[1,64,576]{2,0,1:T(2,128)(2,1)}, bf16[1,64,576]{2,0,1:T(2,128)(2,1)}, u32[]{:S(2)}, u32[]{:S(2)}) collective-permute-start(bf16[1,64,576]{2,0,1:T(2,128)(2,1)} %get-tuple-element.143), channel_id=1, source_target_pairs={{0,1},{1,0},{2,3},{3,2},{4,5},{5,4},{6,7},{7,6},{8,9},{9,8},{10,11... | collective-permute-start | bytes 221192 | tf_op jit(solution)/shard_map/ppermute | solution.py:36
  7.9 69.6 %collective-permute-start.21 = (bf16[1,64,576]{2,0,1:T(2,128)(2,1)}, bf16[1,64,576]{2,0,1:T(2,128)(2,1)}, u32[]{:S(2)}, u32[]{:S(2)}) collective-permute-start(bf16[1,64,576]{2,0,1:T(2,128)(2,1)} %get-tuple-element.142), channel_id=1, source_target_pairs={{0,2},{1,3},{2,0},{3,1},{4,6},{5,7},{6,4},{7,5},{8,10},{9,11},{10,... | collective-permute-start | bytes 221192 | tf_op jit(solution)/shard_map/ppermute | solution.py:36
  10.4 71.0 %collective-permute-start.22 = (bf16[1,64,576]{2,0,1:T(2,128)(2,1)}, bf16[1,64,576]{2,0,1:T(2,128)(2,1)}, u32[]{:S(2)}, u32[]{:S(2)}) collective-permute-start(bf16[1,64,576]{2,0,1:T(2,128)(2,1)} %get-tuple-element.141), channel_id=1, source_target_pairs={{0,3},{1,2},{2,1},{3,0},{4,7},{5,6},{6,5},{7,4},{8,11},{9,10},{10,... | collective-permute-start | bytes 221192 | tf_op jit(solution)/shard_map/ppermute | solution.py:36
  81.4 44.7 %collective-permute-start.44 = (bf16[288,576]{1,0:T(8,128)(2,1)}, bf16[288,576]{1,0:T(8,128)(2,1)S(1)}, u32[]{:S(2)}, u32[]{:S(2)}) collective-permute-start(bf16[288,576]{1,0:T(8,128)(2,1)} %bitcast.426), channel_id=1, source_target_pairs={{0,16},{16,0},{1,17},{17,1},{2,18},{18,2},{3,19},{19,3},{4,20},{20... | collective-permute-start | bytes 995336 | tf_op jit(solution)/shard_map/ppermute | solution.py:31
  111.4 75.0 %collective-permute-start.37 = (bf16[288,1152]{1,0:T(8,128)(2,1)}, bf16[288,1152]{1,0:T(8,128)(2,1)}, u32[]{:S(2)}, u32[]{:S(2)}) collective-permute-start(bf16[288,1152]{1,0:T(8,128)(2,1)} %get-tuple-element.95), channel_id=1, source_target_pairs={{0,16},{16,0},{1,17},{17,1},{2,18},{18,2},{3,19},{19,3},{4,20},{20... | collective-permute-start | bytes 1990664 | tf_op jit(solution)/shard_map/ppermute | solution.py:31
  116.9 66.8 %collective-permute-start = (bf16[128,2304]{1,0:T(8,128)(2,1)S(1)}, bf16[128,2304]{1,0:T(8,128)(2,1)}, u32[]{:S(2)}, u32[]{:S(2)}) collective-permute-start(bf16[128,2304]{1,0:T(8,128)(2,1)S(1)} %copy-done.2), channel_id=1, source_target_pairs={{0,2},{1,3},{2,0},{3,1},{4,6},{5,7},{6,4},{7,5},{8,10},{9,11},{10,... | collective-permute-start | bytes 1769480 | tf_op jit(solution)/shard_map/ppermute | solution.py:36
  138.8 51.1 %collective-permute-start.38 = (bf16[288,1152]{1,0:T(8,128)(2,1)}, bf16[288,1152]{1,0:T(8,128)(2,1)}, u32[]{:S(2)}, u32[]{:S(2)}) collective-permute-start(bf16[288,1152]{1,0:T(8,128)(2,1)} %get-tuple-element.97), channel_id=1, source_target_pairs={{0,4},{4,8},{8,12},{12,0},{1,5},{5,9},{9,13},{13,1},{2,6},{6,10},{... | collective-permute-start | bytes 1990664 | tf_op jit(solution)/shard_map/ppermute | solution.py:31
  152.9 43.9 %collective-permute-start.47 = (bf16[288,576]{1,0:T(8,128)(2,1)}, bf16[288,576]{1,0:T(8,128)(2,1)}, u32[]{:S(2)}, u32[]{:S(2)}) collective-permute-start(bf16[288,576]{1,0:T(8,128)(2,1)} %bitcast.420), channel_id=1, source_target_pairs={{0,8},{4,12},{8,0},{12,4},{1,9},{5,13},{9,1},{13,5},{2,10},{6,14},... | collective-permute-start | bytes 995336 | tf_op jit(solution)/shard_map/ppermute | solution.py:31
  155.3 165.4 %collective-permute-start.10 = (bf16[288,1024]{1,0:T(8,128)(2,1)S(1)}, bf16[288,1024]{1,0:T(8,128)(2,1)}, u32[]{:S(2)}, u32[]{:S(2)}) collective-permute-start(bf16[288,1024]{1,0:T(8,128)(2,1)S(1)} %bitcast.451), channel_id=1, source_target_pairs={{0,16},{16,0},{1,17},{17,1},{2,18},{18,2},{3,19},{19,3},{4,20},{20... | collective-permute-start | bytes 1769480 | tf_op jit(solution)/shard_map/ppermute | solution.py:31
  196.8 124.5 %collective-permute-start.11 = (bf16[288,1024]{1,0:T(8,128)(2,1)S(1)}, bf16[288,1024]{1,0:T(8,128)(2,1)}, u32[]{:S(2)}, u32[]{:S(2)}) collective-permute-start(bf16[288,1024]{1,0:T(8,128)(2,1)S(1)} %bitcast.452), channel_id=1, source_target_pairs={{0,4},{4,8},{8,12},{12,0},{1,5},{5,9},{9,13},{13,1},{2,6},{6,10},{... | collective-permute-start | bytes 1769480 | tf_op jit(solution)/shard_map/ppermute | solution.py:31
  223.3 99.1 %collective-permute-start.13 = (bf16[288,1024]{1,0:T(8,128)(2,1)S(1)}, bf16[288,1024]{1,0:T(8,128)(2,1)}, u32[]{:S(2)}, u32[]{:S(2)}) collective-permute-start(bf16[288,1024]{1,0:T(8,128)(2,1)S(1)} %bitcast.453), channel_id=1, source_target_pairs={{0,8},{4,12},{8,0},{12,4},{1,9},{5,13},{9,1},{13,5},{2,10},{6,14},... | collective-permute-start | bytes 1769480 | tf_op jit(solution)/shard_map/ppermute | solution.py:31
  228.0 82.5 %collective-permute-start.48 = (bf16[288,576]{1,0:T(8,128)(2,1)}, bf16[288,576]{1,0:T(8,128)(2,1)}, u32[]{:S(2)}, u32[]{:S(2)}) collective-permute-start(bf16[288,576]{1,0:T(8,128)(2,1)} %collective-permute-done.47), channel_id=1, source_target_pairs={{0,16},{16,0},{1,17},{17,1},{2,18},{18,2},{3,19},{19,3},{4,20},{20... | collective-permute-start | bytes 995336 | tf_op jit(solution)/shard_map/ppermute | solution.py:31
  233.7 80.6 %collective-permute-start.49 = (bf16[288,576]{1,0:T(8,128)(2,1)}, bf16[288,576]{1,0:T(8,128)(2,1)}, u32[]{:S(2)}, u32[]{:S(2)}) collective-permute-start(bf16[288,576]{1,0:T(8,128)(2,1)} %bitcast.484), channel_id=1, source_target_pairs={{0,12},{4,0},{8,4},{12,8},{1,13},{5,1},{9,5},{13,9},{2,14},{6,2},{... | collective-permute-start | bytes 995336 | tf_op jit(solution)/shard_map/ppermute | solution.py:31
  314.3 84.6 %collective-permute-start.15 = (bf16[288,1024]{1,0:T(8,128)(2,1)S(1)}, bf16[288,1024]{1,0:T(8,128)(2,1)}, u32[]{:S(2)}, u32[]{:S(2)}) collective-permute-start(bf16[288,1024]{1,0:T(8,128)(2,1)S(1)} %bitcast.454), channel_id=1, source_target_pairs={{0,12},{4,0},{8,4},{12,8},{1,13},{5,1},{9,5},{13,9},{2,14},{6,2},{... | collective-permute-start | bytes 1769480 | tf_op jit(solution)/shard_map/ppermute | solution.py:31
  321.3 52.4 %collective-permute-start.32 = (bf16[1,512,576]{1,2,0:T(8,128)(2,1)}, bf16[1,512,576]{1,2,0:T(8,128)(2,1)}, u32[]{:S(2)}, u32[]{:S(2)}) collective-permute-start(bf16[1,512,576]{1,2,0:T(8,128)(2,1)} %copy.223), channel_id=1, source_target_pairs={{0,3},{1,2},{2,1},{3,0},{4,7},{5,6},{6,5},{7,4},{8,11},{9,10},{10,... | collective-permute-start | bytes 1769480 | tf_op jit(solution)/shard_map/ppermute | solution.py:36
  322.3 76.6 %collective-permute-start.12 = (bf16[288,1024]{1,0:T(8,128)(2,1)}, bf16[288,1024]{1,0:T(8,128)(2,1)}, u32[]{:S(2)}, u32[]{:S(2)}) collective-permute-start(bf16[288,1024]{1,0:T(8,128)(2,1)} %collective-permute-done.11), channel_id=1, source_target_pairs={{0,16},{16,0},{1,17},{17,1},{2,18},{18,2},{3,19},{19,3},{4,20},{20... | collective-permute-start | bytes 1769480 | tf_op jit(solution)/shard_map/ppermute | solution.py:31
  326.5 76.7 %collective-permute-start.14 = (bf16[288,1024]{1,0:T(8,128)(2,1)}, bf16[288,1024]{1,0:T(8,128)(2,1)}, u32[]{:S(2)}, u32[]{:S(2)}) collective-permute-start(bf16[288,1024]{1,0:T(8,128)(2,1)} %collective-permute-done.13), channel_id=1, source_target_pairs={{0,16},{16,0},{1,17},{17,1},{2,18},{18,2},{3,19},{19,3},{4,20},{20... | collective-permute-start | bytes 1769480 | tf_op jit(solution)/shard_map/ppermute | solution.py:31
  350.6 113.5 %collective-permute-start.40 = (bf16[288,1152]{1,0:T(8,128)(2,1)}, bf16[288,1152]{1,0:T(8,128)(2,1)}, u32[]{:S(2)}, u32[]{:S(2)}) collective-permute-start(bf16[288,1152]{1,0:T(8,128)(2,1)} %get-tuple-element.96), channel_id=1, source_target_pairs={{0,8},{4,12},{8,0},{12,4},{1,9},{5,13},{9,1},{13,5},{2,10},{6,14},... | collective-permute-start | bytes 1990664 | tf_op jit(solution)/shard_map/ppermute | solution.py:31
  373.6 91.1 %collective-permute-start.42 = (bf16[288,1152]{1,0:T(8,128)(2,1)}, bf16[288,1152]{1,0:T(8,128)(2,1)}, u32[]{:S(2)}, u32[]{:S(2)}) collective-permute-start(bf16[288,1152]{1,0:T(8,128)(2,1)} %get-tuple-element.94), channel_id=1, source_target_pairs={{0,12},{4,0},{8,4},{12,8},{1,13},{5,1},{9,5},{13,9},{2,14},{6,2},{... | collective-permute-start | bytes 1990664 | tf_op jit(solution)/shard_map/ppermute | solution.py:31
  403.2 79.2 %collective-permute-start.50 = (bf16[288,576]{1,0:T(8,128)(2,1)}, bf16[288,576]{1,0:T(8,128)(2,1)}, u32[]{:S(2)}, u32[]{:S(2)}) collective-permute-start(bf16[288,576]{1,0:T(8,128)(2,1)} %collective-permute-done.49), channel_id=1, source_target_pairs={{0,16},{16,0},{1,17},{17,1},{2,18},{18,2},{3,19},{19,3},{4,20},{20... | collective-permute-start | bytes 995336 | tf_op jit(solution)/shard_map/ppermute | solution.py:31
  427.3 45.1 %collective-permute-start.18 = (bf16[2,1,512,256]{3,2,1,0:T(8,128)(2,1)S(1)}, bf16[2,1,512,256]{3,2,1,0:T(8,128)(2,1)S(1)}, u32[]{:S(2)}, u32[]{:S(2)}) collective-permute-start(bf16[2,1,512,256]{3,2,1,0:T(8,128)(2,1)S(1)} %pad_maximum_fusion.19), channel_id=1, source_target_pairs={{0,8},{4,12},{8,0},{12,4},{1,9},{5,13},{9,1},{13,5},{2,10},{6,14},... | collective-permute-start | bytes 1572872 | tf_op jit(solution)/shard_map/ppermute | solution.py:31
  509.3 49.5 %collective-permute-start.59 = (bf16[128,2304]{1,0:T(8,128)(2,1)S(1)}, bf16[128,2304]{1,0:T(8,128)(2,1)S(1)}, u32[]{:S(2)}, u32[]{:S(2)}) collective-permute-start(bf16[128,2304]{1,0:T(8,128)(2,1)S(1)} %get-tuple-element.51), channel_id=1, source_target_pairs={{0,8},{4,12},{8,0},{12,4},{1,9},{5,13},{9,1},{13,5},{2,10},{6,14},... | collective-permute-start | bytes 1769480 | tf_op jit(solution)/shard_map/ppermute | solution.py:31
  510.9 48.5 %collective-permute-start.53 = (bf16[128,2304]{1,0:T(8,128)(2,1)S(1)}, bf16[128,2304]{1,0:T(8,128)(2,1)S(1)}, u32[]{:S(2)}, u32[]{:S(2)}) collective-permute-start(bf16[128,2304]{1,0:T(8,128)(2,1)S(1)} %get-tuple-element.51), channel_id=1, source_target_pairs={{0,4},{4,8},{8,12},{12,0},{1,5},{5,9},{9,13},{13,1},{2,6},{6,10},{... | collective-permute-start | bytes 1769480 | tf_op jit(solution)/shard_map/ppermute | solution.py:31
  522.5 63.6 %collective-permute-start.36 = (bf16[256,2304]{1,0:T(8,128)(2,1)S(1)}, bf16[256,2304]{1,0:T(8,128)(2,1)S(1)}, u32[]{:S(2)}, u32[]{:S(2)}) collective-permute-start(bf16[256,2304]{1,0:T(8,128)(2,1)S(1)} %pad_maximum_fusion.3), channel_id=1, source_target_pairs={{0,1},{1,0},{2,3},{3,2},{4,5},{5,4},{6,7},{7,6},{8,9},{9,8},{10,11... | collective-permute-start | bytes 3538952 | tf_op jit(solution)/shard_map/ppermute | solution.py:36
  636.4 55.9 %collective-permute-start.52 = (bf16[128,2304]{1,0:T(8,128)(2,1)S(1)}, bf16[128,2304]{1,0:T(8,128)(2,1)S(1)}, u32[]{:S(2)}, u32[]{:S(2)}) collective-permute-start(bf16[128,2304]{1,0:T(8,128)(2,1)S(1)} %slice.672), channel_id=1, source_target_pairs={{0,2},{1,3},{2,0},{3,1},{4,6},{5,7},{6,4},{7,5},{8,10},{9,11},{10,... | collective-permute-start | bytes 1769480 | tf_op jit(solution)/shard_map/ppermute | solution.py:36
  640.1 50.0 %collective-permute-start.57 = (bf16[128,2304]{1,0:T(8,128)(2,1)S(1)}, bf16[128,2304]{1,0:T(8,128)(2,1)S(1)}, u32[]{:S(2)}, u32[]{:S(2)}) collective-permute-start(bf16[128,2304]{1,0:T(8,128)(2,1)S(1)} %slice.671), channel_id=1, source_target_pairs={{0,2},{1,3},{2,0},{3,1},{4,6},{5,7},{6,4},{7,5},{8,10},{9,11},{10,... | collective-permute-start | bytes 1769480 | tf_op jit(solution)/shard_map/ppermute | solution.py:36
  722.7 53.1 %collective-permute-start.81 = (bf16[128,2304]{1,0:T(8,128)(2,1)S(1)}, bf16[128,2304]{1,0:T(8,128)(2,1)S(1)}, u32[]{:S(2)}, u32[]{:S(2)}) collective-permute-start(bf16[128,2304]{1,0:T(8,128)(2,1)S(1)} %get-tuple-element.46), channel_id=1, source_target_pairs={{0,8},{4,12},{8,0},{12,4},{1,9},{5,13},{9,1},{13,5},{2,10},{6,14},... | collective-permute-start | bytes 1769480 | tf_op jit(solution)/shard_map/ppermute | solution.py:31
  726.1 50.3 %collective-permute-start.75 = (bf16[128,2304]{1,0:T(8,128)(2,1)S(1)}, bf16[128,2304]{1,0:T(8,128)(2,1)S(1)}, u32[]{:S(2)}, u32[]{:S(2)}) collective-permute-start(bf16[128,2304]{1,0:T(8,128)(2,1)S(1)} %get-tuple-element.46), channel_id=1, source_target_pairs={{0,4},{4,8},{8,12},{12,0},{1,5},{5,9},{9,13},{13,1},{2,6},{6,10},{... | collective-permute-start | bytes 1769480 | tf_op jit(solution)/shard_map/ppermute | solution.py:31
  736.7 42.0 %collective-permute-start.88 = (bf16[128,2304]{1,0:T(8,128)(2,1)S(1)}, bf16[128,2304]{1,0:T(8,128)(2,1)S(1)}, u32[]{:S(2)}, u32[]{:S(2)}) collective-permute-start(bf16[128,2304]{1,0:T(8,128)(2,1)S(1)} %collective-permute-done.87), channel_id=1, source_target_pairs={{0,2},{1,3},{2,0},{3,1},{4,6},{5,7},{6,4},{7,5},{8,10},{9,11},{10,... | collective-permute-start | bytes 1769480 | tf_op jit(solution)/shard_map/ppermute | solution.py:36
  737.3 65.7 %collective-permute-start.72 = (bf16[256,2304]{1,0:T(8,128)(2,1)S(1)}, bf16[256,2304]{1,0:T(8,128)(2,1)S(1)}, u32[]{:S(2)}, u32[]{:S(2)}) collective-permute-start(bf16[256,2304]{1,0:T(8,128)(2,1)S(1)} %pad_maximum_fusion.7), channel_id=1, source_target_pairs={{0,1},{1,0},{2,3},{3,2},{4,5},{5,4},{6,7},{7,6},{8,9},{9,8},{10,11... | collective-permute-start | bytes 3538952 | tf_op jit(solution)/shard_map/ppermute | solution.py:36
  814.6 133.9 %collective-permute-start.73 = (bf16[256,2304]{1,0:T(8,128)(2,1)S(1)}, bf16[256,2304]{1,0:T(8,128)(2,1)}, u32[]{:S(2)}, u32[]{:S(2)}) collective-permute-start(bf16[256,2304]{1,0:T(8,128)(2,1)S(1)} %slice.428), channel_id=1, source_target_pairs={{0,1},{1,0},{2,3},{3,2},{4,5},{5,4},{6,7},{7,6},{8,9},{9,8},{10,11... | collective-permute-start | bytes 3538952 | tf_op jit(solution)/shard_map/ppermute | solution.py:36
  905.8 130.6 %collective-permute-start.90 = (bf16[256,2304]{1,0:T(8,128)(2,1)}, bf16[256,2304]{1,0:T(8,128)(2,1)}, u32[]{:S(2)}, u32[]{:S(2)}) collective-permute-start(bf16[256,2304]{1,0:T(8,128)(2,1)} %slice.440), channel_id=1, source_target_pairs={{0,1},{1,0},{2,3},{3,2},{4,5},{5,4},{6,7},{7,6},{8,9},{9,8},{10,11... | collective-permute-start | bytes 3538952 | tf_op jit(solution)/shard_map/ppermute | solution.py:36
  913.7 129.6 %collective-permute-start.84 = (bf16[256,2304]{1,0:T(8,128)(2,1)}, bf16[256,2304]{1,0:T(8,128)(2,1)}, u32[]{:S(2)}, u32[]{:S(2)}) collective-permute-start(bf16[256,2304]{1,0:T(8,128)(2,1)} %slice.436), channel_id=1, source_target_pairs={{0,1},{1,0},{2,3},{3,2},{4,5},{5,4},{6,7},{7,6},{8,9},{9,8},{10,11... | collective-permute-start | bytes 3538952 | tf_op jit(solution)/shard_map/ppermute | solution.py:36
  921.6 110.6 %collective-permute-start.128 = (bf16[288,1152]{1,0:T(8,128)(2,1)}, bf16[288,1152]{1,0:T(8,128)(2,1)}, u32[]{:S(2)}, u32[]{:S(2)}) collective-permute-start(bf16[288,1152]{1,0:T(8,128)(2,1)} %get-tuple-element.67), channel_id=1, source_target_pairs={{0,16},{16,0},{1,17},{17,1},{2,18},{18,2},{3,19},{19,3},{4,20},{20... | collective-permute-start | bytes 1990664 | tf_op jit(solution)/shard_map/ppermute | solution.py:31
  968.4 63.9 %collective-permute-start.126 = (bf16[288,1152]{1,0:T(8,128)(2,1)}, bf16[288,1152]{1,0:T(8,128)(2,1)}, u32[]{:S(2)}, u32[]{:S(2)}) collective-permute-start(bf16[288,1152]{1,0:T(8,128)(2,1)} %get-tuple-element.68), channel_id=1, source_target_pairs={{0,16},{16,0},{1,17},{17,1},{2,18},{18,2},{3,19},{19,3},{4,20},{20... | collective-permute-start | bytes 1990664 | tf_op jit(solution)/shard_map/ppermute | solution.py:31
  970.5 62.4 %collective-permute-start.124 = (bf16[288,1152]{1,0:T(8,128)(2,1)}, bf16[288,1152]{1,0:T(8,128)(2,1)}, u32[]{:S(2)}, u32[]{:S(2)}) collective-permute-start(bf16[288,1152]{1,0:T(8,128)(2,1)} %get-tuple-element.69), channel_id=1, source_target_pairs={{0,16},{16,0},{1,17},{17,1},{2,18},{18,2},{3,19},{19,3},{4,20},{20... | collective-permute-start | bytes 1990664 | tf_op jit(solution)/shard_map/ppermute | solution.py:31
  1032.3 58.3 %collective-permute-start.123 = (bf16[288,1152]{1,0:T(8,128)(2,1)S(1)}, bf16[288,1152]{1,0:T(8,128)(2,1)S(1)}, u32[]{:S(2)}, u32[]{:S(2)}) collective-permute-start(bf16[288,1152]{1,0:T(8,128)(2,1)S(1)} %copy-done.76), channel_id=1, source_target_pairs={{0,16},{16,0},{1,17},{17,1},{2,18},{18,2},{3,19},{19,3},{4,20},{20... | collective-permute-start | bytes 1990664 | tf_op jit(solution)/shard_map/ppermute | solution.py:31
  1032.8 69.9 %collective-permute-start.74 = (bf16[128,2304]{1,0:T(8,128)(2,1)S(1)}, bf16[128,2304]{1,0:T(8,128)(2,1)S(1)}, u32[]{:S(2)}, u32[]{:S(2)}) collective-permute-start(bf16[128,2304]{1,0:T(8,128)(2,1)S(1)} %copy-done.85), channel_id=1, source_target_pairs={{0,2},{1,3},{2,0},{3,1},{4,6},{5,7},{6,4},{7,5},{8,10},{9,11},{10,... | collective-permute-start | bytes 1769480 | tf_op jit(solution)/shard_map/ppermute | solution.py:36
  1036.4 63.2 %collective-permute-start.125 = (bf16[288,1152]{1,0:T(8,128)(2,1)S(1)}, bf16[288,1152]{1,0:T(8,128)(2,1)S(1)}, u32[]{:S(2)}, u32[]{:S(2)}) collective-permute-start(bf16[288,1152]{1,0:T(8,128)(2,1)S(1)} %get-tuple-element.66), channel_id=1, source_target_pairs={{0,4},{4,8},{8,12},{12,0},{1,5},{5,9},{9,13},{13,1},{2,6},{6,10},{... | collective-permute-start | bytes 1990664 | tf_op jit(solution)/shard_map/ppermute | solution.py:31
  1099.6 61.3 %collective-permute-start.127 = (bf16[288,1152]{1,0:T(8,128)(2,1)S(1)}, bf16[288,1152]{1,0:T(8,128)(2,1)S(1)}, u32[]{:S(2)}, u32[]{:S(2)}) collective-permute-start(bf16[288,1152]{1,0:T(8,128)(2,1)S(1)} %get-tuple-element.65), channel_id=1, source_target_pairs={{0,8},{4,12},{8,0},{12,4},{1,9},{5,13},{9,1},{13,5},{2,10},{6,14},... | collective-permute-start | bytes 1990664 | tf_op jit(solution)/shard_map/ppermute | solution.py:31
  1102.8 59.2 %collective-permute-start.129 = (bf16[288,1152]{1,0:T(8,128)(2,1)S(1)}, bf16[288,1152]{1,0:T(8,128)(2,1)S(1)}, u32[]{:S(2)}, u32[]{:S(2)}) collective-permute-start(bf16[288,1152]{1,0:T(8,128)(2,1)S(1)} %get-tuple-element.64), channel_id=1, source_target_pairs={{0,12},{4,0},{8,4},{12,8},{1,13},{5,1},{9,5},{13,9},{2,14},{6,2},{... | collective-permute-start | bytes 1990664 | tf_op jit(solution)/shard_map/ppermute | solution.py:31
  1123.6 64.5 %collective-permute-start.93 = (bf16[128,2304]{1,0:T(8,128)(2,1)S(1)}, bf16[128,2304]{1,0:T(8,128)(2,1)S(1)}, u32[]{:S(2)}, u32[]{:S(2)}) collective-permute-start(bf16[128,2304]{1,0:T(8,128)(2,1)S(1)} %multiply_convert_fusion.12), channel_id=1, source_target_pairs={{0,2},{1,3},{2,0},{3,1},{4,6},{5,7},{6,4},{7,5},{8,10},{9,11},{10,... | collective-permute-start | bytes 1769480 | tf_op jit(solution)/shard_map/ppermute | solution.py:36
  1238.9 42.2 %collective-permute-start.95 = (bf16[2,1,512,256]{3,2,1,0:T(8,128)(2,1)}, bf16[2,1,512,256]{3,2,1,0:T(8,128)(2,1)}, u32[]{:S(2)}, u32[]{:S(2)}) collective-permute-start(bf16[2,1,512,256]{3,2,1,0:T(8,128)(2,1)} %pad_maximum_fusion.20), channel_id=1, source_target_pairs={{0,8},{4,12},{8,0},{12,4},{1,9},{5,13},{9,1},{13,5},{2,10},{6,14},... | collective-permute-start | bytes 1572872 | tf_op jit(solution)/shard_map/ppermute | solution.py:31
  1342.9 88.2 %collective-permute-start.98 = (bf16[256,2304]{1,0:T(8,128)(2,1)}, bf16[256,2304]{1,0:T(8,128)(2,1)}, u32[]{:S(2)}, u32[]{:S(2)}) collective-permute-start(bf16[256,2304]{1,0:T(8,128)(2,1)} %slice.450), channel_id=1, source_target_pairs={{0,1},{1,0},{2,3},{3,2},{4,5},{5,4},{6,7},{7,6},{8,9},{9,8},{10,11... | collective-permute-start | bytes 3538952 | tf_op jit(solution)/shard_map/ppermute | solution.py:36
  1343.4 46.4 %collective-permute-start.100 = (bf16[288,1024]{1,0:T(8,128)(2,1)S(1)}, bf16[288,1024]{1,0:T(8,128)(2,1)}, u32[]{:S(2)}, u32[]{:S(2)}) collective-permute-start(bf16[288,1024]{1,0:T(8,128)(2,1)S(1)} %get-tuple-element.71), channel_id=1, source_target_pairs={{0,16},{16,0},{1,17},{17,1},{2,18},{18,2},{3,19},{19,3},{4,20},{20... | collective-permute-start | bytes 1769480 | tf_op jit(solution)/shard_map/ppermute | solution.py:31
  1381.1 43.4 %collective-permute-start.104 = (bf16[288,1024]{1,0:T(8,128)(2,1)}, bf16[288,1024]{1,0:T(8,128)(2,1)}, u32[]{:S(2)}, u32[]{:S(2)}) collective-permute-start(bf16[288,1024]{1,0:T(8,128)(2,1)} %get-tuple-element.77), channel_id=1, source_target_pairs={{0,8},{4,12},{8,0},{12,4},{1,9},{5,13},{9,1},{13,5},{2,10},{6,14},... | collective-permute-start | bytes 1769480 | tf_op jit(solution)/shard_map/ppermute | solution.py:31
  (245 other events, 4330.5 us)

commit v2 on v1

v2 whole, which is shorter than its diff:
```python
import functools
import math

import jax
import jax.numpy as jnp
from jax import lax
from jax.experimental import pallas as pl
from jax.experimental.pallas import tpu as pltpu
from jax.sharding import PartitionSpec as P

QH = 8
KVH = 4
HD = 256
STEP = 10


SOFT_CAP = 50.0
EPS_NORM = 1e-06
ROPE_BASE = 10000.0
BETA_ONE = 0.9
BETA_TWO = 0.95
EPS_ADAM = 1e-08
RATE_MATRIX = 0.05
RATE_DOWN = 0.025
RATE_GAIN = 0.5
WEIGHT_DECAY = 0.1

BF16 = jnp.bfloat16
F32 = jnp.float32


def after(values, *others):
    return lax.optimization_barrier((values,) + others)[0]


class Line:
    def __init__(self, depth):
        self.depth = depth
        self.came = []

    def send(self, sendings):
        values = tuple(one for one, _, _ in sendings)
        if len(self.came) >= self.depth:
            values = after(values, *self.came[-self.depth])
        results = [
            lax.ppermute(one, axes, pairs) for one, (_, axes, pairs) in zip(values, sendings)
        ]
        self.came.append(tuple(results))
        return results


class Lines:
    def __init__(self):
        self.fsdp, self.ctx, self.head = Line(DEPTH), Line(DEPTH), Line(DEPTH)


DEPTH = 2


def ring_pairs(size, step):
    return [(i, (i + step) % size) for i in range(size)]


def swap_bit(lines, values, bit):
    size = lax.axis_size("head")
    pairs = [(i, i ^ bit) for i in range(size)]
    if bit == 1 and size > 2:
        return lax.ppermute(values, "head", pairs)
    return lines.head.send([(values, "head", pairs)])[0]


def send_ctx(lines, values, step):
    return lines.ctx.send([(values, "ctx", ring_pairs(lax.axis_size("ctx"), step))])[0]


def swap_fsdp(lines, values, valid=lambda z: True):
    size_x, size_z = lax.axis_size("fsdp"), lax.axis_size("ctx")
    return [
        lines.fsdp.send(
            [
                (
                    values,
                    ("fsdp", "ctx"),
                    [
                        (x * size_z + z, (x + step) % size_x * size_z + z)
                        for x in range(size_x)
                        for z in range(size_z)
                        if valid(z)
                    ],
                )
            ]
        )[0]
        for step in range(1, size_x)
    ]


def swap_top(lines, values, valid=lambda z: True):
    size_z, size_h = lax.axis_size("ctx"), lax.axis_size("head")
    pairs = [
        (z * size_h + h, z * size_h + (h ^ (size_h // 2)))
        for z in range(size_z)
        for h in range(size_h)
        if valid(z)
    ]
    return lines.head.send([(values, ("ctx", "head"), pairs)])


def head_bits():
    bits = []
    bit = lax.axis_size("head") // 2
    while bit:
        bits.append(bit)
        bit //= 2
    return bits


def head_order():
    order = [0]
    for bit in head_bits():
        order = order + [one ^ bit for one in order]
    return order


def head_gather(lines, rows, bits=None):
    for bit in head_bits() if bits is None else bits:
        rows = jnp.concatenate([rows, swap_bit(lines, rows, bit)], axis=0)
    return rows


def head_reduce(lines, part):
    for bit in reversed(head_bits()):
        half = part.shape[0] // 2
        came = swap_bit(lines, part[half:].astype(BF16), bit)
        part = part[:half].astype(F32) + came.astype(F32)
    return part


def head_exchange(lines, pieces):
    return [pieces[0]] + [swap_bit(lines, pieces[i], i) for i in range(1, len(pieces))]


AHEAD, BACK = [(0, 1), (1, 2), (2, 3)], [(1, 0), (2, 1), (3, 2)]
TWO, ENDS = [(0, 2), (1, 3), (2, 0), (3, 1)], [(2, 3), (1, 0)]
FAR = [(0, 1), (3, 2)]


def spread_ctx(lines, own, swaps):
    size = lax.axis_size("ctx")
    always = lambda z: z >= 0
    parts = [([own] + swaps(lines, own), lambda z: z, always)]
    if size != 4:
        for k in range(1, size):
            one = send_ctx(lines, own, k)
            source = lambda z, k=k: (z - k + size) % size
            parts.append(([one] + swaps(lines, one), source, always))
        return parts
    not_first, not_last, at_end = lambda z: z >= 1, lambda z: z <= 2, lambda z: z % 3 == 0
    ahead, back = lines.ctx.send([(own, "ctx", AHEAD), (own, "ctx", BACK)])
    two = lines.ctx.send([(after(own, ahead, back), "ctx", TWO)])[0]
    parts.append(([ahead] + swaps(lines, ahead, not_first), lambda z: z - 1, not_first))
    parts.append(([back] + swaps(lines, back, not_last), lambda z: z + 1, not_last))
    two = after(two, *parts[1][0][1:])
    ends = lines.ctx.send([(two, "ctx", ENDS)])[0]
    parts.append(([two] + swaps(lines, two), lambda z: z ^ 2, always))
    parts.append(([ends] + swaps(lines, ends, at_end), lambda z: 3 - z, at_end))
    return parts


def put_pieces(parts):
    size_x, size_z = lax.axis_size("fsdp"), lax.axis_size("ctx")
    x, z = lax.axis_index("fsdp"), lax.axis_index("ctx")
    arrays, places = [], []
    for by_step, source, valid in parts:
        for step, one in enumerate(by_step):
            at = lax.rem(x - step + size_x, size_x) * size_z + source(z)
            arrays.append(one)
            places.append(jnp.where(valid(z), at, -1))
    return place(arrays, places, size_x * size_z)


def ctx_slots(lines, values, swaps=lambda lines, values, valid=None: [], join=lambda arrays: arrays[0]):
    size = lax.axis_size("ctx")
    arrays = [join(by_step) for by_step, _, _ in spread_ctx(lines, values, swaps)]
    if size != 4:
        return [arrays[0]] + [arrays[size - k] for k in range(1, size)]
    z = lax.axis_index("ctx")
    own, ahead, back, two, ends = arrays
    return [own, jnp.where(z == 3, ends, back), two, jnp.where(z == 0, ends, ahead)]


def sum_ctx_slots(lines, part_of):
    size = lax.axis_size("ctx")
    z = lax.axis_index("ctx")
    if size != 4:
        total = 0.0
        for k in ctx_order():
            part = part_of(k)
            total = total + (send_ctx(lines, part.astype(BF16), k).astype(F32) if k else part)
        return total
    part_one = part_of(1).astype(BF16)
    part_three = part_of(3).astype(BF16)
    far = lines.ctx.send([(jnp.where(z == 0, part_three, part_one), "ctx", FAR)])[0]
    ahead, back = lines.ctx.send([(part_one, "ctx", AHEAD), (part_three, "ctx", BACK)])
    part_two = part_of(2).astype(F32) + far.astype(F32)
    two = lines.ctx.send([(part_two.astype(BF16), "ctx", TWO)])[0]
    return part_of(0).astype(F32) + ahead.astype(F32) + back.astype(F32) + two.astype(F32)


def far_first(size):
    return sorted(range(size), key=lambda k: -min(k, size - k))


def ctx_order():
    size = lax.axis_size("ctx")
    return [1, 3, 2, 0] if size == 4 else far_first(size)


def sum_over_fsdp(lines, pieces, order):
    size_x, size_z = lax.axis_size("fsdp"), lax.axis_size("ctx")
    x, z = lax.axis_index("fsdp"), lax.axis_index("ctx")
    chosen = [(k, step) for k in order for step in range(size_x)]
    picked = pick_pieces(
        pieces,
        [lax.rem(x + step, size_x) * size_z + lax.rem(z + k, size_z) for k, step in chosen],
    )
    picked = dict(zip(chosen, picked))
    sums = {}
    for k in order:
        total = picked[k, 0].astype(F32)
        for step in range(1, size_x):
            pairs = ring_pairs(size_x, step)
            total = total + lines.fsdp.send([(picked[k, step], "fsdp", pairs)])[0].astype(F32)
        sums[k] = total
    return sums


def exchange_all(pieces):
    return lax.all_to_all(
        pieces, ("fsdp", "ctx", "head"), split_axis=0, concat_axis=0, tiled=True
    )


def device_count():
    return lax.axis_size("fsdp") * lax.axis_size("ctx") * lax.axis_size("head")


def gather_gains(gains):
    rows = exchange_all(jnp.broadcast_to(gains.astype(BF16).T[None], (device_count(),) + gains.shape[::-1]))
    return jnp.transpose(rows, (1, 0, 2)).reshape(gains.shape[1], -1).astype(F32)


def scatter_gains(rows):
    pieces = jnp.transpose(rows.reshape(rows.shape[0], device_count(), -1), (1, 0, 2))
    return jnp.sum(exchange_all(pieces), axis=0).T


ANYWHERE = pl.BlockSpec(memory_space=pl.ANY)
SCALARS = pl.BlockSpec(memory_space=pltpu.SMEM)
IN_VMEM = pl.BlockSpec(memory_space=pltpu.VMEM)
VMEM_LIMIT = 48 * 1024 * 1024


def scalars(*values):
    return jnp.stack([jnp.asarray(one, jnp.int32) for one in values])


def cost(byte_count, flops=0):
    return pl.CostEstimate(flops=flops, bytes_accessed=byte_count, transcendentals=0)


def params():
    return pltpu.CompilerParams(vmem_limit_bytes=VMEM_LIMIT)


def place(pieces, places, total=None):
    count = len(pieces)
    shape = (total or count,) + pieces[0].shape

    def kernel(places_ref, *refs):
        out_ref, sems = refs[count], refs[count + 1]

        def each(act):
            for i in range(count):
                copy = pltpu.make_async_copy(
                    refs[i], out_ref.at[jnp.maximum(places_ref[i], 0)], sems.at[i]
                )
                pl.when(places_ref[i] >= 0)(functools.partial(act, copy))

        each(lambda copy: copy.start())
        each(lambda copy: copy.wait())

    return pl.pallas_call(
        kernel,
        out_shape=jax.ShapeDtypeStruct(shape, pieces[0].dtype),
        in_specs=[SCALARS] + [ANYWHERE] * count,
        out_specs=IN_VMEM,
        scratch_shapes=[pltpu.SemaphoreType.DMA((count,))],
        compiler_params=params(),
        cost_estimate=cost(2 * math.prod(shape) * pieces[0].dtype.itemsize),
        name="place",
    )(scalars(*places), *pieces)


def pick_pieces(stacked, places):
    count = len(places)
    shape = stacked.shape[1:]

    def kernel(places_ref, in_ref, *refs):
        sems = refs[count]
        copies = [
            pltpu.make_async_copy(in_ref.at[places_ref[i]], refs[i], sems.at[i])
            for i in range(count)
        ]
        for copy in copies:
            copy.start()
        for copy in copies:
            copy.wait()

    return pl.pallas_call(
        kernel,
        out_shape=[jax.ShapeDtypeStruct(shape, stacked.dtype)] * count,
        in_specs=[SCALARS, IN_VMEM],
        out_specs=[ANYWHERE] * count,
        scratch_shapes=[pltpu.SemaphoreType.DMA((count,))],
        compiler_params=params(),
        cost_estimate=cost(2 * count * math.prod(shape) * stacked.dtype.itemsize),
        name="pick_pieces",
    )(scalars(*places), stacked)


def kv_start(head):
    return lax.div(head * KVH, lax.axis_size("head")) * HD


def split_heads(weight, own):
    rows = weight.shape[0]
    size = lax.axis_size("head")
    query_cols, kv_cols = QH * HD // size, max(1, KVH // size) * HD
    local_cols = query_cols + 2 * kv_cols

    def kernel(own_ref, weight_ref, *outs):
        for other in range(size):
            head = own_ref[0] ^ other
            starts = (head * query_cols, QH * HD + kv_start(head), (QH + KVH) * HD + kv_start(head))
            at = 0
            for start, count in zip(starts, (query_cols, kv_cols, kv_cols)):
                columns = pl.ds(pl.multiple_of(start, HD), count)
                outs[other][:, at : at + count] = weight_ref[:, columns].astype(BF16)
                at += count

    return pl.pallas_call(
        kernel,
        out_shape=[jax.ShapeDtypeStruct((rows, local_cols), BF16)] * size,
        in_specs=[SCALARS, IN_VMEM],
        out_specs=[IN_VMEM] * size,
        compiler_params=params(),
        cost_estimate=cost(weight.size * 6),
        name="split_heads",
    )(scalars(own), weight)


def join_rows(pieces, own):
    rows, cols = pieces[0].shape
    size = len(pieces)
    if rows % 8:
        stacked = jnp.stack(pieces)
        return stacked[own ^ jnp.arange(size)].reshape(size * rows, cols)

    def kernel(own_ref, *refs):
        out_ref, wide_ref = refs[size], refs[size + 1]
        for other in range(size):
            at = pl.multiple_of((own_ref[0] ^ other) * rows, 8)
            wide_ref[pl.ds(at, rows), :] = refs[other][...].astype(F32)
        out_ref[...] = wide_ref[...].astype(BF16)

    return pl.pallas_call(
        kernel,
        out_shape=jax.ShapeDtypeStruct((size * rows, cols), BF16),
        in_specs=[SCALARS] + [IN_VMEM] * size,
        out_specs=IN_VMEM,
        scratch_shapes=[pltpu.VMEM((size * rows, cols), F32)],
        compiler_params=params(),
        cost_estimate=cost(size * rows * cols * 4),
        name="join_rows",
    )(scalars(own), *pieces)


def split_rows(parts, own):
    size = lax.axis_size("head")
    rows, cols = parts[0].shape[0] // size, parts[0].shape[1]
    if rows % 8:
        total = sum(part.astype(F32) for part in parts).reshape(size, rows, cols)
        total = total[own ^ jnp.arange(size)].astype(BF16)
        return [total[other] for other in range(size)]

    def kernel(own_ref, *refs):
        outs, wide_ref = refs[len(parts) : -1], refs[-1]
        total = refs[0][...].astype(F32)
        for part in refs[1 : len(parts)]:
            total = total + part[...].astype(F32)
        wide_ref[...] = total
        for other in range(size):
            at = pl.multiple_of((own_ref[0] ^ other) * rows, 8)
            outs[other][...] = wide_ref[pl.ds(at, rows), :].astype(BF16)

    return pl.pallas_call(
        kernel,
        out_shape=[jax.ShapeDtypeStruct((rows, cols), BF16)] * size,
        in_specs=[SCALARS] + [IN_VMEM] * len(parts),
        out_specs=[IN_VMEM] * size,
        scratch_shapes=[pltpu.VMEM((size * rows, cols), F32)],
        compiler_params=params(),
        cost_estimate=cost(size * rows * cols * 12),
        name="split_rows",
    )(scalars(own), *parts)


def row_block(rows, most):
    return max(one for one in range(1, rows + 1) if rows % one == 0 and one <= most and (one % 16 == 0 or one == rows))


def split_units(weight, z):
    size = lax.axis_size("ctx")
    count, rows, cols = weight.shape[0], weight.shape[1], weight.shape[2] // size
    block = row_block(rows, 96)

    def kernel(z_ref, in_ref, *refs):
        outs, kept = refs[:size], refs[size]
        for part in range(size):
            for one in range(count):
                kept[part, :, one * cols : (one + 1) * cols] = in_ref[
                    one, :, part * cols : (part + 1) * cols
                ]
        for k in range(size):
            outs[k][...] = kept[lax.rem(z_ref[0] + k, size)].astype(BF16)

    return pl.pallas_call(
        kernel,
        grid=(rows // block,),
        out_shape=[jax.ShapeDtypeStruct((rows, count * cols), BF16)] * size,
        in_specs=[SCALARS, pl.BlockSpec((count, block, size * cols), lambda i: (0, i, 0))],
        out_specs=[pl.BlockSpec((block, count * cols), lambda i: (i, 0))] * size,
        scratch_shapes=[pltpu.VMEM((size, block, count * cols), F32)],
        compiler_params=params(),
        cost_estimate=cost(weight.size * 6),
        name="split_units",
    )(scalars(z), weight)


def adam_units(came, z, weight, first_old, second_old, step_rate):
    size = len(came)
    count = weight.shape[0]
    rows, cols = came[0].shape[0], came[0].shape[1] // count
    block = row_block(rows, 96 // count)

    def kernel(z_ref, *refs):
        pieces, (weight_ref, first_ref, second_ref) = refs[:size], refs[size : size + 3]
        outs, kept = refs[size + 3 : size + 7], refs[size + 7]
        for k in range(size):
            kept[lax.rem(z_ref[0] + (size - k), size)] = pieces[k][...].astype(F32)
        for part in range(size):
            for one in range(count):
                outs[0][one, :, part * cols : (part + 1) * cols] = kept[
                    part, :, one * cols : (one + 1) * cols
                ]
        outs[1][...], outs[2][...], outs[3][...] = adam_step(
            weight_ref[...], first_ref[...], second_ref[...], outs[0][...], step_rate, WEIGHT_DECAY
        )

    whole = pl.BlockSpec((count, block, size * cols), lambda i: (0, i, 0))
    return pl.pallas_call(
        kernel,
        grid=(rows // block,),
        out_shape=[jax.ShapeDtypeStruct(weight.shape, F32)] * 4,
        in_specs=[SCALARS]
        + [pl.BlockSpec((block, count * cols), lambda i: (i, 0))] * size
        + [whole] * 3,
        out_specs=[whole] * 4,
        scratch_shapes=[pltpu.VMEM((size, block, count * cols), F32)],
        compiler_params=params(),
        cost_estimate=cost(weight.size * 30),
        name="adam_units",
    )(scalars(z), *came, weight, first_old, second_old)


def adam_qkv(query_pieces, kv_pieces, own, weight, first_old, second_old):
    size = len(query_pieces)
    query_cols, kv_cols = query_pieces[0].shape[1], kv_pieces[0].shape[1] // 2

    def kernel(own_ref, *refs):
        (weight_ref, first_ref, second_ref), outs = refs[2 * size : 2 * size + 3], refs[2 * size + 3 :]
        grad_ref = outs[0]
        if size > KVH:
            grad_ref[:, QH * HD :] = jnp.zeros_like(grad_ref[:, QH * HD :])
        for other in range(size):
            head = own_ref[0] ^ other
            columns = pl.ds(pl.multiple_of(head * query_cols, HD), query_cols)
            grad_ref[:, columns] = refs[other][...].astype(F32)
            for at in (0, 1):
                start = (QH + at * KVH) * HD + kv_start(head)
                columns = pl.ds(pl.multiple_of(start, HD), kv_cols)
                piece = refs[size + other][:, at * kv_cols : (at + 1) * kv_cols].astype(F32)
                if size > KVH:
                    piece = piece + grad_ref[:, columns]
                grad_ref[:, columns] = piece
        outs[1][...], outs[2][...], outs[3][...] = adam_step(
            weight_ref[...], first_ref[...], second_ref[...], grad_ref[...], RATE_MATRIX, WEIGHT_DECAY
        )

    return pl.pallas_call(
        kernel,
        out_shape=[jax.ShapeDtypeStruct(weight.shape, F32)] * 4,
        in_specs=[SCALARS] + [IN_VMEM] * (2 * size + 3),
        out_specs=[IN_VMEM] * 4,
        compiler_params=params(),
        cost_estimate=cost(weight.size * 30),
        name="adam_qkv",
    )(scalars(own), *query_pieces, *kv_pieces, weight, first_old, second_old)


def matmul(left, right):
    return jnp.dot(left, right, preferred_element_type=F32)


def matmul_nt(left, right):
    return lax.dot_general(left, right, (((1,), (1,)), ((), ())), preferred_element_type=F32)


def matmul_tn(left, right):
    return lax.dot_general(left, right, (((0,), (0,)), ((), ())), preferred_element_type=F32)


def rms_norm(values, gain_row):
    inv_scale = lax.rsqrt(jnp.mean(values * values, axis=-1, keepdims=True) + EPS_NORM)
    return values * inv_scale * (1.0 + gain_row)


def norm_back(values, gain_row, upstream):
    inv_scale = lax.rsqrt(jnp.mean(values * values, axis=-1, keepdims=True) + EPS_NORM)
    unit_rows = values * inv_scale
    scaled = upstream * (1.0 + gain_row)
    result = inv_scale * (scaled - unit_rows * jnp.mean(scaled * unit_rows, axis=-1, keepdims=True))
    return (result, jnp.sum(upstream * unit_rows, axis=0))


def rope_tables(position, half_dim):
    freq_table = ROPE_BASE ** (-(jnp.arange(half_dim, dtype=F32) * 2.0 / (2 * half_dim)))
    angle_table = position.astype(F32)[:, None] * freq_table[None, :]
    return (jnp.cos(angle_table), jnp.sin(angle_table))


def rope_turn(values, cosine, sine_table):
    half_dim = values.shape[-1] // 2
    lead_half = values[..., :half_dim]
    tail_half = values[..., half_dim:]
    return jnp.concatenate(
        [lead_half * cosine - tail_half * sine_table, tail_half * cosine + lead_half * sine_table],
        axis=-1,
    )


def rope_back(grad_rows, cosine, sine_table):
    return rope_turn(grad_rows, cosine, -sine_table)


def gated_unit(gate_in, up_in):
    return jax.nn.gelu(gate_in, approximate=True) * up_in


def adam_step(weight, first_old, second_old, gradient, step_rate, decay_rate):
    first_new = BETA_ONE * first_old + (1.0 - BETA_ONE) * gradient
    second_new = BETA_TWO * second_old + (1.0 - BETA_TWO) * gradient * gradient
    first_hat = first_new / (1.0 - BETA_ONE**STEP)
    second_hat = second_new / (1.0 - BETA_TWO**STEP)
    weight_new = weight - step_rate * (
        first_hat / (jnp.sqrt(second_hat) + EPS_ADAM) + decay_rate * weight
    )
    return (first_new, second_new, weight_new)


def block_weights(queries, keys, query_pos, key_pos):
    scores = jnp.einsum("kqd,krd->kqr", queries, keys, preferred_element_type=F32)
    unit = jnp.tanh(scores / SOFT_CAP)
    allowed = key_pos[None, None, :] <= query_pos[None, :, None]
    return (unit, jnp.where(allowed, jnp.exp(SOFT_CAP * unit), 0.0))


def block_forward(queries, keys, values, query_pos, key_pos):
    unused, weights = block_weights(queries, keys, query_pos, key_pos)
    return (
        jnp.sum(weights, axis=-1, keepdims=True),
        jnp.einsum("kqr,krd->kqd", weights.astype(BF16), values, preferred_element_type=F32),
    )


def block_backward(queries, keys, values, query_pos, key_pos, grad_summed, delta):
    unit, weights = block_weights(queries, keys, query_pos, key_pos)
    grad_weights = jnp.einsum("kqd,krd->kqr", grad_summed, values, preferred_element_type=F32)
    grad_scores = (weights * (grad_weights - delta) * (1.0 - unit * unit)).astype(BF16)
    return (
        jnp.einsum("kqr,krd->kqd", grad_scores, keys, preferred_element_type=F32),
        jnp.einsum("kqr,kqd->krd", grad_scores, queries, preferred_element_type=F32),
        jnp.einsum("kqr,kqd->krd", weights.astype(BF16), grad_summed, preferred_element_type=F32),
    )


def shards(
    tokens,
    positions,
    cotangent,
    qkv_weight,
    qkv_first,
    qkv_second,
    out_weight,
    out_first,
    out_second,
    gate_up,
    gate_up_first,
    gate_up_second,
    down_weight,
    down_first,
    down_second,
    gains,
    gains_first,
    gains_second,
):
    size_x, size_z, size_h = lax.axis_size("fsdp"), lax.axis_size("ctx"), lax.axis_size("head")
    z, own_h = lax.axis_index("ctx"), lax.axis_index("head")
    tok_rows, width = tokens.shape
    block_rows = tok_rows * size_h
    order = head_order()
    copies = max(1, size_h // KVH)
    kv_local = KVH * copies // size_h
    query_local = QH // size_h
    group = query_local // kv_local
    query_scale = 1.0 / math.sqrt(HD)
    query_cols, kv_cols = query_local * HD, kv_local * HD

    def positions_of(block):
        rows = lax.dynamic_slice_in_dim(positions, block * block_rows, block_rows)
        return jnp.concatenate(
            [lax.dynamic_slice_in_dim(rows, (own_h ^ one) * tok_rows, tok_rows) for one in order]
        )

    lines = Lines()
    unit_order = [k for k in far_first(size_z) if k]
    far_k = unit_order[0]

    pieces = head_exchange(lines, split_heads(qkv_weight, own_h))
    qkv_piece = join_rows(pieces, own_h)
    qkv_rows, local_cols = qkv_weight.shape[0], qkv_piece.shape[1]
    more_tokens = [tokens] + swap_top(lines, tokens) if size_h > 1 else [tokens]
    qkv_parts = spread_ctx(lines, qkv_piece, swap_fsdp)
    qkv_full = put_pieces(qkv_parts).reshape(width, local_cols)
    gain_rows = gather_gains(after(gains, qkv_piece))

    out_rows = out_weight.shape[0]
    out_groups = size_x * size_z // size_h
    out_low = after(out_weight, qkv_piece).astype(BF16)
    out_parts = spread_ctx(lines, out_low, swap_fsdp)
    out_own = put_pieces(out_parts).reshape(size_h, out_groups, out_rows, width)
    out_sets = head_exchange(lines, pick_pieces(out_own, [own_h ^ i for i in range(size_h)]))
    out_full = place(out_sets, [own_h ^ i for i in range(size_h)])
    out_full = jnp.transpose(out_full, (1, 0, 2, 3)).reshape(query_cols, width)

    ff_rows = gate_up.shape[1]
    ff_cols = gate_up.shape[2] // size_z
    down_turned = down_weight.T[None]
    gate_up_low = split_units(after(gate_up, qkv_piece), z)
    down_low = split_units(after(down_turned, qkv_piece), z)

    def unit_part(k, low):
        one = send_ctx(lines, low[k], k) if k else low[0]
        source = lambda z: lax.rem(z - k + size_z, size_z)
        return ([one] + swap_fsdp(lines, one), source, lambda z: z >= 0)

    gate_up_parts = [unit_part(k, gate_up_low) for k in (0, far_k)]

    block_tokens = head_gather(lines, jnp.concatenate(more_tokens), head_bits()[1:]).astype(F32)
    inputs = tokens.astype(F32)
    first_normed = rms_norm(block_tokens, gain_rows[0]).astype(BF16)
    projected = matmul(first_normed, qkv_full)
    block_pos = positions_of(z)
    cosine, sine_table = rope_tables(block_pos, HD // 2)

    def heads_of(values, count):
        return jnp.transpose(values.reshape(block_rows, count, HD), (1, 0, 2))

    queries = heads_of(projected[:, :query_cols], query_local)
    queries = (rope_turn(queries, cosine, sine_table) * query_scale).astype(BF16)
    queries = queries.reshape(kv_local, group * block_rows, HD)
    own_keys = heads_of(projected[:, query_cols : query_cols + kv_cols], kv_local)
    own_keys = rope_turn(own_keys, cosine, sine_table).astype(BF16)
    own_values = heads_of(projected[:, query_cols + kv_cols :], kv_local).astype(BF16)
    query_pos = jnp.tile(block_pos, group)
    own_kv = jnp.stack([own_keys, own_values])
    kv_slots = ctx_slots(lines, own_kv)
    gate_up_parts += [unit_part(k, gate_up_low) for k in unit_order[1:]]
    pos_slots = [positions_of(lax.rem(z + k, size_z)) for k in range(size_z)]
    exp_total = 0.0
    summed = 0.0
    for kv_slot, key_pos in zip(kv_slots, pos_slots):
        total_part, summed_part = block_forward(
            queries, kv_slot[0], kv_slot[1], query_pos, key_pos
        )
        exp_total = exp_total + total_part
        summed = summed + summed_part
    attended = summed / exp_total

    def rows_of(heads):
        heads = heads.reshape(-1, block_rows, HD)
        return jnp.transpose(heads, (1, 0, 2)).reshape(block_rows, -1)

    attended_low = rows_of(attended.astype(BF16))
    attn_out = head_reduce(lines, matmul(attended_low, out_full).astype(BF16))
    middle = inputs + rms_norm(attn_out, gain_rows[1])
    second_normed = rms_norm(middle, gain_rows[2]).astype(BF16)

    def all_slots(rows):
        if size_h < 2:
            return ctx_slots(lines, rows)
        slots = ctx_slots(lines, rows, swap_top, jnp.concatenate)
        return [head_gather(lines, one, head_bits()[1:]) for one in slots]

    def sum_slots(parts):
        return sum_ctx_slots(lines, lambda k: head_reduce(lines, parts[k]))

    normed_slots = all_slots(second_normed)
    down_parts = [unit_part(k, down_low) for k in [0] + unit_order]
    gate_up_full = put_pieces(gate_up_parts).reshape(width, 2 * ff_cols)
    down_full = put_pieces(down_parts).reshape(width, ff_cols)
    act_slots = [matmul(rows, gate_up_full) for rows in normed_slots]
    hidden_slots = [
        gated_unit(act[:, :ff_cols], act[:, ff_cols:]).astype(BF16) for act in act_slots
    ]
    ffn_out = sum_slots([matmul_nt(hidden, down_full).astype(BF16) for hidden in hidden_slots])
    mixed_out = (middle + rms_norm(ffn_out, gain_rows[3])).astype(BF16)

    upstream = cotangent.astype(F32)
    grad_ffn, gain_grad_ffn = norm_back(ffn_out, gain_rows[3], upstream)
    grad_slots = all_slots(grad_ffn.astype(BF16))

    def units_back(term, cols):
        sums = sum_over_fsdp(
            lines, term.reshape(size_x * size_z, ff_rows, cols), unit_order + [0]
        )
        return {k: one if k == 0 else one.astype(BF16) for k, one in sums.items()}

    down_term = matmul_tn(jnp.concatenate(grad_slots), jnp.concatenate(hidden_slots)).astype(BF16)
    down_back = units_back(down_term, ff_cols)
    for k in unit_order:
        down_back[k] = send_ctx(lines, down_back[k], k)
    grad_act_slots = []
    for rows, act in zip(grad_slots, act_slots):
        grad_hidden = matmul(rows, down_full)
        unit_out, unit_back = jax.vjp(gated_unit, act[:, :ff_cols], act[:, ff_cols:])
        grad_act_slots.append(jnp.concatenate(unit_back(grad_hidden), axis=1).astype(BF16))
    grad_second_parts = [matmul_nt(rows, gate_up_full).astype(BF16) for rows in grad_act_slots]
    gate_up_term = matmul_tn(jnp.concatenate(normed_slots), jnp.concatenate(grad_act_slots))
    gate_up_term = gate_up_term.astype(BF16)
    grad_second_parts[0] = after(grad_second_parts[0], gate_up_term)
    grad_second = sum_slots(grad_second_parts)
    gate_up_back = units_back(gate_up_term, 2 * ff_cols)
    gate_up_back[far_k] = send_ctx(lines, gate_up_back[far_k], far_k)

    grad_middle_part, gain_grad_middle = norm_back(middle, gain_rows[2], grad_second)
    grad_middle = upstream + grad_middle_part
    grad_attn, gain_grad_attn = norm_back(attn_out, gain_rows[1], grad_middle)
    block_grad_attn = head_gather(lines, grad_attn.astype(BF16))
    out_term = matmul_tn(attended_low, block_grad_attn).astype(BF16)
    out_term = jnp.transpose(
        out_term.reshape(out_groups, size_h, out_rows, width), (1, 0, 2, 3)
    )
    grad_attended = matmul_nt(block_grad_attn, out_full).astype(BF16)
    grad_attended = heads_of(grad_attended, query_local).astype(F32)
    grad_attended = grad_attended.reshape(kv_local, group * block_rows, HD)
    row_delta = jnp.sum(grad_attended * attended, axis=-1, keepdims=True)
    delta = row_delta / exp_total
    grad_summed = (grad_attended / exp_total).astype(BF16)
    grad_query = 0.0
    kv_parts = {}
    for k in ctx_order():
        query_part, key_part, value_part = block_backward(
            queries, kv_slots[k][0], kv_slots[k][1], query_pos, pos_slots[k], grad_summed, delta
        )
        grad_query = grad_query + query_part
        kv_parts[k] = jnp.stack([key_part, value_part])
    grad_kv = sum_ctx_slots(lines, lambda k: kv_parts[k])
    for k in unit_order[1:]:
        gate_up_back[k] = send_ctx(lines, gate_up_back[k], k)
    out_sets = head_exchange(lines, pick_pieces(out_term, [own_h ^ i for i in range(size_h)]))
    out_term = place(out_sets, [own_h ^ i for i in range(size_h)])

    grad_query = grad_query.astype(BF16).astype(F32).reshape(query_local, block_rows, HD)
    query_proj = rows_of(rope_back(grad_query, cosine, sine_table) * query_scale).astype(BF16)
    query_term = matmul_tn(first_normed, query_proj).astype(BF16)
    query_sums = sum_over_fsdp(
        lines, query_term.reshape(size_x * size_z, size_h * qkv_rows, query_cols), ctx_order()
    )
    query_sum = sum_ctx_slots(lines, lambda k: query_sums[k])
    grad_kv = grad_kv.astype(BF16).astype(F32)
    kv_proj = jnp.concatenate(
        [rows_of(rope_back(grad_kv[0], cosine, sine_table)), rows_of(grad_kv[1])], axis=1
    ).astype(BF16)
    kv_term = matmul_tn(first_normed, kv_proj).astype(BF16)
    kv_sums = sum_over_fsdp(
        lines, kv_term.reshape(size_x * size_z, size_h * qkv_rows, 2 * kv_cols), ctx_order()
    )
    kv_sum = sum_ctx_slots(lines, lambda k: kv_sums[k])
    grad_proj = jnp.concatenate([query_proj, kv_proj], axis=1)
    grad_first = head_reduce(lines, matmul_nt(grad_proj, qkv_full).astype(BF16))
    grad_input_part, gain_grad_input = norm_back(inputs, gain_rows[0], grad_first)
    tokens_grad = (grad_middle + grad_input_part).astype(BF16)

    query_pieces = head_exchange(lines, split_rows([query_sum], own_h))
    kv_pieces = head_exchange(lines, split_rows([kv_sum], own_h))
    out_sums = sum_over_fsdp(
        lines, out_term.reshape(size_x * size_z, out_rows, width), ctx_order()
    )
    out_grad = sum_ctx_slots(lines, lambda k: out_sums[k])
    gains_grad = scatter_gains(
        jnp.stack([gain_grad_input, gain_grad_attn, gain_grad_middle, gain_grad_ffn])
    )

    qkv_grad, qkv_first_new, qkv_second_new, qkv_new = adam_qkv(
        query_pieces, kv_pieces, own_h, qkv_weight, qkv_first, qkv_second
    )
    out_first_new, out_second_new, out_new = adam_step(
        out_weight, out_first, out_second, out_grad, RATE_MATRIX, WEIGHT_DECAY
    )
    gate_up_grad, gate_up_first_new, gate_up_second_new, gate_up_new = adam_units(
        [gate_up_back[k] for k in range(size_z)], z, gate_up, gate_up_first, gate_up_second, RATE_MATRIX
    )
    down_outs = adam_units(
        [down_back[k] for k in range(size_z)],
        z,
        down_turned,
        down_first.T[None],
        down_second.T[None],
        RATE_DOWN,
    )
    down_grad, down_first_new, down_second_new, down_new = [one[0].T for one in down_outs]
    gains_first_new, gains_second_new, gains_new = adam_step(
        gains, gains_first, gains_second, gains_grad, RATE_GAIN, 0.0
    )
    return (
        mixed_out,
        tokens_grad,
        qkv_grad,
        qkv_first_new,
        qkv_second_new,
        qkv_new,
        out_grad,
        out_first_new,
        out_second_new,
        out_new,
        gate_up_grad,
        gate_up_first_new,
        gate_up_second_new,
        gate_up_new,
        down_grad,
        down_first_new,
        down_second_new,
        down_new,
        gains_grad,
        gains_first_new,
        gains_second_new,
        gains_new,
    )


TOKEN_SPEC = P(("fsdp", "ctx", "head"), None)
GATE_UP_SPEC = P(None, ("fsdp", "ctx"), "head")
DOWN_SPEC = P("head", ("fsdp", "ctx"))


def solution(mesh):
    in_specs = (
        (TOKEN_SPEC, P("fsdp"))
        + (TOKEN_SPEC,) * 7
        + (GATE_UP_SPEC,) * 3
        + (DOWN_SPEC,) * 3
        + (TOKEN_SPEC,) * 3
    )
    out_specs = (
        (TOKEN_SPEC,) * 10 + (GATE_UP_SPEC,) * 4 + (DOWN_SPEC,) * 4 + (TOKEN_SPEC,) * 4
    )
    return jax.shard_map(shards, mesh=mesh, in_specs=in_specs, out_specs=out_specs, check_vma=False)
```

time: 1500 us -> 1030 us (0.69)
  local copies, waits for them, and re-layouts: 483 us -> 71.9 us
  waiting for transfers between devices: 509 us -> 424 us
  Pallas kernels: 0 us -> 74 us
  matrix products: 153 us -> 126 us
  other arithmetic: 109 us -> 86.7 us
    dynamic_update_slice x56 -> x0, local copies, waits for them, and re-layouts: 301 us -> none  [the longest x20 102 us: head_exchange(): result = lax.dynamic_update_slice_in_dim(result, came, own ^ other, 0)]
    ppermute x142 -> x151, waiting for transfers between devices: 509 us -> 421 us  [the longest x126 418 us: send(): lax.ppermute(one, axes, pairs)]
    pallas_call x0 -> x22, Pallas kernels: none -> 74 us  [the longest x6 27.8 us: place(): pl.pallas_call(kernel, out_shape=jax.ShapeDtypeStruct(shape, pieces[0].dt...]
    reshape x12 -> x1, local copies, waits for them, and re-layouts: 52.1 us -> 0.15 us  [shards(): out_term.reshape(out_groups, size_h, out_rows, width)]
    broadcast_in_dim x17 -> x1, local copies, waits for them, and re-layouts: 29.5 us -> 0.63 us  [gather_gains(): jnp.broadcast_to(gains.astype(BF16).T[None], (device_count(),) + gains.sh...]
    sub x5 -> x2, other arithmetic: 29.7 us -> 3.97 us  [adam_step(): weight - step_rate * (first_hat / (jnp.sqrt(second_hat) + EPS_ADAM) + dec...]
    dot_general x10, matrix products: 51.7 us -> 32.2 us  [matmul_nt(): lax.dot_general(left, right, (((1,), (1,)), ((), ())), preferred_element_...]
    dynamic_slice x11 -> x0, local copies, waits for them, and re-layouts: 15.9 us -> none  [the longest x10 11.8 us: head_exchange(): lax.dynamic_index_in_dim(pieces, own ^ other, 0, keepdims=True)]
  transfers between devices with their start and end apart: 142 -> 153, of which waited for: 54 -> 55; matrix products, arithmetic and copies ran while one was open for 47% -> 23% of each run, Pallas kernels for 0% -> 7%
where the time goes in v2:
time: 1030 us; the launch traced here: 1020 us
  waiting for transfers between devices  424 us (41%)
  starting transfers between devices  236 us (23%)
  matrix products  126 us (12%)
  other arithmetic  86.7 us (8%)
  Pallas kernels  74 us (7%)
  local copies, waits for them, and re-layouts  71.9 us (7%)
    ppermute x126, waiting for transfers between devices, send(): lax.ppermute(one, axes, pairs)  418 us
    ppermute x126, starting transfers between devices, send(): lax.ppermute(one, axes, pairs)  219 us
    unnamed x438, local copies, waits for them, and re-layouts  47.9 us
    dot_general x10, matrix products, matmul(): return jnp.dot(left, right, preferred_element_type=F32)  40.3 us
    dot_general x5, matrix products, matmul_tn(): lax.dot_general(left, right, (((0,), (0,)), ((), ())), preferred_element_...  33.6 us
    dot_general x10, matrix products, matmul_nt(): lax.dot_general(left, right, (((1,), (1,)), ((), ())), preferred_element_...  32.2 us
    pallas_call x6, Pallas kernels, place(): pl.pallas_call(kernel, out_shape=jax.ShapeDtypeStruct(shape, pieces[0].dt...  27.8 us
    pallas_call x2, Pallas kernels, adam_units(): pl.pallas_call(kernel, grid=(rows // block,), out_shape=[jax.ShapeDtypeSt...  22.5 us
  transfers between devices with their start and end apart: 153, of which 55 were waited for; matrix products, arithmetic and copies ran while one was open for 23% of the time, Pallas kernels for 7%

profile of v2, /device:TPU:0, one launch (start us, length us, event | category | flops | bytes accessed | tf_op | source)
XLA Modules:
  0.0 1023.1 jit_solution(16241653780213511438)
XLA Ops:
  20.5 8.8 collective-permute-done.8.refs_4_
  41.2 18.9 %collective-permute-done.10.refs_6_ = bf16[288,1024]{1,0:T(8,128)(2,1)} collective-permute-done((bf16[288,1024]{1,0:T(8,128)(2,1)S(1)}, bf16[288,1024]{1,0:T(8,128)(2,1)}, u32[]{:S(2)}, u32[]{:S(2)}) %collective-permute-start.10) | collective-permute-done | bytes 589856 | tf_op jit(solution)/shard_map/ppermute | solution.py:46
  64.5 7.0 all-to-all-start
  71.7 5.1 split_units.2
  98.0 10.4 %collective-permute-done.16.refs_6_ = bf16[64,2304]{1,0:T(8,128)(2,1)S(1)} collective-permute-done((bf16[64,2304]{1,0:T(8,128)(2,1)S(1)}, bf16[64,2304]{1,0:T(8,128)(2,1)S(1)}, u32[]{:S(2)}, u32[]{:S(2)}) %collective-permute-start.16) | collective-permute-done | bytes 294944 | tf_op jit(solution)/shard_map/ppermute | solution.py:46
  112.3 5.0 place.6
  117.4 5.5 fusion.207
  126.6 17.0 %collective-permute-done.18.refs_8_ = bf16[64,2304]{1,0:T(8,128)(2,1)S(1)} collective-permute-done((bf16[64,2304]{1,0:T(8,128)(2,1)S(1)}, bf16[64,2304]{1,0:T(8,128)(2,1)S(1)}, u32[]{:S(2)}, u32[]{:S(2)}) %collective-permute-start.18) | collective-permute-done | bytes 294944 | tf_op jit(solution)/shard_map/ppermute | solution.py:46
  154.9 4.9 collective-permute-done.25.refs_5_
  166.1 5.2 collective-permute-done.27.refs_9_
  176.3 10.6 %collective-permute-done.22 = bf16[2,1,512,256]{3,2,1,0:T(8,128)(2,1)S(1)} collective-permute-done((bf16[2,1,512,256]{3,2,1,0:T(8,128)(2,1)}, bf16[2,1,512,256]{3,2,1,0:T(8,128)(2,1)S(1)}, u32[]{:S(2)}, u32[]{:S(2)}) %collective-permute-start.22) | collective-permute-done | bytes 524320 | tf_op jit(solution)/shard_map/ppermute | solution.py:46
  189.9 9.6 collective-permute-done.30.refs_3_
  199.6 11.7 %place.8 = bf16[4,2,64,2304]{3,2,1,0:T(8,128)(2,1)S(1)} custom-call(s32[4]{0:T(128)S(1)} %pad_add_fusion.5.places_ref, bf16[2,64,2304]{2,1,0:T(8,128)(2,1)S(1)} %get-tuple-element.267.refs_0_, bf16[2,64,2304]{2,1,0:T(8,128)(2,1)S(1)} %collective-permute-done.28.refs_1_, bf16[2,64,2304]{2,1,0:T(8,128)(2,1)S(1)} %collective-permute-done.29.refs_2_, ...), custom_call_target="tpu_custom_call" | custom-call | bytes 4718592 | tf_op jit(solution)/shard_map/place/pallas_call | solution.py:292
  232.0 14.1 %collective-permute-done.32 = bf16[128,2304]{1,0:T(8,128)(2,1)} collective-permute-done((bf16[128,2304]{1,0:T(8,128)(2,1)}, bf16[128,2304]{1,0:T(8,128)(2,1)}, u32[]{:S(2)}, u32[]{:S(2)}) %collective-permute-start.32) | collective-permute-done | bytes 589856 | tf_op jit(solution)/shard_map/ppermute | solution.py:46
  259.1 6.7 collective-permute-done.33
  271.1 11.6 %collective-permute-done.36.refs_3_ = bf16[288,1152]{1,0:T(8,128)(2,1)S(1)} collective-permute-done((bf16[288,1152]{1,0:T(8,128)(2,1)S(1)}, bf16[288,1152]{1,0:T(8,128)(2,1)S(1)}, u32[]{:S(2)}, u32[]{:S(2)}) %collective-permute-start.36) | collective-permute-done | bytes 663584 | tf_op jit(solution)/shard_map/ppermute | solution.py:46
  288.0 13.7 %collective-permute-done.38.refs_5_ = bf16[288,1152]{1,0:T(8,128)(2,1)} collective-permute-done((bf16[288,1152]{1,0:T(8,128)(2,1)}, bf16[288,1152]{1,0:T(8,128)(2,1)}, u32[]{:S(2)}, u32[]{:S(2)}) %collective-permute-start.38) | collective-permute-done | bytes 663584 | tf_op jit(solution)/shard_map/ppermute | solution.py:46
  302.2 13.7 %collective-permute-done.40.refs_7_ = bf16[288,1152]{1,0:T(8,128)(2,1)} collective-permute-done((bf16[288,1152]{1,0:T(8,128)(2,1)}, bf16[288,1152]{1,0:T(8,128)(2,1)}, u32[]{:S(2)}, u32[]{:S(2)}) %collective-permute-start.40) | collective-permute-done | bytes 663584 | tf_op jit(solution)/shard_map/ppermute | solution.py:46
  315.9 5.6 place.9
  326.2 8.1 collective-permute-done.45.refs_2_
  336.2 6.3 fusion.17
  352.5 8.9 collective-permute-done.51.refs_6_
  413.6 13.3 %collective-permute-done.63 = bf16[128,2304]{1,0:T(8,128)(2,1)S(1)} collective-permute-done((bf16[128,2304]{1,0:T(8,128)(2,1)S(1)}, bf16[128,2304]{1,0:T(8,128)(2,1)S(1)}, u32[]{:S(2)}, u32[]{:S(2)}) %collective-permute-start.63) | collective-permute-done | bytes 589856 | tf_op jit(solution)/shard_map/ppermute | solution.py:46
  427.8 11.8 %collective-permute-done.58 = bf16[128,2304]{1,0:T(8,128)(2,1)S(1)} collective-permute-done((bf16[128,2304]{1,0:T(8,128)(2,1)S(1)}, bf16[128,2304]{1,0:T(8,128)(2,1)S(1)}, u32[]{:S(2)}, u32[]{:S(2)}) %collective-permute-start.58) | collective-permute-done | bytes 589856 | tf_op jit(solution)/shard_map/ppermute | solution.py:46
  461.5 7.5 collective-permute-done.64
  468.9 21.0 %collective-permute-done.70 = bf16[128,2304]{1,0:T(8,128)(2,1)} collective-permute-done((bf16[128,2304]{1,0:T(8,128)(2,1)}, bf16[128,2304]{1,0:T(8,128)(2,1)}, u32[]{:S(2)}, u32[]{:S(2)}) %collective-permute-start.70) | collective-permute-done | bytes 589856 | tf_op jit(solution)/shard_map/ppermute | solution.py:46
  500.0 7.8 collective-permute-done.73
  518.0 21.3 %collective-permute-done.75 = bf16[128,2304]{1,0:T(8,128)(2,1)} collective-permute-done((bf16[128,2304]{1,0:T(8,128)(2,1)}, bf16[128,2304]{1,0:T(8,128)(2,1)}, u32[]{:S(2)}, u32[]{:S(2)}) %collective-permute-start.75) | collective-permute-done | bytes 589856 | tf_op jit(solution)/shard_map/ppermute | solution.py:46
  544.8 11.1 %collective-permute-done.77 = bf16[128,2304]{1,0:T(8,128)(2,1)S(1)} collective-permute-done((bf16[128,2304]{1,0:T(8,128)(2,1)}, bf16[128,2304]{1,0:T(8,128)(2,1)S(1)}, u32[]{:S(2)}, u32[]{:S(2)}) %collective-permute-start.77) | collective-permute-done | bytes 589856 | tf_op jit(solution)/shard_map/ppermute | solution.py:46
  608.8 14.6 %convolution_convert_fusion = bf16[2304,1152]{1,0:T(8,128)(2,1)} fusion(bf16[2048,2304]{1,0:T(8,128)(2,1)S(1)} %bitcast.289, bf16[512,1152]{1,0:T(8,128)(2,1)S(1)} %pad_maximum_fusion.10, bf16[512,1152]{1,0:T(8,128)(2,1)S(1)} %pad_maximum_fusion.9, bf16[512,1152]{1,0:T(8,128)(2,1)S(1)} %pad_maximum_fusion.7, bf16[512,1152]{1,0:T(8,128)(2,1)S(1)} %pad_maximum_fusion.6), kind=kOutput, calls=%fused_computation | convolution fusion | flops 10893164544 | bytes 19464192 | tf_op jit(solution)/shard_map/dot_general | solution.py:530
  625.9 10.3 %convolution_convert_fusion.1 = bf16[2304,576]{0,1:T(8,128)(2,1)} fusion(bf16[2048,2304]{1,0:T(8,128)(2,1)} %constant_dynamic-update-slice_fusion.14, bf16[512,576]{1,0:T(8,128)(2,1)S(1)} %copy-done.143, bf16[512,576]{1,0:T(8,128)(2,1)S(1)} %copy-done.139, bf16[512,576]{1,0:T(8,128)(2,1)S(1)} %copy-done.141, bf16[512,576]{1,0:T(8,128)(2,1)S(1)} %copy-done.137), kind=kOutput, calls=%fused_computation.13 | convolution fusion | flops 5446582272 | bytes 14450688 | tf_op jit(solution)/shard_map/dot_general | solution.py:530
  648.4 13.0 %collective-permute-done.90 = bf16[288,576]{1,0:T(8,128)(2,1)S(1)} collective-permute-done((bf16[288,576]{1,0:T(8,128)(2,1)S(1)}, bf16[288,576]{1,0:T(8,128)(2,1)S(1)}, u32[]{:S(2)}, u32[]{:S(2)}) %collective-permute-start.90) | collective-permute-done | bytes 331808 | tf_op jit(solution)/shard_map/ppermute | solution.py:46
  673.1 16.7 %collective-permute-done.92.refs_2_ = bf16[288,576]{1,0:T(8,128)(2,1)S(1)} collective-permute-done((bf16[288,576]{1,0:T(8,128)(2,1)S(1)}, bf16[288,576]{1,0:T(8,128)(2,1)S(1)}, u32[]{:S(2)}, u32[]{:S(2)}) %collective-permute-start.92) | collective-permute-done | bytes 331808 | tf_op jit(solution)/shard_map/ppermute | solution.py:46
  694.8 5.5 collective-permute-done.93.refs_3_
  703.4 7.9 collective-permute-done.100
  713.7 10.3 %collective-permute-done.94 = bf16[128,2304]{1,0:T(8,128)(2,1)S(1)} collective-permute-done((bf16[128,2304]{1,0:T(8,128)(2,1)S(1)}, bf16[128,2304]{1,0:T(8,128)(2,1)S(1)}, u32[]{:S(2)}, u32[]{:S(2)}) %collective-permute-start.94) | collective-permute-done | bytes 589856 | tf_op jit(solution)/shard_map/ppermute | solution.py:46
  724.0 20.7 %collective-permute-done.101 = bf16[128,2304]{1,0:T(8,128)(2,1)S(1)} collective-permute-done((bf16[128,2304]{1,0:T(8,128)(2,1)S(1)}, bf16[128,2304]{1,0:T(8,128)(2,1)S(1)}, u32[]{:S(2)}, u32[]{:S(2)}) %collective-permute-start.101) | collective-permute-done | bytes 589856 | tf_op jit(solution)/shard_map/ppermute | solution.py:46
  766.2 7.8 adam_units.3
  777.8 13.7 %collective-permute-done.104 = bf16[288,1152]{1,0:T(8,128)(2,1)} collective-permute-done((bf16[288,1152]{1,0:T(8,128)(2,1)}, bf16[288,1152]{1,0:T(8,128)(2,1)}, u32[]{:S(2)}, u32[]{:S(2)}) %collective-permute-start.104) | collective-permute-done | bytes 663584 | tf_op jit(solution)/shard_map/ppermute | solution.py:46
  831.1 5.1 collective-permute-start.109
  844.5 25.3 %collective-permute-start.124 = (bf16[288,1152]{1,0:T(8,128)(2,1)S(1)}, bf16[288,1152]{1,0:T(8,128)(2,1)S(1)}, u32[]{:S(2)}, u32[]{:S(2)}) collective-permute-start(bf16[288,1152]{1,0:T(8,128)(2,1)S(1)} %copy-done.135), channel_id=1, source_target_pairs={{0,4},{4,8},{8,12},{12,0},{1,5},{5,9},{9,13},{13,1},{2,6},{6,10},{... | collective-permute-start | bytes 1990664 | tf_op jit(solution)/shard_map/ppermute | solution.py:46
  869.8 5.2 collective-permute-done.109
  914.7 5.3 convolution_convert_fusion.9
  921.5 7.8 collective-permute-done.120.refs_3_
  931.0 14.7 %adam_units.2 = (f32[2,288,2304]{2,1,0:T(8,128)}, f32[2,288,2304]{2,1,0:T(8,128)}, f32[2,288,2304]{2,1,0:T(8,128)}, f32[2,288,2304]{2,1,0:T(8,128)}) custom-call(s32[1]{0:T(128)} %bitcast.23.z_ref, f32[288,1152]{1,0:T(8,128)S(1)} %convert_add_fusion.12.refs_0_, bf16[288,1152]{1,0:T(8,128)(2,1)S(1)} %collective-permute-done.124.refs_1_, ...), custom_call_target="tpu_custom_call" | custom-call | bytes 39813120 | tf_op jit(solution)/shard_map/adam_units/pallas_call | solution.py:471
  960.9 6.2 collective-permute-start.129
  980.6 13.6 %collective-permute-done.138 = bf16[288,512]{1,0:T(8,128)(2,1)S(1)} collective-permute-done((bf16[288,512]{1,0:T(8,128)(2,1)S(1)}, bf16[288,512]{1,0:T(8,128)(2,1)S(1)}, u32[]{:S(2)}, u32[]{:S(2)}) %collective-permute-start.138) | collective-permute-done | bytes 294944 | tf_op jit(solution)/shard_map/ppermute | solution.py:46
  1000.6 5.3 all-to-all-start.1
  (925 shorter events, 507.6 us)
Async XLA Ops:
  30.4 29.7 %collective-permute-start.10 = (bf16[288,1024]{1,0:T(8,128)(2,1)S(1)}, bf16[288,1024]{1,0:T(8,128)(2,1)}, u32[]{:S(2)}, u32[]{:S(2)}) collective-permute-start(bf16[288,1024]{1,0:T(8,128)(2,1)S(1)} %join_rows.1.refs_0_), channel_id=1, source_target_pairs={{0,8},{4,12},{8,0},{12,4},{1,9},{5,13},{9,1},{13,5},{2,10},{6,14},... | collective-permute-start | bytes 1769480 | tf_op jit(solution)/shard_map/ppermute | solution.py:46
  34.1 26.1 %collective-permute-start.7 = (bf16[288,1024]{1,0:T(8,128)(2,1)S(1)}, bf16[288,1024]{1,0:T(8,128)(2,1)S(1)}, u32[]{:S(2)}, u32[]{:S(2)}) collective-permute-start(bf16[288,1024]{1,0:T(8,128)(2,1)S(1)} %collective-permute-done.6.refs_2_), channel_id=1, source_target_pairs={{4,20},{8,24},{12,28},{20,4},{24,8},{28,12},{5,21},{9,25},{13,29},... | collective-permute-start | bytes 1769480 | tf_op jit(solution)/shard_map/ppermute | solution.py:46
  36.9 58.9 %collective-permute-start.2 = (bf16[256,2304]{1,0:T(8,128)(2,1)}, bf16[256,2304]{1,0:T(8,128)(2,1)}, u32[]{:S(2)}, u32[]{:S(2)}) collective-permute-start(bf16[256,2304]{1,0:T(8,128)(2,1)} %pad_maximum_fusion.2), channel_id=1, source_target_pairs={{0,1},{1,0},{2,3},{3,2},{4,5},{5,4},{6,7},{7,6},{8,9},{9,8},{10,11... | collective-permute-start | bytes 3538952 | tf_op jit(solution)/shard_map/ppermute | solution.py:68
  37.8 43.5 %collective-permute-start.9 = (bf16[288,1024]{1,0:T(8,128)(2,1)S(1)}, bf16[288,1024]{1,0:T(8,128)(2,1)}, u32[]{:S(2)}, u32[]{:S(2)}) collective-permute-start(bf16[288,1024]{1,0:T(8,128)(2,1)S(1)} %collective-permute-done.8.refs_4_), channel_id=1, source_target_pairs={{0,16},{4,20},{8,24},{16,0},{20,4},{24,8},{1,17},{5,21},{9,25},{17... | collective-permute-start | bytes 1769480 | tf_op jit(solution)/shard_map/ppermute | solution.py:46
  62.3 29.7 %collective-permute-start.11 = (bf16[288,1024]{1,0:T(8,128)(2,1)}, bf16[288,1024]{1,0:T(8,128)(2,1)}, u32[]{:S(2)}, u32[]{:S(2)}) collective-permute-start(bf16[288,1024]{1,0:T(8,128)(2,1)} %collective-permute-done.10.refs_6_), channel_id=1, source_target_pairs={{0,16},{4,20},{8,24},{12,28},{16,0},{20,4},{24,8},{28,12},{1,17},{... | collective-permute-start | bytes 1769480 | tf_op jit(solution)/shard_map/ppermute | solution.py:46
  82.6 25.8 %collective-permute-start.13 = (bf16[288,1024]{1,0:T(8,128)(2,1)}, bf16[288,1024]{1,0:T(8,128)(2,1)}, u32[]{:S(2)}, u32[]{:S(2)}) collective-permute-start(bf16[288,1024]{1,0:T(8,128)(2,1)} %collective-permute-done.12.refs_8_), channel_id=1, source_target_pairs={{0,16},{12,28},{16,0},{28,12},{1,17},{13,29},{17,1},{29,13},{2,18}... | collective-permute-start | bytes 1769480 | tf_op jit(solution)/shard_map/ppermute | solution.py:46
  92.0 55.3 %collective-permute-start.24 = (bf16[64,2304]{1,0:T(8,128)(2,1)S(1)}, bf16[64,2304]{1,0:T(8,128)(2,1)S(1)}, u32[]{:S(2)}, u32[]{:S(2)}) collective-permute-start(bf16[64,2304]{1,0:T(8,128)(2,1)S(1)} %convert_element_type.622.refs_0_), channel_id=1, source_target_pairs={{0,16},{4,20},{8,24},{12,28},{16,0},{20,4},{24,8},{28,12},{1,17},{... | collective-permute-start | bytes 884744 | tf_op jit(solution)/shard_map/ppermute | solution.py:46
  108.4 53.8 %collective-permute-start.21 = (bf16[288,1152]{1,0:T(8,128)(2,1)}, bf16[288,1152]{1,0:T(8,128)(2,1)S(1)}, u32[]{:S(2)}, u32[]{:S(2)}) collective-permute-start(bf16[288,1152]{1,0:T(8,128)(2,1)} %get-tuple-element.260), channel_id=1, source_target_pairs={{0,8},{4,12},{8,0},{12,4},{1,9},{5,13},{9,1},{13,5},{2,10},{6,14},... | collective-permute-start | bytes 1990664 | tf_op jit(solution)/shard_map/ppermute | solution.py:46
  252.9 29.8 %collective-permute-start.36 = (bf16[288,1152]{1,0:T(8,128)(2,1)S(1)}, bf16[288,1152]{1,0:T(8,128)(2,1)S(1)}, u32[]{:S(2)}, u32[]{:S(2)}) collective-permute-start(bf16[288,1152]{1,0:T(8,128)(2,1)S(1)} %copy-done.13), channel_id=1, source_target_pairs={{0,16},{4,20},{8,24},{12,28},{16,0},{20,4},{24,8},{28,12},{1,17},{... | collective-permute-start | bytes 1990664 | tf_op jit(solution)/shard_map/ppermute | solution.py:46
  254.4 29.7 %collective-permute-start.39 = (bf16[288,1152]{1,0:T(8,128)(2,1)S(1)}, bf16[288,1152]{1,0:T(8,128)(2,1)}, u32[]{:S(2)}, u32[]{:S(2)}) collective-permute-start(bf16[288,1152]{1,0:T(8,128)(2,1)S(1)} %copy-done.60), channel_id=1, source_target_pairs={{0,12},{4,0},{8,4},{12,8},{1,13},{5,1},{9,5},{13,9},{2,14},{6,2},{... | collective-permute-start | bytes 1990664 | tf_op jit(solution)/shard_map/ppermute | solution.py:46
  254.7 30.8 %collective-permute-start.42 = (bf16[128,2304]{1,0:T(8,128)(2,1)}, bf16[128,2304]{1,0:T(8,128)(2,1)}, u32[]{:S(2)}, u32[]{:S(2)}) collective-permute-start(bf16[128,2304]{1,0:T(8,128)(2,1)} %get-tuple-element.274), channel_id=1, source_target_pairs={{0,4},{4,8},{8,12},{1,5},{5,9},{9,13},{2,6},{6,10},{10,14},{3,7},{... | collective-permute-start | bytes 1769480 | tf_op jit(solution)/shard_map/ppermute | solution.py:46
  271.1 64.6 %collective-permute-start.34 = (bf16[256,2304]{1,0:T(8,128)(2,1)}, bf16[256,2304]{1,0:T(8,128)(2,1)}, u32[]{:S(2)}, u32[]{:S(2)}) collective-permute-start(bf16[256,2304]{1,0:T(8,128)(2,1)} %pad_maximum_fusion.3), channel_id=1, source_target_pairs={{0,1},{1,0},{2,3},{3,2},{4,5},{5,4},{6,7},{7,6},{8,9},{9,8},{10,11... | collective-permute-start | bytes 3538952 | tf_op jit(solution)/shard_map/ppermute | solution.py:68
  284.1 31.8 %collective-permute-start.40 = (bf16[288,1152]{1,0:T(8,128)(2,1)}, bf16[288,1152]{1,0:T(8,128)(2,1)}, u32[]{:S(2)}, u32[]{:S(2)}) collective-permute-start(bf16[288,1152]{1,0:T(8,128)(2,1)} %collective-permute-done.39.refs_6_), channel_id=1, source_target_pairs={{0,16},{4,20},{8,24},{12,28},{16,0},{20,4},{24,8},{28,12},{1,17},{... | collective-permute-start | bytes 1990664 | tf_op jit(solution)/shard_map/ppermute | solution.py:46
  285.6 38.4 %collective-permute-start.44 = (bf16[128,2304]{1,0:T(8,128)(2,1)}, bf16[128,2304]{1,0:T(8,128)(2,1)}, u32[]{:S(2)}, u32[]{:S(2)}) collective-permute-start(bf16[128,2304]{1,0:T(8,128)(2,1)} %get-tuple-element.274), channel_id=1, source_target_pairs={{0,8},{4,12},{8,0},{12,4},{1,9},{5,13},{9,1},{13,5},{2,10},{6,14},... | collective-permute-start | bytes 1769480 | tf_op jit(solution)/shard_map/ppermute | solution.py:46
  285.6 39.4 %collective-permute-start.47 = (bf16[128,2304]{1,0:T(8,128)(2,1)}, bf16[128,2304]{1,0:T(8,128)(2,1)}, u32[]{:S(2)}, u32[]{:S(2)}) collective-permute-start(bf16[128,2304]{1,0:T(8,128)(2,1)} %collective-permute-done.42), channel_id=1, source_target_pairs={{4,6},{5,7},{6,4},{7,5},{8,10},{9,11},{10,8},{11,9},{12,14},{13,15... | collective-permute-start | bytes 1769480 | tf_op jit(solution)/shard_map/ppermute | solution.py:46
  301.7 61.2 %collective-permute-start.41 = (bf16[288,576]{1,0:T(8,128)(2,1)S(1)}, bf16[288,576]{1,0:T(8,128)(2,1)S(1)}, u32[]{:S(2)}, u32[]{:S(2)}) collective-permute-start(bf16[288,576]{1,0:T(8,128)(2,1)S(1)} %get-tuple-element.286.refs_0_), channel_id=1, source_target_pairs={{0,16},{4,20},{8,24},{12,28},{16,0},{20,4},{24,8},{28,12},{1,17},{... | collective-permute-start | bytes 995336 | tf_op jit(solution)/shard_map/ppermute | solution.py:46
  321.5 26.3 %collective-permute-start.54 = (bf16[128,2304]{1,0:T(8,128)(2,1)}, bf16[128,2304]{1,0:T(8,128)(2,1)S(1)}, u32[]{:S(2)}, u32[]{:S(2)}) collective-permute-start(bf16[128,2304]{1,0:T(8,128)(2,1)} %collective-permute-done.43), channel_id=1, source_target_pairs={{0,2},{1,3},{2,0},{3,1},{4,6},{5,7},{6,4},{7,5},{8,10},{9,11},{10,... | collective-permute-start | bytes 1769480 | tf_op jit(solution)/shard_map/ppermute | solution.py:46
  377.4 65.1 %collective-permute-start.53 = (bf16[256,2304]{1,0:T(8,128)(2,1)S(1)}, bf16[256,2304]{1,0:T(8,128)(2,1)S(1)}, u32[]{:S(2)}, u32[]{:S(2)}) collective-permute-start(bf16[256,2304]{1,0:T(8,128)(2,1)S(1)} %slice.342), channel_id=1, source_target_pairs={{0,1},{1,0},{2,3},{3,2},{4,5},{5,4},{6,7},{7,6},{8,9},{9,8},{10,11... | collective-permute-start | bytes 3538952 | tf_op jit(solution)/shard_map/ppermute | solution.py:68
  411.9 27.6 %collective-permute-start.58 = (bf16[128,2304]{1,0:T(8,128)(2,1)S(1)}, bf16[128,2304]{1,0:T(8,128)(2,1)S(1)}, u32[]{:S(2)}, u32[]{:S(2)}) collective-permute-start(bf16[128,2304]{1,0:T(8,128)(2,1)S(1)} %slice.577), channel_id=1, source_target_pairs={{0,2},{1,3},{2,0},{3,1},{4,6},{5,7},{6,4},{7,5},{8,10},{9,11},{10,... | collective-permute-start | bytes 1769480 | tf_op jit(solution)/shard_map/ppermute | solution.py:46
  426.9 25.3 %collective-permute-start.68 = (bf16[128,2304]{1,0:T(8,128)(2,1)S(1)}, bf16[128,2304]{1,0:T(8,128)(2,1)S(1)}, u32[]{:S(2)}, u32[]{:S(2)}) collective-permute-start(bf16[128,2304]{1,0:T(8,128)(2,1)S(1)} %slice.575), channel_id=1, source_target_pairs={{0,2},{1,3},{2,0},{3,1},{4,6},{5,7},{6,4},{7,5},{8,10},{9,11},{10,... | collective-permute-start | bytes 1769480 | tf_op jit(solution)/shard_map/ppermute | solution.py:46
  457.2 32.7 %collective-permute-start.70 = (bf16[128,2304]{1,0:T(8,128)(2,1)}, bf16[128,2304]{1,0:T(8,128)(2,1)}, u32[]{:S(2)}, u32[]{:S(2)}) collective-permute-start(bf16[128,2304]{1,0:T(8,128)(2,1)} %fusion.122), channel_id=1, source_target_pairs={{0,8},{4,12},{8,0},{12,4},{1,9},{5,13},{9,1},{13,5},{2,10},{6,14},... | collective-permute-start | bytes 1769480 | tf_op jit(solution)/shard_map/ppermute | solution.py:46
  512.7 26.5 %collective-permute-start.75 = (bf16[128,2304]{1,0:T(8,128)(2,1)}, bf16[128,2304]{1,0:T(8,128)(2,1)}, u32[]{:S(2)}, u32[]{:S(2)}) collective-permute-start(bf16[128,2304]{1,0:T(8,128)(2,1)} %get-tuple-element.314), channel_id=1, source_target_pairs={{0,8},{4,12},{8,0},{12,4},{1,9},{5,13},{9,1},{13,5},{2,10},{6,14},... | collective-permute-start | bytes 1769480 | tf_op jit(solution)/shard_map/ppermute | solution.py:46
  513.9 30.9 %collective-permute-start.78 = (bf16[128,2304]{1,0:T(8,128)(2,1)}, bf16[128,2304]{1,0:T(8,128)(2,1)S(1)}, u32[]{:S(2)}, u32[]{:S(2)}) collective-permute-start(bf16[128,2304]{1,0:T(8,128)(2,1)} %collective-permute-done.74), channel_id=1, source_target_pairs={{0,2},{1,3},{2,0},{3,1},{4,6},{5,7},{6,4},{7,5},{8,10},{9,11},{10,... | collective-permute-start | bytes 1769480 | tf_op jit(solution)/shard_map/ppermute | solution.py:46
  517.9 43.1 %collective-permute-start.72 = (bf16[256,2304]{1,0:T(8,128)(2,1)S(1)}, bf16[256,2304]{1,0:T(8,128)(2,1)S(1)}, u32[]{:S(2)}, u32[]{:S(2)}) collective-permute-start(bf16[256,2304]{1,0:T(8,128)(2,1)S(1)} %pad_maximum_fusion.5), channel_id=1, source_target_pairs={{0,1},{1,0},{2,3},{3,2},{4,5},{5,4},{6,7},{7,6},{8,9},{9,8},{10,11... | collective-permute-start | bytes 3538952 | tf_op jit(solution)/shard_map/ppermute | solution.py:68
  599.1 45.8 %collective-permute-start.88 = (bf16[256,2304]{1,0:T(8,128)(2,1)}, bf16[256,2304]{1,0:T(8,128)(2,1)}, u32[]{:S(2)}, u32[]{:S(2)}) collective-permute-start(bf16[256,2304]{1,0:T(8,128)(2,1)} %slice.370), channel_id=1, source_target_pairs={{0,1},{1,0},{2,3},{3,2},{4,5},{5,4},{6,7},{7,6},{8,9},{9,8},{10,11... | collective-permute-start | bytes 3538952 | tf_op jit(solution)/shard_map/ppermute | solution.py:68
  624.5 38.4 %collective-permute-start.85 = (bf16[256,2304]{1,0:T(8,128)(2,1)}, bf16[256,2304]{1,0:T(8,128)(2,1)}, u32[]{:S(2)}, u32[]{:S(2)}) collective-permute-start(bf16[256,2304]{1,0:T(8,128)(2,1)} %slice.367), channel_id=1, source_target_pairs={{0,1},{1,0},{2,3},{3,2},{4,5},{5,4},{6,7},{7,6},{8,9},{9,8},{10,11... | collective-permute-start | bytes 3538952 | tf_op jit(solution)/shard_map/ppermute | solution.py:68
  648.4 46.0 %collective-permute-start.84 = (bf16[256,2304]{1,0:T(8,128)(2,1)S(1)}, bf16[256,2304]{1,0:T(8,128)(2,1)S(1)}, u32[]{:S(2)}, u32[]{:S(2)}) collective-permute-start(bf16[256,2304]{1,0:T(8,128)(2,1)S(1)} %slice.294), channel_id=1, source_target_pairs={{0,1},{1,0},{2,3},{3,2},{4,5},{5,4},{6,7},{7,6},{8,9},{9,8},{10,11... | collective-permute-start | bytes 3538952 | tf_op jit(solution)/shard_map/ppermute | solution.py:68
  664.5 25.3 %collective-permute-start.86 = (bf16[128,2304]{1,0:T(8,128)(2,1)S(1)}, bf16[128,2304]{1,0:T(8,128)(2,1)S(1)}, u32[]{:S(2)}, u32[]{:S(2)}) collective-permute-start(bf16[128,2304]{1,0:T(8,128)(2,1)S(1)} %slice.573), channel_id=1, source_target_pairs={{0,2},{1,3},{2,0},{3,1},{4,6},{5,7},{6,4},{7,5},{8,10},{9,11},{10,... | collective-permute-start | bytes 1769480 | tf_op jit(solution)/shard_map/ppermute | solution.py:46
  671.3 32.2 %collective-permute-start.97 = (bf16[128,2304]{1,0:T(8,128)(2,1)S(1)}, bf16[128,2304]{1,0:T(8,128)(2,1)S(1)}, u32[]{:S(2)}, u32[]{:S(2)}) collective-permute-start(bf16[128,2304]{1,0:T(8,128)(2,1)S(1)} %copy-done.144), channel_id=1, source_target_pairs={{0,2},{1,3},{2,0},{3,1},{4,6},{5,7},{6,4},{7,5},{8,10},{9,11},{10,... | collective-permute-start | bytes 1769480 | tf_op jit(solution)/shard_map/ppermute | solution.py:46
  711.6 33.1 %collective-permute-start.101 = (bf16[128,2304]{1,0:T(8,128)(2,1)S(1)}, bf16[128,2304]{1,0:T(8,128)(2,1)S(1)}, u32[]{:S(2)}, u32[]{:S(2)}) collective-permute-start(bf16[128,2304]{1,0:T(8,128)(2,1)S(1)} %fusion.115), channel_id=1, source_target_pairs={{0,8},{4,12},{8,0},{12,4},{1,9},{5,13},{9,1},{13,5},{2,10},{6,14},... | collective-permute-start | bytes 1769480 | tf_op jit(solution)/shard_map/ppermute | solution.py:46
  759.6 31.9 %collective-permute-start.104 = (bf16[288,1152]{1,0:T(8,128)(2,1)}, bf16[288,1152]{1,0:T(8,128)(2,1)}, u32[]{:S(2)}, u32[]{:S(2)}) collective-permute-start(bf16[288,1152]{1,0:T(8,128)(2,1)} %get-tuple-element.349), channel_id=1, source_target_pairs={{0,16},{16,0},{1,17},{17,1},{2,18},{18,2},{3,19},{19,3},{4,20},{20... | collective-permute-start | bytes 1990664 | tf_op jit(solution)/shard_map/ppermute | solution.py:46
  764.9 31.4 %collective-permute-start.103 = (bf16[256,2304]{1,0:T(8,128)(2,1)S(1)}, bf16[256,2304]{1,0:T(8,128)(2,1)S(1)}, u32[]{:S(2)}, u32[]{:S(2)}) collective-permute-start(bf16[256,2304]{1,0:T(8,128)(2,1)S(1)} %pad_maximum_fusion.11), channel_id=1, source_target_pairs={{0,1},{1,0},{2,3},{3,2},{4,5},{5,4},{6,7},{7,6},{8,9},{9,8},{10,11... | collective-permute-start | bytes 3538952 | tf_op jit(solution)/shard_map/ppermute | solution.py:68
  777.3 46.1 %collective-permute-start.115 = (bf16[288,1152]{1,0:T(8,128)(2,1)}, bf16[288,1152]{1,0:T(8,128)(2,1)}, u32[]{:S(2)}, u32[]{:S(2)}) collective-permute-start(bf16[288,1152]{1,0:T(8,128)(2,1)} %get-tuple-element.366), channel_id=1, source_target_pairs={{0,16},{16,0},{1,17},{17,1},{2,18},{18,2},{3,19},{19,3},{4,20},{20... | collective-permute-start | bytes 1990664 | tf_op jit(solution)/shard_map/ppermute | solution.py:46
  791.5 33.5 %collective-permute-start.118 = (bf16[288,1152]{1,0:T(8,128)(2,1)}, bf16[288,1152]{1,0:T(8,128)(2,1)}, u32[]{:S(2)}, u32[]{:S(2)}) collective-permute-start(bf16[288,1152]{1,0:T(8,128)(2,1)} %get-tuple-element.372), channel_id=1, source_target_pairs={{0,16},{16,0},{1,17},{17,1},{2,18},{18,2},{3,19},{19,3},{4,20},{20... | collective-permute-start | bytes 1990664 | tf_op jit(solution)/shard_map/ppermute | solution.py:46
  796.2 29.3 %collective-permute-start.105 = (bf16[288,1152]{1,0:T(8,128)(2,1)}, bf16[288,1152]{1,0:T(8,128)(2,1)S(1)}, u32[]{:S(2)}, u32[]{:S(2)}) collective-permute-start(bf16[288,1152]{1,0:T(8,128)(2,1)} %add_convert_fusion.2), channel_id=1, source_target_pairs={{0,8},{4,12},{8,0},{12,4},{1,9},{5,13},{9,1},{13,5},{2,10},{6,14},... | collective-permute-start | bytes 1990664 | tf_op jit(solution)/shard_map/ppermute | solution.py:46
  831.1 43.8 %collective-permute-start.109 = (bf16[2,1,512,256]{3,2,1,0:T(8,128)(2,1)S(1)}, bf16[2,1,512,256]{3,2,1,0:T(8,128)(2,1)}, u32[]{:S(2)}, u32[]{:S(2)}) collective-permute-start(bf16[2,1,512,256]{3,2,1,0:T(8,128)(2,1)S(1)} %fusion.137), channel_id=1, source_target_pairs={{0,8},{4,12},{8,0},{12,4},{1,9},{5,13},{9,1},{13,5},{2,10},{6,14},... | collective-permute-start | bytes 1572872 | tf_op jit(solution)/shard_map/ppermute | solution.py:46
  842.3 50.6 %collective-permute-start.128 = (bf16[2,64,2304]{2,1,0:T(8,128)(2,1)S(1)}, bf16[2,64,2304]{2,1,0:T(8,128)(2,1)S(1)}, u32[]{:S(2)}, u32[]{:S(2)}) collective-permute-start(bf16[2,64,2304]{2,1,0:T(8,128)(2,1)S(1)} %get-tuple-element.390), channel_id=1, source_target_pairs={{0,3},{1,2},{2,1},{3,0},{4,7},{5,6},{6,5},{7,4},{8,11},{9,10},{10,... | collective-permute-start | bytes 1769480 | tf_op jit(solution)/shard_map/ppermute | solution.py:46
  842.3 40.1 %collective-permute-start.117 = (bf16[288,512]{1,0:T(8,128)(2,1)S(1)}, bf16[288,512]{1,0:T(8,128)(2,1)S(1)}, u32[]{:S(2)}, u32[]{:S(2)}) collective-permute-start(bf16[288,512]{1,0:T(8,128)(2,1)S(1)} %get-tuple-element.368), channel_id=1, source_target_pairs={{0,16},{16,0},{1,17},{17,1},{2,18},{18,2},{3,19},{19,3},{4,20},{20... | collective-permute-start | bytes 884744 | tf_op jit(solution)/shard_map/ppermute | solution.py:46
  844.0 38.5 %collective-permute-start.123 = (bf16[288,512]{1,0:T(8,128)(2,1)S(1)}, bf16[288,512]{1,0:T(8,128)(2,1)S(1)}, u32[]{:S(2)}, u32[]{:S(2)}) collective-permute-start(bf16[288,512]{1,0:T(8,128)(2,1)S(1)} %get-tuple-element.381), channel_id=1, source_target_pairs={{0,16},{16,0},{1,17},{17,1},{2,18},{18,2},{3,19},{19,3},{4,20},{20... | collective-permute-start | bytes 884744 | tf_op jit(solution)/shard_map/ppermute | solution.py:46
  844.5 43.1 %collective-permute-start.124 = (bf16[288,1152]{1,0:T(8,128)(2,1)S(1)}, bf16[288,1152]{1,0:T(8,128)(2,1)S(1)}, u32[]{:S(2)}, u32[]{:S(2)}) collective-permute-start(bf16[288,1152]{1,0:T(8,128)(2,1)S(1)} %copy-done.135), channel_id=1, source_target_pairs={{0,4},{4,8},{8,12},{12,0},{1,5},{5,9},{9,13},{13,1},{2,6},{6,10},{... | collective-permute-start | bytes 1990664 | tf_op jit(solution)/shard_map/ppermute | solution.py:46
  912.5 33.1 %collective-permute-start.126 = (bf16[288,512]{1,0:T(8,128)(2,1)S(1)}, bf16[288,512]{1,0:T(8,128)(2,1)S(1)}, u32[]{:S(2)}, u32[]{:S(2)}) collective-permute-start(bf16[288,512]{1,0:T(8,128)(2,1)S(1)} %add_convert_fusion.13), channel_id=1, source_target_pairs={{0,8},{4,12},{8,0},{12,4},{1,9},{5,13},{9,1},{13,5},{2,10},{6,14},... | collective-permute-start | bytes 884744 | tf_op jit(solution)/shard_map/ppermute | solution.py:46
  912.6 34.5 %collective-permute-start.145 = (bf16[64,2304]{1,0:T(8,128)(2,1)}, bf16[64,2304]{1,0:T(8,128)(2,1)S(1)}, u32[]{:S(2)}, u32[]{:S(2)}) collective-permute-start(bf16[64,2304]{1,0:T(8,128)(2,1)} %copy-done.64), channel_id=1, source_target_pairs={{0,16},{16,0},{1,17},{17,1},{2,18},{18,2},{3,19},{19,3},{4,20},{20... | collective-permute-start | bytes 884744 | tf_op jit(solution)/shard_map/ppermute | solution.py:46
  913.1 38.6 %collective-permute-start.143 = (bf16[64,2304]{1,0:T(8,128)(2,1)}, bf16[64,2304]{1,0:T(8,128)(2,1)S(1)}, u32[]{:S(2)}, u32[]{:S(2)}) collective-permute-start(bf16[64,2304]{1,0:T(8,128)(2,1)} %copy-done.63), channel_id=1, source_target_pairs={{0,16},{16,0},{1,17},{17,1},{2,18},{18,2},{3,19},{19,3},{4,20},{20... | collective-permute-start | bytes 884744 | tf_op jit(solution)/shard_map/ppermute | solution.py:46
  920.2 46.9 %collective-permute-start.110 = (bf16[256,2304]{1,0:T(8,128)(2,1)S(1)}, bf16[256,2304]{1,0:T(8,128)(2,1)S(1)}, u32[]{:S(2)}, u32[]{:S(2)}) collective-permute-start(bf16[256,2304]{1,0:T(8,128)(2,1)S(1)} %slice.385), channel_id=1, source_target_pairs={{0,1},{1,0},{2,3},{3,2},{4,5},{5,4},{6,7},{7,6},{8,9},{9,8},{10,11... | collective-permute-start | bytes 3538952 | tf_op jit(solution)/shard_map/ppermute | solution.py:68
  955.5 58.6 %collective-permute-start.144 = (bf16[64,2304]{1,0:T(8,128)(2,1)}, bf16[64,2304]{1,0:T(8,128)(2,1)}, u32[]{:S(2)}, u32[]{:S(2)}) collective-permute-start(bf16[64,2304]{1,0:T(8,128)(2,1)} %get-tuple-element.426), channel_id=1, source_target_pairs={{0,16},{16,0},{1,17},{17,1},{2,18},{18,2},{3,19},{19,3},{4,20},{20... | collective-permute-start | bytes 884744 | tf_op jit(solution)/shard_map/ppermute | solution.py:46
  960.9 36.5 %collective-permute-start.129 = (bf16[72,512]{1,0:T(8,128)(2,1)S(1)}, bf16[72,512]{1,0:T(8,128)(2,1)S(1)}, u32[]{:S(2)}, u32[]{:S(2)}) collective-permute-start(bf16[72,512]{1,0:T(8,128)(2,1)S(1)} %get-tuple-element.391), channel_id=1, source_target_pairs={{0,2},{1,3},{2,0},{3,1},{4,6},{5,7},{6,4},{7,5},{8,10},{9,11},{10,... | collective-permute-start | bytes 221192 | tf_op jit(solution)/shard_map/ppermute | solution.py:46
  968.9 30.0 %collective-permute-start.112 = (bf16[128,2304]{1,0:T(8,128)(2,1)S(1)}, bf16[128,2304]{1,0:T(8,128)(2,1)S(1)}, u32[]{:S(2)}, u32[]{:S(2)}) collective-permute-start(bf16[128,2304]{1,0:T(8,128)(2,1)S(1)} %slice.570), channel_id=1, source_target_pairs={{0,2},{1,3},{2,0},{3,1},{4,6},{5,7},{6,4},{7,5},{8,10},{9,11},{10,... | collective-permute-start | bytes 1769480 | tf_op jit(solution)/shard_map/ppermute | solution.py:46
  977.5 37.2 %collective-permute-start.150 = (bf16[64,2304]{1,0:T(8,128)(2,1)}, bf16[64,2304]{1,0:T(8,128)(2,1)}, u32[]{:S(2)}, u32[]{:S(2)}) collective-permute-start(bf16[64,2304]{1,0:T(8,128)(2,1)} %add_convert_fusion.7), channel_id=1, source_target_pairs={{0,8},{4,12},{8,0},{12,4},{1,9},{5,13},{9,1},{13,5},{2,10},{6,14},... | collective-permute-start | bytes 884744 | tf_op jit(solution)/shard_map/ppermute | solution.py:46
  (317 other events, 4626.5 us)

commit v3 on v2

--- a/solution.py
+++ b/solution.py
@@ -51,7 +51,7 @@
 
 class Lines:
     def __init__(self):
-        self.fsdp, self.ctx, self.head = Line(DEPTH), Line(DEPTH), Line(DEPTH)
+        self.fsdp, self.ctx, self.head, self.pair = Line(2), Line(2), Line(2), Line(2)
 
 
 DEPTH = 2
@@ -71,6 +71,44 @@
 
 def send_ctx(lines, values, step):
     return lines.ctx.send([(values, "ctx", ring_pairs(lax.axis_size("ctx"), step))])[0]
+
+
+def swap_ctx(lines, values, other):
+    pairs = [(z, z ^ other) for z in range(lax.axis_size("ctx"))]
+    line = lines.pair if other == 1 else lines.ctx
+    return line.send([(values, "ctx", pairs)])[0]
+
+
+def unit_part(lines, one, other):
+    return ([one] + swap_fsdp(lines, one), lambda z: z ^ other, lambda z: z >= 0)
+
+
+def units_back(lines, pieces):
+    size_x, size_z = lax.axis_size("fsdp"), lax.axis_size("ctx")
+    x, z = lax.axis_index("fsdp"), lax.axis_index("ctx")
+    order = [k ^ 1 for k in range(2, size_z)] + [1, 0]
+    chosen = [(k, step) for k in order for step in range(size_x)]
+    picked = pick_pieces(
+        pieces, [lax.rem(x + step, size_x) * size_z + (z ^ k) for k, step in chosen]
+    )
+    picked = dict(zip(chosen, picked))
+    sums = {}
+    for k in order:
+        sums[k] = picked[k, 0].astype(F32)
+        for step in range(1, size_x):
+            pairs = ring_pairs(size_x, step)
+            came = lines.fsdp.send([(picked[k, step], "fsdp", pairs)])[0]
+            sums[k] = sums[k] + came.astype(F32)
+    return sums
+
+
+def units_sent(lines, sums, low, *others):
+    total = sums[low]
+    for other in range(2, lax.axis_size("ctx"), 2):
+        one = sums[other ^ low].astype(BF16)
+        one = swap_ctx(lines, after(one, *others) if others else one, other)
+        total = total + one.astype(F32)
+    return swap_ctx(lines, total.astype(BF16), 1) if low else total
 
 
 def swap_fsdp(lines, values, valid=lambda z: True):
@@ -419,12 +457,11 @@
     return max(one for one in range(1, rows + 1) if rows % one == 0 and one <= most and (one % 16 == 0 or one == rows))
 
 
-def split_units(weight, z):
-    size = lax.axis_size("ctx")
+def split_units(weight, own, size):
     count, rows, cols = weight.shape[0], weight.shape[1], weight.shape[2] // size
     block = row_block(rows, 96)
 
-    def kernel(z_ref, in_ref, *refs):
+    def kernel(own_ref, in_ref, *refs):
         outs, kept = refs[:size], refs[size]
         for part in range(size):
             for one in range(count):
@@ -432,7 +469,7 @@
                     one, :, part * cols : (part + 1) * cols
                 ]
         for k in range(size):
-            outs[k][...] = kept[lax.rem(z_ref[0] + k, size)].astype(BF16)
+            outs[k][...] = kept[own_ref[0] ^ k].astype(BF16)
 
     return pl.pallas_call(
         kernel,
@@ -444,20 +481,20 @@
         compiler_params=params(),
         cost_estimate=cost(weight.size * 6),
         name="split_units",
-    )(scalars(z), weight)
-
-
-def adam_units(came, z, weight, first_old, second_old, step_rate):
+    )(scalars(own), weight)
+
+
+def adam_units(came, own, weight, first_old, second_old, step_rate):
     size = len(came)
     count = weight.shape[0]
     rows, cols = came[0].shape[0], came[0].shape[1] // count
     block = row_block(rows, 96 // count)
 
-    def kernel(z_ref, *refs):
+    def kernel(own_ref, *refs):
         pieces, (weight_ref, first_ref, second_ref) = refs[:size], refs[size : size + 3]
         outs, kept = refs[size + 3 : size + 7], refs[size + 7]
         for k in range(size):
-            kept[lax.rem(z_ref[0] + (size - k), size)] = pieces[k][...].astype(F32)
+            kept[own_ref[0] ^ k] = pieces[k][...].astype(F32)
         for part in range(size):
             for one in range(count):
                 outs[0][one, :, part * cols : (part + 1) * cols] = kept[
@@ -480,7 +517,7 @@
         compiler_params=params(),
         cost_estimate=cost(weight.size * 30),
         name="adam_units",
-    )(scalars(z), *came, weight, first_old, second_old)
+    )(scalars(own), *came, weight, first_old, second_old)
 
 
 def adam_qkv(query_pieces, kv_pieces, own, weight, first_old, second_old):
@@ -643,8 +680,6 @@
         )
 
     lines = Lines()
-    unit_order = [k for k in far_first(size_z) if k]
-    far_k = unit_order[0]
 
     pieces = head_exchange(lines, split_heads(qkv_weight, own_h))
     qkv_piece = join_rows(pieces, own_h)
@@ -664,17 +699,24 @@
     out_full = jnp.transpose(out_full, (1, 0, 2, 3)).reshape(query_cols, width)
 
     ff_rows = gate_up.shape[1]
-    ff_cols = gate_up.shape[2] // size_z
+    ff_cols = gate_up.shape[2] // 2
+    low = lax.rem(z, 2)
     down_turned = down_weight.T[None]
-    gate_up_low = split_units(after(gate_up, qkv_piece), z)
-    down_low = split_units(after(down_turned, qkv_piece), z)
-
-    def unit_part(k, low):
-        one = send_ctx(lines, low[k], k) if k else low[0]
-        source = lambda z: lax.rem(z - k + size_z, size_z)
-        return ([one] + swap_fsdp(lines, one), source, lambda z: z >= 0)
-
-    gate_up_parts = [unit_part(k, gate_up_low) for k in (0, far_k)]
+    gate_up_halves = split_units(after(gate_up, qkv_piece), low, 2)
+    down_halves = split_units(after(down_turned, qkv_piece), low, 2)
+    hops = range(2, size_z, 2)
+
+    def far_units(one, k):
+        return [(swap_ctx(lines, one, other), k ^ other) for other in hops]
+
+    def unit_parts(pieces):
+        return [unit_part(lines, one, k) for one, k in pieces]
+
+    gate_up_parts = unit_parts([(gate_up_halves[0], 0)])
+    gate_up_far = far_units(gate_up_halves[0], 0)
+    gate_up_near = swap_ctx(lines, gate_up_halves[1], 1)
+    down_near = swap_ctx(lines, down_halves[1], 1)
+    gate_up_parts += unit_parts(gate_up_far) + unit_parts([(gate_up_near, 1)])
 
     block_tokens = head_gather(lines, jnp.concatenate(more_tokens), head_bits()[1:]).astype(F32)
     inputs = tokens.astype(F32)
@@ -695,7 +737,9 @@
     query_pos = jnp.tile(block_pos, group)
     own_kv = jnp.stack([own_keys, own_values])
     kv_slots = ctx_slots(lines, own_kv)
-    gate_up_parts += [unit_part(k, gate_up_low) for k in unit_order[1:]]
+    down_parts = unit_parts([(down_halves[0], 0), (down_near, 1)])
+    gate_up_parts += unit_parts(far_units(gate_up_near, 1))
+    down_parts += unit_parts(far_units(down_halves[0], 0) + far_units(down_near, 1))
     pos_slots = [positions_of(lax.rem(z + k, size_z)) for k in range(size_z)]
     exp_total = 0.0
     summed = 0.0
@@ -716,52 +760,51 @@
     middle = inputs + rms_norm(attn_out, gain_rows[1])
     second_normed = rms_norm(middle, gain_rows[2]).astype(BF16)
 
-    def all_slots(rows):
-        if size_h < 2:
-            return ctx_slots(lines, rows)
-        slots = ctx_slots(lines, rows, swap_top, jnp.concatenate)
-        return [head_gather(lines, one, head_bits()[1:]) for one in slots]
-
-    def sum_slots(parts):
-        return sum_ctx_slots(lines, lambda k: head_reduce(lines, parts[k]))
-
-    normed_slots = all_slots(second_normed)
-    down_parts = [unit_part(k, down_low) for k in [0] + unit_order]
+    low_bits, top_bits = head_bits()[1:], head_bits()[:1]
+
+    def both_blocks(rows):
+        other = swap_ctx(lines, rows, 1)
+        return [head_gather(lines, rows), head_gather(lines, other)]
+
+    def sum_blocks(parts):
+        own, other = parts
+        other = swap_ctx(lines, head_reduce(lines, other).astype(BF16), 1)
+        return head_reduce(lines, own) + other.astype(F32)
+
+    normed_slots = both_blocks(second_normed)
     gate_up_full = put_pieces(gate_up_parts).reshape(width, 2 * ff_cols)
     down_full = put_pieces(down_parts).reshape(width, ff_cols)
     act_slots = [matmul(rows, gate_up_full) for rows in normed_slots]
     hidden_slots = [
         gated_unit(act[:, :ff_cols], act[:, ff_cols:]).astype(BF16) for act in act_slots
     ]
-    ffn_out = sum_slots([matmul_nt(hidden, down_full).astype(BF16) for hidden in hidden_slots])
+    ffn_out = sum_blocks([matmul_nt(hidden, down_full).astype(BF16) for hidden in hidden_slots])
     mixed_out = (middle + rms_norm(ffn_out, gain_rows[3])).astype(BF16)
 
     upstream = cotangent.astype(F32)
     grad_ffn, gain_grad_ffn = norm_back(ffn_out, gain_rows[3], upstream)
-    grad_slots = all_slots(grad_ffn.astype(BF16))
-
-    def units_back(term, cols):
-        sums = sum_over_fsdp(
-            lines, term.reshape(size_x * size_z, ff_rows, cols), unit_order + [0]
-        )
-        return {k: one if k == 0 else one.astype(BF16) for k, one in sums.items()}
-
-    down_term = matmul_tn(jnp.concatenate(grad_slots), jnp.concatenate(hidden_slots)).astype(BF16)
-    down_back = units_back(down_term, ff_cols)
-    for k in unit_order:
-        down_back[k] = send_ctx(lines, down_back[k], k)
-    grad_act_slots = []
+    grad_slots = both_blocks(grad_ffn.astype(BF16))
+    grad_act_slots, grad_second_parts = [], []
     for rows, act in zip(grad_slots, act_slots):
         grad_hidden = matmul(rows, down_full)
         unit_out, unit_back = jax.vjp(gated_unit, act[:, :ff_cols], act[:, ff_cols:])
         grad_act_slots.append(jnp.concatenate(unit_back(grad_hidden), axis=1).astype(BF16))
-    grad_second_parts = [matmul_nt(rows, gate_up_full).astype(BF16) for rows in grad_act_slots]
-    gate_up_term = matmul_tn(jnp.concatenate(normed_slots), jnp.concatenate(grad_act_slots))
+        grad_second_parts.append(matmul_nt(grad_act_slots[-1], gate_up_full).astype(BF16))
+    other = head_reduce(lines, grad_second_parts[1]).astype(BF16)
+    other_came = lines.head.came[-1] if size_h > 1 else ()
+    other = swap_ctx(lines, other, 1)
+    own = head_reduce(lines, grad_second_parts[0])
+    down_rows = after(jnp.concatenate(grad_slots), grad_second_parts[1])
+    down_term = matmul_tn(down_rows, jnp.concatenate(hidden_slots)).astype(BF16)
+    down_back = units_back(lines, down_term.reshape(size_x * size_z, ff_rows, ff_cols))
+    gate_up_rows = after(jnp.concatenate(normed_slots), down_term, *other_came)
+    gate_up_term = matmul_tn(gate_up_rows, jnp.concatenate(grad_act_slots))
     gate_up_term = gate_up_term.astype(BF16)
-    grad_second_parts[0] = after(grad_second_parts[0], gate_up_term)
-    grad_second = sum_slots(grad_second_parts)
-    gate_up_back = units_back(gate_up_term, 2 * ff_cols)
-    gate_up_back[far_k] = send_ctx(lines, gate_up_back[far_k], far_k)
+    grad_second = own + other.astype(F32)
+    down_other = units_sent(lines, down_back, 1, other)
+    down_back = [units_sent(lines, down_back, 0), down_other]
+    gate_up_back = units_back(lines, gate_up_term.reshape(size_x * size_z, ff_rows, 2 * ff_cols))
+    gate_up_other = units_sent(lines, gate_up_back, 1)
 
     grad_middle_part, gain_grad_middle = norm_back(middle, gain_rows[2], grad_second)
     grad_middle = upstream + grad_middle_part
@@ -786,34 +829,27 @@
         grad_query = grad_query + query_part
         kv_parts[k] = jnp.stack([key_part, value_part])
     grad_kv = sum_ctx_slots(lines, lambda k: kv_parts[k])
-    for k in unit_order[1:]:
-        gate_up_back[k] = send_ctx(lines, gate_up_back[k], k)
+    gate_up_back = [units_sent(lines, gate_up_back, 0), gate_up_other]
     out_sets = head_exchange(lines, pick_pieces(out_term, [own_h ^ i for i in range(size_h)]))
     out_term = place(out_sets, [own_h ^ i for i in range(size_h)])
 
     grad_query = grad_query.astype(BF16).astype(F32).reshape(query_local, block_rows, HD)
     query_proj = rows_of(rope_back(grad_query, cosine, sine_table) * query_scale).astype(BF16)
-    query_term = matmul_tn(first_normed, query_proj).astype(BF16)
-    query_sums = sum_over_fsdp(
-        lines, query_term.reshape(size_x * size_z, size_h * qkv_rows, query_cols), ctx_order()
-    )
-    query_sum = sum_ctx_slots(lines, lambda k: query_sums[k])
     grad_kv = grad_kv.astype(BF16).astype(F32)
     kv_proj = jnp.concatenate(
         [rows_of(rope_back(grad_kv[0], cosine, sine_table)), rows_of(grad_kv[1])], axis=1
     ).astype(BF16)
-    kv_term = matmul_tn(first_normed, kv_proj).astype(BF16)
-    kv_sums = sum_over_fsdp(
-        lines, kv_term.reshape(size_x * size_z, size_h * qkv_rows, 2 * kv_cols), ctx_order()
-    )
-    kv_sum = sum_ctx_slots(lines, lambda k: kv_sums[k])
     grad_proj = jnp.concatenate([query_proj, kv_proj], axis=1)
+    qkv_term = matmul_tn(first_normed, grad_proj).astype(BF16)
+    qkv_sums = sum_over_fsdp(
+        lines, qkv_term.reshape(size_x * size_z, size_h * qkv_rows, local_cols), ctx_order()
+    )
+    qkv_sum = sum_ctx_slots(lines, lambda k: qkv_sums[k])
     grad_first = head_reduce(lines, matmul_nt(grad_proj, qkv_full).astype(BF16))
     grad_input_part, gain_grad_input = norm_back(inputs, gain_rows[0], grad_first)
     tokens_grad = (grad_middle + grad_input_part).astype(BF16)
 
-    query_pieces = head_exchange(lines, split_rows([query_sum], own_h))
-    kv_pieces = head_exchange(lines, split_rows([kv_sum], own_h))
+    qkv_pieces = head_exchange(lines, split_rows([qkv_sum], own_h))
     out_sums = sum_over_fsdp(
         lines, out_term.reshape(size_x * size_z, out_rows, width), ctx_order()
     )
@@ -823,17 +859,19 @@
     )
 
     qkv_grad, qkv_first_new, qkv_second_new, qkv_new = adam_qkv(
-        query_pieces, kv_pieces, own_h, qkv_weight, qkv_first, qkv_second
+        [one[:, :query_cols] for one in qkv_pieces],
+        [one[:, query_cols:] for one in qkv_pieces],
+        own_h, qkv_weight, qkv_first, qkv_second
     )
     out_first_new, out_second_new, out_new = adam_step(
         out_weight, out_first, out_second, out_grad, RATE_MATRIX, WEIGHT_DECAY
     )
     gate_up_grad, gate_up_first_new, gate_up_second_new, gate_up_new = adam_units(
-        [gate_up_back[k] for k in range(size_z)], z, gate_up, gate_up_first, gate_up_second, RATE_MATRIX
+        gate_up_back, low, gate_up, gate_up_first, gate_up_second, RATE_MATRIX
     )
     down_outs = adam_units(
-        [down_back[k] for k in range(size_z)],
-        z,
+        down_back,
+        low,
         down_turned,
         down_first.T[None],
         down_second.T[None],

time: 1030 us -> 953 us (0.925)
  starting transfers between devices: 236 us -> 154 us
  local copies, waits for them, and re-layouts: 71.9 us -> 52.1 us
  matrix products: 126 us -> 139 us
    ppermute x126 -> x94, starting transfers between devices: 219 us -> 142 us  [send(): lax.ppermute(one, axes, pairs)]
    unnamed x438 -> x332, local copies, waits for them, and re-layouts: 47.9 us -> 28.2 us
    unnamed x9 -> x5, other arithmetic: 13.3 us -> 2.36 us
    dot_general x10 -> x6, matrix products: 40.3 us -> 47.1 us  [matmul(): return jnp.dot(left, right, preferred_element_type=F32)]
    ppermute x126 -> x94, waiting for transfers between devices: 418 us -> 425 us  [send(): lax.ppermute(one, axes, pairs)]
    dot_general x5 -> x4, matrix products: 33.6 us -> 36.6 us  [matmul_tn(): lax.dot_general(left, right, (((0,), (0,)), ((), ())), preferred_element_...]
    dot_general x10 -> x6, matrix products: 32.2 us -> 32.1 us  [matmul_nt(): lax.dot_general(left, right, (((1,), (1,)), ((), ())), preferred_element_...]
  transfers between devices with their start and end apart: 153 -> 112, of which waited for: 55 -> 48; matrix products, arithmetic and copies ran while one was open for 23% -> 25% of each run, Pallas kernels for 7% -> 8%
where the time goes in v3:
time: 953 us; the launch traced here: 942 us
  waiting for transfers between devices  430 us (45%)
  starting transfers between devices  154 us (16%)
  matrix products  139 us (15%)
  other arithmetic  84 us (9%)
  Pallas kernels  79.2 us (8%)
  local copies, waits for them, and re-layouts  52.1 us (5%)
    ppermute x94, waiting for transfers between devices, send(): lax.ppermute(one, axes, pairs)  425 us
    ppermute x94, starting transfers between devices, send(): lax.ppermute(one, axes, pairs)  142 us
    dot_general x6, matrix products, matmul(): return jnp.dot(left, right, preferred_element_type=F32)  47.1 us
    dot_general x4, matrix products, matmul_tn(): lax.dot_general(left, right, (((0,), (0,)), ((), ())), preferred_element_...  36.6 us
    dot_general x6, matrix products, matmul_nt(): lax.dot_general(left, right, (((1,), (1,)), ((), ())), preferred_element_...  32.1 us
    unnamed x332, local copies, waits for them, and re-layouts  28.2 us
    pallas_call x2, Pallas kernels, adam_units(): pl.pallas_call(kernel, grid=(rows // block,), out_shape=[jax.ShapeDtypeSt...  25.7 us
    pallas_call x6, Pallas kernels, place(): pl.pallas_call(kernel, out_shape=jax.ShapeDtypeStruct(shape, pieces[0].dt...  23.3 us
  transfers between devices with their start and end apart: 112, of which 48 were waited for; matrix products, arithmetic and copies ran while one was open for 25% of the time, Pallas kernels for 8%

profile of v3, /device:TPU:0, one launch (start us, length us, event | category | flops | bytes accessed | tf_op | source)
XLA Modules:
  0.0 942.4 jit_solution(1854401414137362134)
XLA Ops:
  20.9 8.3 collective-permute-done.8.refs_4_
  41.5 18.5 %collective-permute-done.10.refs_6_ = bf16[288,1024]{1,0:T(8,128)(2,1)S(1)} collective-permute-done((bf16[288,1024]{1,0:T(8,128)(2,1)S(1)}, bf16[288,1024]{1,0:T(8,128)(2,1)S(1)}, u32[]{:S(2)}, u32[]{:S(2)}) %collective-permute-start.10) | collective-permute-done | bytes 589856 | tf_op jit(solution)/shard_map/ppermute | solution.py:46
  65.4 7.1 all-to-all-start
  99.8 10.3 %collective-permute-done.16.refs_6_ = bf16[64,2304]{1,0:T(8,128)(2,1)S(1)} collective-permute-done((bf16[64,2304]{1,0:T(8,128)(2,1)S(1)}, bf16[64,2304]{1,0:T(8,128)(2,1)S(1)}, u32[]{:S(2)}, u32[]{:S(2)}) %collective-permute-start.16) | collective-permute-done | bytes 294944 | tf_op jit(solution)/shard_map/ppermute | solution.py:46
  115.8 5.5 fusion.158
  125.0 7.0 collective-permute-done.18.refs_8_
  153.7 25.0 %collective-permute-done.20 = bf16[2,1,512,256]{3,2,1,0:T(8,128)(2,1)} collective-permute-done((bf16[2,1,512,256]{3,2,1,0:T(8,128)(2,1)}, bf16[2,1,512,256]{3,2,1,0:T(8,128)(2,1)}, u32[]{:S(2)}, u32[]{:S(2)}) %collective-permute-start.20) | collective-permute-done | bytes 524320 | tf_op jit(solution)/shard_map/ppermute | solution.py:46
  187.7 16.0 %collective-permute-done.22 = bf16[2,1,512,256]{3,2,1,0:T(8,128)(2,1)S(1)} collective-permute-done((bf16[2,1,512,256]{3,2,1,0:T(8,128)(2,1)}, bf16[2,1,512,256]{3,2,1,0:T(8,128)(2,1)S(1)}, u32[]{:S(2)}, u32[]{:S(2)}) %collective-permute-start.22) | collective-permute-done | bytes 524320 | tf_op jit(solution)/shard_map/ppermute | solution.py:46
  214.2 12.4 %collective-permute-done.23 = bf16[2,1,512,256]{3,2,1,0:T(8,128)(2,1)S(1)} collective-permute-done((bf16[2,1,512,256]{3,2,1,0:T(8,128)(2,1)S(1)}, bf16[2,1,512,256]{3,2,1,0:T(8,128)(2,1)S(1)}, u32[]{:S(2)}, u32[]{:S(2)}) %collective-permute-start.23) | collective-permute-done | bytes 524320 | tf_op jit(solution)/shard_map/ppermute | solution.py:46
  248.3 23.9 %collective-permute-done.35.refs_1_ = bf16[288,2304]{1,0:T(8,128)(2,1)} collective-permute-done((bf16[288,2304]{1,0:T(8,128)(2,1)}, bf16[288,2304]{1,0:T(8,128)(2,1)}, u32[]{:S(2)}, u32[]{:S(2)}) %collective-permute-start.35) | collective-permute-done | bytes 1327136 | tf_op jit(solution)/shard_map/ppermute | solution.py:46
  273.1 27.8 %collective-permute-done.39.refs_6_ = bf16[288,2304]{1,0:T(8,128)(2,1)} collective-permute-done((bf16[288,2304]{1,0:T(8,128)(2,1)}, bf16[288,2304]{1,0:T(8,128)(2,1)}, u32[]{:S(2)}, u32[]{:S(2)}) %collective-permute-start.39) | collective-permute-done | bytes 1327136 | tf_op jit(solution)/shard_map/ppermute | solution.py:46
  308.5 6.4 collective-permute-done.38.refs_5_
  315.7 6.3 collective-permute-done.33
  323.1 29.6 %collective-permute-done.44.refs_4_ = bf16[288,1152]{1,0:T(8,128)(2,1)} collective-permute-done((bf16[288,1152]{1,0:T(8,128)(2,1)S(1)}, bf16[288,1152]{1,0:T(8,128)(2,1)}, u32[]{:S(2)}, u32[]{:S(2)}) %collective-permute-start.44) | collective-permute-done | bytes 663584 | tf_op jit(solution)/shard_map/ppermute | solution.py:46
  358.8 8.1 collective-permute-done.46.refs_6_
  369.5 8.7 place.9
  378.1 10.9 %collective-permute-done.47.refs_7_ = bf16[288,1152]{1,0:T(8,128)(2,1)} collective-permute-done((bf16[288,1152]{1,0:T(8,128)(2,1)}, bf16[288,1152]{1,0:T(8,128)(2,1)}, u32[]{:S(2)}, u32[]{:S(2)}) %collective-permute-start.47) | collective-permute-done | bytes 663584 | tf_op jit(solution)/shard_map/ppermute | solution.py:46
  389.0 5.6 place.10
  396.3 9.5 %fusion.24 = f32[512,2304]{1,0:T(8,128)S(1)} fusion(bf16[2304,2304]{1,0:T(8,128)(2,1)} %bitcast.220, bf16[256,2304]{1,0:T(8,128)(2,1)} %collective-permute-done.34, bf16[128,2304]{1,0:T(8,128)(2,1)S(1)} %copy-done.56, bf16[128,2304]{1,0:T(8,128)(2,1)S(1)} %copy-done.60), kind=kOutput, calls=%fused_computation.45 | convolution fusion | flops 5442895872 | bytes 17694720 | tf_op jit(solution)/shard_map/dot_general | solution.py:559
  405.9 8.1 fusion.30
  431.4 11.2 %collective-permute-done.54 = bf16[128,2304]{1,0:T(8,128)(2,1)S(1)} collective-permute-done((bf16[128,2304]{1,0:T(8,128)(2,1)S(1)}, bf16[128,2304]{1,0:T(8,128)(2,1)S(1)}, u32[]{:S(2)}, u32[]{:S(2)}) %collective-permute-start.54) | collective-permute-done | bytes 589856 | tf_op jit(solution)/shard_map/ppermute | solution.py:46
  445.2 9.5 %collective-permute-done.51 = bf16[128,2304]{1,0:T(8,128)(2,1)} collective-permute-done((bf16[128,2304]{1,0:T(8,128)(2,1)}, bf16[128,2304]{1,0:T(8,128)(2,1)}, u32[]{:S(2)}, u32[]{:S(2)}) %collective-permute-start.51) | collective-permute-done | bytes 589856 | tf_op jit(solution)/shard_map/ppermute | solution.py:46
  466.7 8.7 collective-permute-done.56
  484.8 8.8 collective-permute-done.60
  496.0 10.3 %fusion.16 = (bf16[512,1152]{1,0:T(8,128)(2,1)}, bf16[512,1152]{1,0:T(8,128)(2,1)}) fusion(f32[512,2304]{1,0:T(8,128)} %copy-done.43, bf16[2304,1152]{1,0:T(8,128)(2,1)} %bitcast.229, bf16[256,2304]{1,0:T(8,128)(2,1)} %collective-permute-done.57, bf16[128,2304]{1,0:T(8,128)(2,1)S(1)} %copy-done.58, bf16[128,2304]{1,0:T(8,128)(2,1)S(1)} %copy-done.62), kind=kOutput, calls=%fused_computation.36 | convolution fusion | flops 2739142656 | bytes 14745600 | tf_op jit(solution)/shard_map/dot_general | solution.py:559
  506.4 8.4 convolution_convert_fusion.8
  522.7 10.3 %fusion.23 = (bf16[512,1152]{1,0:T(8,128)(2,1)}, bf16[512,1152]{1,0:T(8,128)(2,1)}) fusion(f32[512,2304]{1,0:T(8,128)} %copy-done.42, bf16[2304,1152]{1,0:T(8,128)(2,1)} %bitcast.230, bf16[256,2304]{1,0:T(8,128)(2,1)} %collective-permute-done.62, bf16[128,2304]{1,0:T(8,128)(2,1)} %collective-permute-done.60, bf16[128,2304]{1,0:T(8,128)(2,1)S(1)} %collective-permute-done.59), kind=kOutput, calls=%fused_computation.43 | convolution fusion | flops 2739142656 | bytes 14745600 | tf_op jit(solution)/shard_map/dot_general | solution.py:559
  533.1 8.2 convolution_convert_fusion.7
  545.2 9.8 %convolution_convert_fusion.1 = bf16[2304,1152]{1,0:T(8,128)(2,1)} fusion(bf16[1024,2304]{1,0:T(8,128)(2,1)} %constant_dynamic-update-slice_fusion.6, bf16[512,1152]{1,0:T(8,128)(2,1)S(1)} %copy-done.86, bf16[512,1152]{1,0:T(8,128)(2,1)S(1)} %copy-done.88), kind=kOutput, calls=%fused_computation.1 | convolution fusion | flops 5443190784 | bytes 12386304 | tf_op jit(solution)/shard_map/dot_general | solution.py:567
  567.7 9.5 %collective-permute-done.75 = bf16[288,1152]{1,0:T(8,128)(2,1)S(1)} collective-permute-done((bf16[288,1152]{1,0:T(8,128)(2,1)S(1)}, bf16[288,1152]{1,0:T(8,128)(2,1)S(1)}, u32[]{:S(2)}, u32[]{:S(2)}) %collective-permute-start.75) | collective-permute-done | bytes 663584 | tf_op jit(solution)/shard_map/ppermute | solution.py:46
  579.7 11.8 %collective-permute-done.68 = bf16[288,1152]{1,0:T(8,128)(2,1)S(1)} collective-permute-done((bf16[288,1152]{1,0:T(8,128)(2,1)S(1)}, bf16[288,1152]{1,0:T(8,128)(2,1)S(1)}, u32[]{:S(2)}, u32[]{:S(2)}) %collective-permute-start.68) | collective-permute-done | bytes 663584 | tf_op jit(solution)/shard_map/ppermute | solution.py:46
  594.9 17.3 %convolution_convert_fusion = bf16[2304,2304]{1,0:T(8,128)(2,1)} fusion(bf16[1024,2304]{1,0:T(8,128)(2,1)} %copy-done.114, bf16[512,1152]{1,0:T(8,128)(2,1)} %get-tuple-element.385, bf16[512,1152]{1,0:T(8,128)(2,1)} %get-tuple-element.384, bf16[512,1152]{1,0:T(8,128)(2,1)} %get-tuple-element.383, bf16[512,1152]{1,0:T(8,128)(2,1)} %get-tuple-element.382), kind=kOutput, calls=%fused_computation | convolution fusion | flops 10895818752 | bytes 20054016 | tf_op jit(solution)/shard_map/dot_general | solution.py:567
  612.2 7.6 pick_pieces.7
  636.4 8.7 collective-permute-done.66
  646.5 7.5 collective-permute-done.71
  661.3 19.3 %collective-permute-done.83 = bf16[288,2304]{1,0:T(8,128)(2,1)} collective-permute-done((bf16[288,2304]{1,0:T(8,128)(2,1)}, bf16[288,2304]{1,0:T(8,128)(2,1)}, u32[]{:S(2)}, u32[]{:S(2)}) %collective-permute-start.83) | collective-permute-done | bytes 1327136 | tf_op jit(solution)/shard_map/ppermute | solution.py:46
  683.4 8.5 adam_units.3
  741.4 6.7 collective-permute-done.80.refs_2_
  753.7 19.6 %collective-permute-done.78 = bf16[2,1,512,256]{3,2,1,0:T(8,128)(2,1)S(1)} collective-permute-done((bf16[2,1,512,256]{3,2,1,0:T(8,128)(2,1)S(1)}, bf16[2,1,512,256]{3,2,1,0:T(8,128)(2,1)S(1)}, u32[]{:S(2)}, u32[]{:S(2)}) %collective-permute-start.78) | collective-permute-done | bytes 524320 | tf_op jit(solution)/shard_map/ppermute | solution.py:46
  775.3 6.9 convolution_convert_fusion.2
  787.8 5.3 convolution_convert_fusion.6
  793.3 8.7 collective-permute-done.88
  802.6 12.0 %collective-permute-done.85 = bf16[288,1024]{1,0:T(8,128)(2,1)S(1)} collective-permute-done((bf16[288,1024]{1,0:T(8,128)(2,1)S(1)}, bf16[288,1024]{1,0:T(8,128)(2,1)S(1)}, u32[]{:S(2)}, u32[]{:S(2)}) %collective-permute-start.85) | collective-permute-done | bytes 589856 | tf_op jit(solution)/shard_map/ppermute | solution.py:46
  815.9 13.5 %collective-permute-done.89 = bf16[288,2304]{1,0:T(8,128)(2,1)} collective-permute-done((bf16[288,2304]{1,0:T(8,128)(2,1)}, bf16[288,2304]{1,0:T(8,128)(2,1)}, u32[]{:S(2)}, u32[]{:S(2)}) %collective-permute-start.89) | collective-permute-done | bytes 1327136 | tf_op jit(solution)/shard_map/ppermute | solution.py:46
  835.3 17.3 %adam_units.2 = (f32[2,288,2304]{2,1,0:T(8,128)}, f32[2,288,2304]{2,1,0:T(8,128)}, f32[2,288,2304]{2,1,0:T(8,128)}, f32[2,288,2304]{2,1,0:T(8,128)}) custom-call(s32[1]{0:T(128)} %bitcast.23.own_ref, f32[288,2304]{1,0:T(8,128)S(1)} %convert_add_fusion.refs_0_, bf16[288,2304]{1,0:T(8,128)(2,1)S(1)} %collective-permute-done.108.refs_1_, ...), custom_call_target="tpu_custom_call" | custom-call | bytes 39813120 | tf_op jit(solution)/shard_map/adam_units/pallas_call | solution.py:508
  871.5 14.3 %collective-permute-start.106 = (bf16[64,2304]{1,0:T(8,128)(2,1)}, bf16[64,2304]{1,0:T(8,128)(2,1)}, u32[]{:S(2)}, u32[]{:S(2)}) collective-permute-start(bf16[64,2304]{1,0:T(8,128)(2,1)} %get-tuple-element.328), channel_id=1, source_target_pairs={{0,4},{12,8},{1,5},{13,9},{2,6},{14,10},{3,7},{15,11},{16,20},{28,... | collective-permute-start | bytes 884744 | tf_op jit(solution)/shard_map/ppermute | solution.py:46
  885.8 8.9 collective-permute-done.94
  928.0 11.3 %collective-permute-done.107 = bf16[64,2304]{1,0:T(8,128)(2,1)S(1)} collective-permute-done((bf16[64,2304]{1,0:T(8,128)(2,1)S(1)}, bf16[64,2304]{1,0:T(8,128)(2,1)S(1)}, u32[]{:S(2)}, u32[]{:S(2)}) %collective-permute-start.107) | collective-permute-done | bytes 294944 | tf_op jit(solution)/shard_map/ppermute | solution.py:46
  (701 shorter events, 383.5 us)
Async XLA Ops:
  30.4 29.6 %collective-permute-start.10 = (bf16[288,1024]{1,0:T(8,128)(2,1)S(1)}, bf16[288,1024]{1,0:T(8,128)(2,1)S(1)}, u32[]{:S(2)}, u32[]{:S(2)}) collective-permute-start(bf16[288,1024]{1,0:T(8,128)(2,1)S(1)} %join_rows.1.refs_0_), channel_id=1, source_target_pairs={{0,8},{4,12},{8,0},{12,4},{1,9},{5,13},{9,1},{13,5},{2,10},{6,14},... | collective-permute-start | bytes 1769480 | tf_op jit(solution)/shard_map/ppermute | solution.py:46
  36.9 60.7 %collective-permute-start.2 = (bf16[256,2304]{1,0:T(8,128)(2,1)}, bf16[256,2304]{1,0:T(8,128)(2,1)}, u32[]{:S(2)}, u32[]{:S(2)}) collective-permute-start(bf16[256,2304]{1,0:T(8,128)(2,1)} %pad_maximum_fusion.2), channel_id=1, source_target_pairs={{0,1},{1,0},{2,3},{3,2},{4,5},{5,4},{6,7},{7,6},{8,9},{9,8},{10,11... | collective-permute-start | bytes 3538952 | tf_op jit(solution)/shard_map/ppermute | solution.py:68
  38.1 44.9 %collective-permute-start.9 = (bf16[288,1024]{1,0:T(8,128)(2,1)S(1)}, bf16[288,1024]{1,0:T(8,128)(2,1)}, u32[]{:S(2)}, u32[]{:S(2)}) collective-permute-start(bf16[288,1024]{1,0:T(8,128)(2,1)S(1)} %collective-permute-done.8.refs_4_), channel_id=1, source_target_pairs={{0,16},{4,20},{8,24},{16,0},{20,4},{24,8},{1,17},{5,21},{9,25},{17... | collective-permute-start | bytes 1769480 | tf_op jit(solution)/shard_map/ppermute | solution.py:46
  63.3 30.5 %collective-permute-start.11 = (bf16[288,1024]{1,0:T(8,128)(2,1)S(1)}, bf16[288,1024]{1,0:T(8,128)(2,1)}, u32[]{:S(2)}, u32[]{:S(2)}) collective-permute-start(bf16[288,1024]{1,0:T(8,128)(2,1)S(1)} %collective-permute-done.10.refs_6_), channel_id=1, source_target_pairs={{0,16},{4,20},{8,24},{12,28},{16,0},{20,4},{24,8},{28,12},{1,17},{... | collective-permute-start | bytes 1769480 | tf_op jit(solution)/shard_map/ppermute | solution.py:46
  93.8 42.7 %collective-permute-start.24 = (bf16[64,2304]{1,0:T(8,128)(2,1)S(1)}, bf16[64,2304]{1,0:T(8,128)(2,1)S(1)}, u32[]{:S(2)}, u32[]{:S(2)}) collective-permute-start(bf16[64,2304]{1,0:T(8,128)(2,1)S(1)} %convert_element_type.496.refs_0_), channel_id=1, source_target_pairs={{0,16},{4,20},{8,24},{12,28},{16,0},{20,4},{24,8},{28,12},{1,17},{... | collective-permute-start | bytes 884744 | tf_op jit(solution)/shard_map/ppermute | solution.py:46
  110.1 68.7 %collective-permute-start.21 = (bf16[288,2304]{1,0:T(8,128)(2,1)}, bf16[288,2304]{1,0:T(8,128)(2,1)}, u32[]{:S(2)}, u32[]{:S(2)}) collective-permute-start(bf16[288,2304]{1,0:T(8,128)(2,1)} %get-tuple-element.208.refs_0_), channel_id=1, source_target_pairs={{0,8},{4,12},{8,0},{12,4},{1,9},{5,13},{9,1},{13,5},{2,10},{6,14},... | collective-permute-start | bytes 3981320 | tf_op jit(solution)/shard_map/ppermute | solution.py:46
  134.2 44.5 %collective-permute-start.20 = (bf16[2,1,512,256]{3,2,1,0:T(8,128)(2,1)}, bf16[2,1,512,256]{3,2,1,0:T(8,128)(2,1)}, u32[]{:S(2)}, u32[]{:S(2)}) collective-permute-start(bf16[2,1,512,256]{3,2,1,0:T(8,128)(2,1)} %pad_maximum_fusion.11), channel_id=1, source_target_pairs={{4,0},{8,4},{12,8},{5,1},{9,5},{13,9},{6,2},{10,6},{14,10},{7,3},{... | collective-permute-start | bytes 1572872 | tf_op jit(solution)/shard_map/ppermute | solution.py:46
  141.4 99.5 %collective-permute-start.37 = (bf16[288,2304]{1,0:T(8,128)(2,1)}, bf16[288,2304]{1,0:T(8,128)(2,1)}, u32[]{:S(2)}, u32[]{:S(2)}) collective-permute-start(bf16[288,2304]{1,0:T(8,128)(2,1)} %get-tuple-element.225), channel_id=1, source_target_pairs={{0,4},{4,0},{8,12},{12,8},{1,5},{5,1},{9,13},{13,9},{2,6},{6,2},{1... | collective-permute-start | bytes 3981320 | tf_op jit(solution)/shard_map/ppermute | solution.py:46
  146.9 34.4 %collective-permute-start.26 = (bf16[64,2304]{1,0:T(8,128)(2,1)S(1)}, bf16[64,2304]{1,0:T(8,128)(2,1)S(1)}, u32[]{:S(2)}, u32[]{:S(2)}) collective-permute-start(bf16[64,2304]{1,0:T(8,128)(2,1)S(1)} %copy-done.19), channel_id=1, source_target_pairs={{0,16},{4,20},{8,24},{12,28},{16,0},{20,4},{24,8},{28,12},{1,17},{... | collective-permute-start | bytes 884744 | tf_op jit(solution)/shard_map/ppermute | solution.py:46
  151.2 30.1 %collective-permute-start.27 = (bf16[64,2304]{1,0:T(8,128)(2,1)S(1)}, bf16[64,2304]{1,0:T(8,128)(2,1)S(1)}, u32[]{:S(2)}, u32[]{:S(2)}) collective-permute-start(bf16[64,2304]{1,0:T(8,128)(2,1)S(1)} %collective-permute-done.18.refs_8_), channel_id=1, source_target_pairs={{0,16},{12,28},{16,0},{28,12},{1,17},{13,29},{17,1},{29,13},{2,18}... | collective-permute-start | bytes 884744 | tf_op jit(solution)/shard_map/ppermute | solution.py:46
  206.7 34.3 %collective-permute-start.36 = (bf16[288,2304]{1,0:T(8,128)(2,1)}, bf16[288,2304]{1,0:T(8,128)(2,1)}, u32[]{:S(2)}, u32[]{:S(2)}) collective-permute-start(bf16[288,2304]{1,0:T(8,128)(2,1)} %collective-permute-done.21.refs_2_), channel_id=1, source_target_pairs={{0,16},{4,20},{8,24},{12,28},{16,0},{20,4},{24,8},{28,12},{1,17},{... | collective-permute-start | bytes 3981320 | tf_op jit(solution)/shard_map/ppermute | solution.py:46
  240.0 32.2 %collective-permute-start.35 = (bf16[288,2304]{1,0:T(8,128)(2,1)}, bf16[288,2304]{1,0:T(8,128)(2,1)}, u32[]{:S(2)}, u32[]{:S(2)}) collective-permute-start(bf16[288,2304]{1,0:T(8,128)(2,1)} %get-tuple-element.208.refs_0_), channel_id=1, source_target_pairs={{0,16},{4,20},{8,24},{12,28},{16,0},{20,4},{24,8},{28,12},{1,17},{... | collective-permute-start | bytes 3981320 | tf_op jit(solution)/shard_map/ppermute | solution.py:46
  240.9 60.0 %collective-permute-start.39 = (bf16[288,2304]{1,0:T(8,128)(2,1)}, bf16[288,2304]{1,0:T(8,128)(2,1)}, u32[]{:S(2)}, u32[]{:S(2)}) collective-permute-start(bf16[288,2304]{1,0:T(8,128)(2,1)} %collective-permute-done.37.refs_4_), channel_id=1, source_target_pairs={{0,8},{4,12},{8,0},{12,4},{1,9},{5,13},{9,1},{13,5},{2,10},{6,14},... | collective-permute-start | bytes 3981320 | tf_op jit(solution)/shard_map/ppermute | solution.py:46
  240.9 60.0 %collective-permute-start.40 = (bf16[288,1152]{1,0:T(8,128)(2,1)S(1)}, bf16[288,1152]{1,0:T(8,128)(2,1)}, u32[]{:S(2)}, u32[]{:S(2)}) collective-permute-start(bf16[288,1152]{1,0:T(8,128)(2,1)S(1)} %get-tuple-element.234.refs_0_), channel_id=1, source_target_pairs={{0,16},{4,20},{8,24},{12,28},{16,0},{20,4},{24,8},{28,12},{1,17},{... | collective-permute-start | bytes 1990664 | tf_op jit(solution)/shard_map/ppermute | solution.py:46
  246.0 56.1 %collective-permute-start.32 = (bf16[128,2304]{1,0:T(8,128)(2,1)}, bf16[128,2304]{1,0:T(8,128)(2,1)}, u32[]{:S(2)}, u32[]{:S(2)}) collective-permute-start(bf16[128,2304]{1,0:T(8,128)(2,1)} %slice.455), channel_id=1, source_target_pairs={{0,2},{1,3},{2,0},{3,1},{4,6},{5,7},{6,4},{7,5},{8,10},{9,11},{10,... | collective-permute-start | bytes 1769480 | tf_op jit(solution)/shard_map/ppermute | solution.py:46
  247.4 61.0 %collective-permute-start.42 = (bf16[288,1152]{1,0:T(8,128)(2,1)}, bf16[288,1152]{1,0:T(8,128)(2,1)}, u32[]{:S(2)}, u32[]{:S(2)}) collective-permute-start(bf16[288,1152]{1,0:T(8,128)(2,1)} %get-tuple-element.232), channel_id=1, source_target_pairs={{0,4},{4,0},{8,12},{12,8},{1,5},{5,1},{9,13},{13,9},{2,6},{6,2},{1... | collective-permute-start | bytes 1990664 | tf_op jit(solution)/shard_map/ppermute | solution.py:46
  272.3 42.6 %collective-permute-start.38 = (bf16[288,2304]{1,0:T(8,128)(2,1)}, bf16[288,2304]{1,0:T(8,128)(2,1)S(1)}, u32[]{:S(2)}, u32[]{:S(2)}) collective-permute-start(bf16[288,2304]{1,0:T(8,128)(2,1)} %collective-permute-done.37.refs_4_), channel_id=1, source_target_pairs={{0,16},{4,20},{8,24},{12,28},{16,0},{20,4},{24,8},{28,12},{1,17},{... | collective-permute-start | bytes 3981320 | tf_op jit(solution)/shard_map/ppermute | solution.py:46
  300.9 65.9 %collective-permute-start.41 = (bf16[288,2304]{1,0:T(8,128)(2,1)}, bf16[288,2304]{1,0:T(8,128)(2,1)S(1)}, u32[]{:S(2)}, u32[]{:S(2)}) collective-permute-start(bf16[288,2304]{1,0:T(8,128)(2,1)} %collective-permute-done.39.refs_6_), channel_id=1, source_target_pairs={{0,16},{4,20},{8,24},{12,28},{16,0},{20,4},{24,8},{28,12},{1,17},{... | collective-permute-start | bytes 3981320 | tf_op jit(solution)/shard_map/ppermute | solution.py:46
  308.4 44.3 %collective-permute-start.44 = (bf16[288,1152]{1,0:T(8,128)(2,1)S(1)}, bf16[288,1152]{1,0:T(8,128)(2,1)}, u32[]{:S(2)}, u32[]{:S(2)}) collective-permute-start(bf16[288,1152]{1,0:T(8,128)(2,1)S(1)} %get-tuple-element.234.refs_0_), channel_id=1, source_target_pairs={{0,8},{4,12},{8,0},{12,4},{1,9},{5,13},{9,1},{13,5},{2,10},{6,14},... | collective-permute-start | bytes 1990664 | tf_op jit(solution)/shard_map/ppermute | solution.py:46
  314.8 42.2 %collective-permute-start.43 = (bf16[288,1152]{1,0:T(8,128)(2,1)}, bf16[288,1152]{1,0:T(8,128)(2,1)S(1)}, u32[]{:S(2)}, u32[]{:S(2)}) collective-permute-start(bf16[288,1152]{1,0:T(8,128)(2,1)} %collective-permute-done.42.refs_2_), channel_id=1, source_target_pairs={{0,16},{4,20},{8,24},{12,28},{16,0},{20,4},{24,8},{28,12},{1,17},{... | collective-permute-start | bytes 1990664 | tf_op jit(solution)/shard_map/ppermute | solution.py:46
  315.7 51.2 %collective-permute-start.46 = (bf16[288,1152]{1,0:T(8,128)(2,1)}, bf16[288,1152]{1,0:T(8,128)(2,1)}, u32[]{:S(2)}, u32[]{:S(2)}) collective-permute-start(bf16[288,1152]{1,0:T(8,128)(2,1)} %collective-permute-done.42.refs_2_), channel_id=1, source_target_pairs={{0,8},{4,12},{8,0},{12,4},{1,9},{5,13},{9,1},{13,5},{2,10},{6,14},... | collective-permute-start | bytes 1990664 | tf_op jit(solution)/shard_map/ppermute | solution.py:46
  322.0 46.6 %collective-permute-start.49 = (bf16[128,2304]{1,0:T(8,128)(2,1)S(1)}, bf16[128,2304]{1,0:T(8,128)(2,1)}, u32[]{:S(2)}, u32[]{:S(2)}) collective-permute-start(bf16[128,2304]{1,0:T(8,128)(2,1)S(1)} %get-tuple-element.222), channel_id=1, source_target_pairs={{0,4},{4,0},{8,12},{12,8},{1,5},{5,1},{9,13},{13,9},{2,6},{6,2},{1... | collective-permute-start | bytes 1769480 | tf_op jit(solution)/shard_map/ppermute | solution.py:46
  352.7 43.6 %collective-permute-start.34 = (bf16[256,2304]{1,0:T(8,128)(2,1)}, bf16[256,2304]{1,0:T(8,128)(2,1)}, u32[]{:S(2)}, u32[]{:S(2)}) collective-permute-start(bf16[256,2304]{1,0:T(8,128)(2,1)} %pad_maximum_fusion.3), channel_id=1, source_target_pairs={{0,1},{1,0},{2,3},{3,2},{4,5},{5,4},{6,7},{7,6},{8,9},{9,8},{10,11... | collective-permute-start | bytes 3538952 | tf_op jit(solution)/shard_map/ppermute | solution.py:68
  517.1 44.5 %collective-permute-start.58 = (bf16[256,2304]{1,0:T(8,128)(2,1)}, bf16[256,2304]{1,0:T(8,128)(2,1)}, u32[]{:S(2)}, u32[]{:S(2)}) collective-permute-start(bf16[256,2304]{1,0:T(8,128)(2,1)} %slice.297), channel_id=1, source_target_pairs={{0,1},{1,0},{2,3},{3,2},{4,5},{5,4},{6,7},{7,6},{8,9},{9,8},{10,11... | collective-permute-start | bytes 3538952 | tf_op jit(solution)/shard_map/ppermute | solution.py:68
  560.4 31.1 %collective-permute-start.68 = (bf16[288,1152]{1,0:T(8,128)(2,1)S(1)}, bf16[288,1152]{1,0:T(8,128)(2,1)S(1)}, u32[]{:S(2)}, u32[]{:S(2)}) collective-permute-start(bf16[288,1152]{1,0:T(8,128)(2,1)S(1)} %get-tuple-element.256), channel_id=1, source_target_pairs={{0,16},{16,0},{1,17},{17,1},{2,18},{18,2},{3,19},{19,3},{4,20},{20... | collective-permute-start | bytes 1990664 | tf_op jit(solution)/shard_map/ppermute | solution.py:46
  564.0 58.8 %collective-permute-start.61 = (bf16[128,2304]{1,0:T(8,128)(2,1)}, bf16[128,2304]{1,0:T(8,128)(2,1)S(1)}, u32[]{:S(2)}, u32[]{:S(2)}) collective-permute-start(bf16[128,2304]{1,0:T(8,128)(2,1)} %slice.452), channel_id=1, source_target_pairs={{0,2},{1,3},{2,0},{3,1},{4,6},{5,7},{6,4},{7,5},{8,10},{9,11},{10,... | collective-permute-start | bytes 1769480 | tf_op jit(solution)/shard_map/ppermute | solution.py:46
  578.3 53.1 %collective-permute-start.82 = (bf16[288,1152]{1,0:T(8,128)(2,1)S(1)}, bf16[288,1152]{1,0:T(8,128)(2,1)}, u32[]{:S(2)}, u32[]{:S(2)}) collective-permute-start(bf16[288,1152]{1,0:T(8,128)(2,1)S(1)} %get-tuple-element.280), channel_id=1, source_target_pairs={{0,16},{16,0},{1,17},{17,1},{2,18},{18,2},{3,19},{19,3},{4,20},{20... | collective-permute-start | bytes 1990664 | tf_op jit(solution)/shard_map/ppermute | solution.py:46
  579.1 52.2 %collective-permute-start.76 = (bf16[288,1152]{1,0:T(8,128)(2,1)}, bf16[288,1152]{1,0:T(8,128)(2,1)}, u32[]{:S(2)}, u32[]{:S(2)}) collective-permute-start(bf16[288,1152]{1,0:T(8,128)(2,1)} %add_convert_fusion.4), channel_id=1, source_target_pairs={{0,8},{4,12},{8,0},{12,4},{1,9},{5,13},{9,1},{13,5},{2,10},{6,14},... | collective-permute-start | bytes 1990664 | tf_op jit(solution)/shard_map/ppermute | solution.py:46
  594.3 28.5 %collective-permute-start.65 = (bf16[128,2304]{1,0:T(8,128)(2,1)}, bf16[128,2304]{1,0:T(8,128)(2,1)S(1)}, u32[]{:S(2)}, u32[]{:S(2)}) collective-permute-start(bf16[128,2304]{1,0:T(8,128)(2,1)} %fusion.86), channel_id=1, source_target_pairs={{0,4},{4,0},{8,12},{12,8},{1,5},{5,1},{9,13},{13,9},{2,6},{6,2},{1... | collective-permute-start | bytes 1769480 | tf_op jit(solution)/shard_map/ppermute | solution.py:46
  619.8 35.9 %collective-permute-start.70 = (bf16[288,2304]{1,0:T(8,128)(2,1)}, bf16[288,2304]{1,0:T(8,128)(2,1)}, u32[]{:S(2)}, u32[]{:S(2)}) collective-permute-start(bf16[288,2304]{1,0:T(8,128)(2,1)} %get-tuple-element.258), channel_id=1, source_target_pairs={{0,16},{16,0},{1,17},{17,1},{2,18},{18,2},{3,19},{19,3},{4,20},{20... | collective-permute-start | bytes 3981320 | tf_op jit(solution)/shard_map/ppermute | solution.py:46
  622.8 31.3 %collective-permute-start.71 = (bf16[288,1152]{1,0:T(8,128)(2,1)}, bf16[288,1152]{1,0:T(8,128)(2,1)}, u32[]{:S(2)}, u32[]{:S(2)}) collective-permute-start(bf16[288,1152]{1,0:T(8,128)(2,1)} %add_convert_fusion.5), channel_id=1, source_target_pairs={{0,8},{4,12},{8,0},{12,4},{1,9},{5,13},{9,1},{13,5},{2,10},{6,14},... | collective-permute-start | bytes 1990664 | tf_op jit(solution)/shard_map/ppermute | solution.py:46
  633.9 46.7 %collective-permute-start.83 = (bf16[288,2304]{1,0:T(8,128)(2,1)}, bf16[288,2304]{1,0:T(8,128)(2,1)}, u32[]{:S(2)}, u32[]{:S(2)}) collective-permute-start(bf16[288,2304]{1,0:T(8,128)(2,1)} %get-tuple-element.281), channel_id=1, source_target_pairs={{0,16},{16,0},{1,17},{17,1},{2,18},{18,2},{3,19},{19,3},{4,20},{20... | collective-permute-start | bytes 3981320 | tf_op jit(solution)/shard_map/ppermute | solution.py:46
  646.5 45.4 %collective-permute-start.67 = (bf16[256,2304]{1,0:T(8,128)(2,1)S(1)}, bf16[256,2304]{1,0:T(8,128)(2,1)S(1)}, u32[]{:S(2)}, u32[]{:S(2)}) collective-permute-start(bf16[256,2304]{1,0:T(8,128)(2,1)S(1)} %pad_maximum_fusion.7), channel_id=1, source_target_pairs={{0,1},{1,0},{2,3},{3,2},{4,5},{5,4},{6,7},{7,6},{8,9},{9,8},{10,11... | collective-permute-start | bytes 3538952 | tf_op jit(solution)/shard_map/ppermute | solution.py:68
  658.6 74.9 %collective-permute-start.87 = (bf16[288,2304]{1,0:T(8,128)(2,1)}, bf16[288,2304]{1,0:T(8,128)(2,1)}, u32[]{:S(2)}, u32[]{:S(2)}) collective-permute-start(bf16[288,2304]{1,0:T(8,128)(2,1)} %get-tuple-element.288), channel_id=1, source_target_pairs={{0,16},{16,0},{1,17},{17,1},{2,18},{18,2},{3,19},{19,3},{4,20},{20... | collective-permute-start | bytes 3981320 | tf_op jit(solution)/shard_map/ppermute | solution.py:46
  659.5 71.0 %collective-permute-start.72 = (bf16[288,2304]{1,0:T(8,128)(2,1)}, bf16[288,2304]{1,0:T(8,128)(2,1)}, u32[]{:S(2)}, u32[]{:S(2)}) collective-permute-start(bf16[288,2304]{1,0:T(8,128)(2,1)} %add_convert_fusion.2), channel_id=1, source_target_pairs={{0,8},{4,12},{8,0},{12,4},{1,9},{5,13},{9,1},{13,5},{2,10},{6,14},... | collective-permute-start | bytes 3981320 | tf_op jit(solution)/shard_map/ppermute | solution.py:46
  735.3 38.0 %collective-permute-start.78 = (bf16[2,1,512,256]{3,2,1,0:T(8,128)(2,1)S(1)}, bf16[2,1,512,256]{3,2,1,0:T(8,128)(2,1)S(1)}, u32[]{:S(2)}, u32[]{:S(2)}) collective-permute-start(bf16[2,1,512,256]{3,2,1,0:T(8,128)(2,1)S(1)} %fusion.99), channel_id=1, source_target_pairs={{0,8},{4,12},{8,0},{12,4},{1,9},{5,13},{9,1},{13,5},{2,10},{6,14},... | collective-permute-start | bytes 1572872 | tf_op jit(solution)/shard_map/ppermute | solution.py:46
  748.1 37.6 %collective-permute-start.84 = (bf16[288,2304]{1,0:T(8,128)(2,1)}, bf16[288,2304]{1,0:T(8,128)(2,1)}, u32[]{:S(2)}, u32[]{:S(2)}) collective-permute-start(bf16[288,2304]{1,0:T(8,128)(2,1)} %get-tuple-element.282), channel_id=1, source_target_pairs={{0,16},{16,0},{1,17},{17,1},{2,18},{18,2},{3,19},{19,3},{4,20},{20... | collective-permute-start | bytes 3981320 | tf_op jit(solution)/shard_map/ppermute | solution.py:46
  749.3 84.4 %collective-permute-start.108 = (bf16[288,2304]{1,0:T(8,128)(2,1)}, bf16[288,2304]{1,0:T(8,128)(2,1)S(1)}, u32[]{:S(2)}, u32[]{:S(2)}) collective-permute-start(bf16[288,2304]{1,0:T(8,128)(2,1)} %add_convert_fusion), channel_id=1, source_target_pairs={{0,4},{4,0},{8,12},{12,8},{1,5},{5,1},{9,13},{13,9},{2,6},{6,2},{1... | collective-permute-start | bytes 3981320 | tf_op jit(solution)/shard_map/ppermute | solution.py:46
  752.2 77.2 %collective-permute-start.89 = (bf16[288,2304]{1,0:T(8,128)(2,1)}, bf16[288,2304]{1,0:T(8,128)(2,1)}, u32[]{:S(2)}, u32[]{:S(2)}) collective-permute-start(bf16[288,2304]{1,0:T(8,128)(2,1)} %add_convert_fusion.1), channel_id=1, source_target_pairs={{0,8},{4,12},{8,0},{12,4},{1,9},{5,13},{9,1},{13,5},{2,10},{6,14},... | collective-permute-start | bytes 3981320 | tf_op jit(solution)/shard_map/ppermute | solution.py:46
  793.2 64.3 %collective-permute-start.79 = (bf16[256,2304]{1,0:T(8,128)(2,1)S(1)}, bf16[256,2304]{1,0:T(8,128)(2,1)S(1)}, u32[]{:S(2)}, u32[]{:S(2)}) collective-permute-start(bf16[256,2304]{1,0:T(8,128)(2,1)S(1)} %slice.311), channel_id=1, source_target_pairs={{0,1},{1,0},{2,3},{3,2},{4,5},{5,4},{6,7},{7,6},{8,9},{9,8},{10,11... | collective-permute-start | bytes 3538952 | tf_op jit(solution)/shard_map/ppermute | solution.py:68
  802.0 50.6 %collective-permute-start.92 = (bf16[288,1024]{1,0:T(8,128)(2,1)S(1)}, bf16[288,1024]{1,0:T(8,128)(2,1)}, u32[]{:S(2)}, u32[]{:S(2)}) collective-permute-start(bf16[288,1024]{1,0:T(8,128)(2,1)S(1)} %get-tuple-element.297), channel_id=1, source_target_pairs={{0,16},{16,0},{1,17},{17,1},{2,18},{18,2},{3,19},{19,3},{4,20},{20... | collective-permute-start | bytes 1769480 | tf_op jit(solution)/shard_map/ppermute | solution.py:46
  815.2 38.7 %collective-permute-start.86 = (bf16[288,1024]{1,0:T(8,128)(2,1)S(1)}, bf16[288,1024]{1,0:T(8,128)(2,1)S(1)}, u32[]{:S(2)}, u32[]{:S(2)}) collective-permute-start(bf16[288,1024]{1,0:T(8,128)(2,1)S(1)} %get-tuple-element.284), channel_id=1, source_target_pairs={{0,16},{16,0},{1,17},{17,1},{2,18},{18,2},{3,19},{19,3},{4,20},{20... | collective-permute-start | bytes 1769480 | tf_op jit(solution)/shard_map/ppermute | solution.py:46
  833.7 36.3 %collective-permute-start.90 = (bf16[288,1024]{1,0:T(8,128)(2,1)S(1)}, bf16[288,1024]{1,0:T(8,128)(2,1)S(1)}, u32[]{:S(2)}, u32[]{:S(2)}) collective-permute-start(bf16[288,1024]{1,0:T(8,128)(2,1)S(1)} %get-tuple-element.293), channel_id=1, source_target_pairs={{0,4},{4,8},{8,12},{1,5},{5,9},{9,13},{2,6},{6,10},{10,14},{3,7},{... | collective-permute-start | bytes 1769480 | tf_op jit(solution)/shard_map/ppermute | solution.py:46
  857.5 37.2 %collective-permute-start.94 = (bf16[288,1024]{1,0:T(8,128)(2,1)S(1)}, bf16[288,1024]{1,0:T(8,128)(2,1)S(1)}, u32[]{:S(2)}, u32[]{:S(2)}) collective-permute-start(bf16[288,1024]{1,0:T(8,128)(2,1)S(1)} %add_convert_fusion.6), channel_id=1, source_target_pairs={{0,8},{4,12},{8,0},{12,4},{1,9},{5,13},{9,1},{13,5},{2,10},{6,14},... | collective-permute-start | bytes 1769480 | tf_op jit(solution)/shard_map/ppermute | solution.py:46
  863.9 34.2 %collective-permute-start.81 = (bf16[128,2304]{1,0:T(8,128)(2,1)S(1)}, bf16[128,2304]{1,0:T(8,128)(2,1)S(1)}, u32[]{:S(2)}, u32[]{:S(2)}) collective-permute-start(bf16[128,2304]{1,0:T(8,128)(2,1)S(1)} %slice.450), channel_id=1, source_target_pairs={{0,2},{1,3},{2,0},{3,1},{4,6},{5,7},{6,4},{7,5},{8,10},{9,11},{10,... | collective-permute-start | bytes 1769480 | tf_op jit(solution)/shard_map/ppermute | solution.py:46
  868.4 47.6 %collective-permute-start.105 = (bf16[64,2304]{1,0:T(8,128)(2,1)}, bf16[64,2304]{1,0:T(8,128)(2,1)}, u32[]{:S(2)}, u32[]{:S(2)}) collective-permute-start(bf16[64,2304]{1,0:T(8,128)(2,1)} %get-tuple-element.327), channel_id=1, source_target_pairs={{0,16},{16,0},{1,17},{17,1},{2,18},{18,2},{3,19},{19,3},{4,20},{20... | collective-permute-start | bytes 884744 | tf_op jit(solution)/shard_map/ppermute | solution.py:46
  870.0 56.9 %collective-permute-start.101 = (bf16[64,2304]{1,0:T(8,128)(2,1)}, bf16[64,2304]{1,0:T(8,128)(2,1)}, u32[]{:S(2)}, u32[]{:S(2)}) collective-permute-start(bf16[64,2304]{1,0:T(8,128)(2,1)} %get-tuple-element.318), channel_id=1, source_target_pairs={{0,16},{16,0},{1,17},{17,1},{2,18},{18,2},{3,19},{19,3},{4,20},{20... | collective-permute-start | bytes 884744 | tf_op jit(solution)/shard_map/ppermute | solution.py:46
  871.5 45.9 %collective-permute-start.106 = (bf16[64,2304]{1,0:T(8,128)(2,1)}, bf16[64,2304]{1,0:T(8,128)(2,1)}, u32[]{:S(2)}, u32[]{:S(2)}) collective-permute-start(bf16[64,2304]{1,0:T(8,128)(2,1)} %get-tuple-element.328), channel_id=1, source_target_pairs={{0,4},{12,8},{1,5},{13,9},{2,6},{14,10},{3,7},{15,11},{16,20},{28,... | collective-permute-start | bytes 884744 | tf_op jit(solution)/shard_map/ppermute | solution.py:46
  (226 other events, 3284.5 us)

commit v4 on v3

--- a/solution.py
+++ b/solution.py
@@ -793,7 +793,7 @@
     other = head_reduce(lines, grad_second_parts[1]).astype(BF16)
     other_came = lines.head.came[-1] if size_h > 1 else ()
     other = swap_ctx(lines, other, 1)
-    own = head_reduce(lines, grad_second_parts[0])
+    own = head_reduce(lines, after(grad_second_parts[0], *other_came))
     down_rows = after(jnp.concatenate(grad_slots), grad_second_parts[1])
     down_term = matmul_tn(down_rows, jnp.concatenate(hidden_slots)).astype(BF16)
     down_back = units_back(lines, down_term.reshape(size_x * size_z, ff_rows, ff_cols))

time: 953 us -> 946 us (level)
    unnamed x332 -> x330, local copies, waits for them, and re-layouts: 28.2 us -> 36.1 us
  transfers between devices with their start and end apart: 112 -> 112, of which waited for: 48 -> 47; matrix products, arithmetic and copies ran while one was open for 25% -> 24% of each run, Pallas kernels for 8% -> 9%
where the time goes in v4:
time: 946 us; the launch traced here: 935 us
  waiting for transfers between devices  421 us (45%)
  starting transfers between devices  149 us (16%)
  matrix products  134 us (14%)
  other arithmetic  87.2 us (9%)
  Pallas kernels  79.7 us (8%)
  local copies, waits for them, and re-layouts  59.5 us (6%)
    ppermute x94, waiting for transfers between devices, send(): lax.ppermute(one, axes, pairs)  416 us
    ppermute x94, starting transfers between devices, send(): lax.ppermute(one, axes, pairs)  138 us
    dot_general x6, matrix products, matmul(): return jnp.dot(left, right, preferred_element_type=F32)  44.6 us
    unnamed x330, local copies, waits for them, and re-layouts  36.1 us
    dot_general x4, matrix products, matmul_tn(): lax.dot_general(left, right, (((0,), (0,)), ((), ())), preferred_element_...  36 us
    dot_general x6, matrix products, matmul_nt(): lax.dot_general(left, right, (((1,), (1,)), ((), ())), preferred_element_...  33.9 us
    pallas_call x2, Pallas kernels, adam_units(): pl.pallas_call(kernel, grid=(rows // block,), out_shape=[jax.ShapeDtypeSt...  25.8 us
    pallas_call x6, Pallas kernels, place(): pl.pallas_call(kernel, out_shape=jax.ShapeDtypeStruct(shape, pieces[0].dt...  23.3 us
  transfers between devices with their start and end apart: 112, of which 47 were waited for; matrix products, arithmetic and copies ran while one was open for 24% of the time, Pallas kernels for 9%

profile of v4, /device:TPU:0, one launch (start us, length us, event | category | flops | bytes accessed | tf_op | source)
XLA Modules:
  0.0 934.8 jit_solution(3154854280251258142)
XLA Ops:
  20.9 8.3 collective-permute-done.8.refs_4_
  41.7 18.3 %collective-permute-done.10.refs_6_ = bf16[288,1024]{1,0:T(8,128)(2,1)S(1)} collective-permute-done((bf16[288,1024]{1,0:T(8,128)(2,1)S(1)}, bf16[288,1024]{1,0:T(8,128)(2,1)S(1)}, u32[]{:S(2)}, u32[]{:S(2)}) %collective-permute-start.10) | collective-permute-done | bytes 589856 | tf_op jit(solution)/shard_map/ppermute | solution.py:46
  65.4 7.1 all-to-all-start
  74.2 5.0 split_units.2
  99.7 10.3 %collective-permute-done.16.refs_6_ = bf16[64,2304]{1,0:T(8,128)(2,1)S(1)} collective-permute-done((bf16[64,2304]{1,0:T(8,128)(2,1)S(1)}, bf16[64,2304]{1,0:T(8,128)(2,1)S(1)}, u32[]{:S(2)}, u32[]{:S(2)}) %collective-permute-start.16) | collective-permute-done | bytes 294944 | tf_op jit(solution)/shard_map/ppermute | solution.py:46
  115.6 5.7 fusion.158
  124.9 7.2 collective-permute-done.18.refs_8_
  153.6 25.0 %collective-permute-done.20 = bf16[2,1,512,256]{3,2,1,0:T(8,128)(2,1)} collective-permute-done((bf16[2,1,512,256]{3,2,1,0:T(8,128)(2,1)}, bf16[2,1,512,256]{3,2,1,0:T(8,128)(2,1)}, u32[]{:S(2)}, u32[]{:S(2)}) %collective-permute-start.20) | collective-permute-done | bytes 524320 | tf_op jit(solution)/shard_map/ppermute | solution.py:46
  187.7 16.0 %collective-permute-done.22 = bf16[2,1,512,256]{3,2,1,0:T(8,128)(2,1)S(1)} collective-permute-done((bf16[2,1,512,256]{3,2,1,0:T(8,128)(2,1)}, bf16[2,1,512,256]{3,2,1,0:T(8,128)(2,1)S(1)}, u32[]{:S(2)}, u32[]{:S(2)}) %collective-permute-start.22) | collective-permute-done | bytes 524320 | tf_op jit(solution)/shard_map/ppermute | solution.py:46
  214.1 12.6 %collective-permute-done.23 = bf16[2,1,512,256]{3,2,1,0:T(8,128)(2,1)S(1)} collective-permute-done((bf16[2,1,512,256]{3,2,1,0:T(8,128)(2,1)S(1)}, bf16[2,1,512,256]{3,2,1,0:T(8,128)(2,1)S(1)}, u32[]{:S(2)}, u32[]{:S(2)}) %collective-permute-start.23) | collective-permute-done | bytes 524320 | tf_op jit(solution)/shard_map/ppermute | solution.py:46
  248.5 24.0 %collective-permute-done.35.refs_1_ = bf16[288,2304]{1,0:T(8,128)(2,1)} collective-permute-done((bf16[288,2304]{1,0:T(8,128)(2,1)}, bf16[288,2304]{1,0:T(8,128)(2,1)}, u32[]{:S(2)}, u32[]{:S(2)}) %collective-permute-start.35) | collective-permute-done | bytes 1327136 | tf_op jit(solution)/shard_map/ppermute | solution.py:46
  273.3 27.8 %collective-permute-done.39.refs_6_ = bf16[288,2304]{1,0:T(8,128)(2,1)} collective-permute-done((bf16[288,2304]{1,0:T(8,128)(2,1)}, bf16[288,2304]{1,0:T(8,128)(2,1)}, u32[]{:S(2)}, u32[]{:S(2)}) %collective-permute-start.39) | collective-permute-done | bytes 1327136 | tf_op jit(solution)/shard_map/ppermute | solution.py:46
  308.8 6.2 collective-permute-done.38.refs_5_
  315.9 6.4 collective-permute-done.33
  323.4 29.6 %collective-permute-done.44.refs_4_ = bf16[288,1152]{1,0:T(8,128)(2,1)} collective-permute-done((bf16[288,1152]{1,0:T(8,128)(2,1)S(1)}, bf16[288,1152]{1,0:T(8,128)(2,1)}, u32[]{:S(2)}, u32[]{:S(2)}) %collective-permute-start.44) | collective-permute-done | bytes 663584 | tf_op jit(solution)/shard_map/ppermute | solution.py:46
  358.9 8.2 collective-permute-done.46.refs_6_
  369.8 8.7 place.9
  378.4 10.8 %collective-permute-done.47.refs_7_ = bf16[288,1152]{1,0:T(8,128)(2,1)} collective-permute-done((bf16[288,1152]{1,0:T(8,128)(2,1)}, bf16[288,1152]{1,0:T(8,128)(2,1)}, u32[]{:S(2)}, u32[]{:S(2)}) %collective-permute-start.47) | collective-permute-done | bytes 663584 | tf_op jit(solution)/shard_map/ppermute | solution.py:46
  389.2 5.6 place.10
  396.5 9.5 %fusion.24 = f32[512,2304]{1,0:T(8,128)S(1)} fusion(bf16[2304,2304]{1,0:T(8,128)(2,1)} %bitcast.220, bf16[256,2304]{1,0:T(8,128)(2,1)} %collective-permute-done.34, bf16[128,2304]{1,0:T(8,128)(2,1)S(1)} %copy-done.49, bf16[128,2304]{1,0:T(8,128)(2,1)S(1)} %copy-done.53), kind=kOutput, calls=%fused_computation.45 | convolution fusion | flops 5442895872 | bytes 17694720 | tf_op jit(solution)/shard_map/dot_general | solution.py:559
  406.1 8.1 fusion.30
  431.6 11.2 %collective-permute-done.54 = bf16[128,2304]{1,0:T(8,128)(2,1)S(1)} collective-permute-done((bf16[128,2304]{1,0:T(8,128)(2,1)S(1)}, bf16[128,2304]{1,0:T(8,128)(2,1)S(1)}, u32[]{:S(2)}, u32[]{:S(2)}) %collective-permute-start.54) | collective-permute-done | bytes 589856 | tf_op jit(solution)/shard_map/ppermute | solution.py:46
  446.6 8.3 collective-permute-done.51
  466.9 8.7 collective-permute-done.56
  484.4 9.6 %collective-permute-done.59 = bf16[128,2304]{1,0:T(8,128)(2,1)} collective-permute-done((bf16[128,2304]{1,0:T(8,128)(2,1)}, bf16[128,2304]{1,0:T(8,128)(2,1)}, u32[]{:S(2)}, u32[]{:S(2)}) %collective-permute-start.59) | collective-permute-done | bytes 589856 | tf_op jit(solution)/shard_map/ppermute | solution.py:46
  502.7 10.3 %fusion.16 = (bf16[512,1152]{1,0:T(8,128)(2,1)}, bf16[512,1152]{1,0:T(8,128)(2,1)}) fusion(f32[512,2304]{1,0:T(8,128)} %copy-done.33, bf16[2304,1152]{1,0:T(8,128)(2,1)} %bitcast.229, bf16[256,2304]{1,0:T(8,128)(2,1)} %collective-permute-done.57, bf16[128,2304]{1,0:T(8,128)(2,1)S(1)} %copy-done.51, bf16[128,2304]{1,0:T(8,128)(2,1)S(1)} %copy-done.56), kind=kOutput, calls=%fused_computation.36 | convolution fusion | flops 2739142656 | bytes 14745600 | tf_op jit(solution)/shard_map/dot_general | solution.py:559
  513.1 7.7 fusion.23
  520.8 8.4 convolution_convert_fusion.7
  532.3 9.8 %convolution_convert_fusion.1 = bf16[2304,1152]{1,0:T(8,128)(2,1)} fusion(bf16[1024,2304]{1,0:T(8,128)(2,1)} %constant_dynamic-update-slice_fusion.6, bf16[512,1152]{1,0:T(8,128)(2,1)S(1)} %copy-done.83, bf16[512,1152]{1,0:T(8,128)(2,1)S(1)} %copy-done.85), kind=kOutput, calls=%fused_computation.1 | convolution fusion | flops 5443190784 | bytes 12386304 | tf_op jit(solution)/shard_map/dot_general | solution.py:567
  550.7 10.3 %convolution_convert_fusion.8 = bf16[512,2304]{1,0:T(8,128)(2,1)S(1)} fusion(bf16[2304,2304]{1,0:T(8,128)(2,1)} %bitcast.221, bf16[512,1152]{1,0:T(8,128)(2,1)} %get-tuple-element.385, bf16[512,1152]{1,0:T(8,128)(2,1)} %get-tuple-element.384), kind=kOutput, calls=%fused_computation.20 | convolution fusion | flops 5441716224 | bytes 15335424 | tf_op jit(solution)/shard_map/dot_general | solution.py:563
  568.0 10.7 %collective-permute-done.68 = bf16[288,1152]{1,0:T(8,128)(2,1)} collective-permute-done((bf16[288,1152]{1,0:T(8,128)(2,1)S(1)}, bf16[288,1152]{1,0:T(8,128)(2,1)}, u32[]{:S(2)}, u32[]{:S(2)}) %collective-permute-start.68) | collective-permute-done | bytes 663584 | tf_op jit(solution)/shard_map/ppermute | solution.py:46
  587.1 16.6 %convolution_convert_fusion = bf16[2304,2304]{1,0:T(8,128)(2,1)} fusion(bf16[1024,2304]{1,0:T(8,128)(2,1)} %copy-done.110, bf16[512,1152]{1,0:T(8,128)(2,1)} %get-tuple-element.387, bf16[512,1152]{1,0:T(8,128)(2,1)} %get-tuple-element.386, bf16[512,1152]{1,0:T(8,128)(2,1)S(1)} %copy-done.147, bf16[512,1152]{1,0:T(8,128)(2,1)S(1)} %copy-done.146), kind=kOutput, calls=%fused_computation | convolution fusion | flops 10895818752 | bytes 20054016 | tf_op jit(solution)/shard_map/dot_general | solution.py:567
  603.8 7.1 pick_pieces.7
  623.6 20.4 %collective-permute-done.71 = bf16[288,1152]{1,0:T(8,128)(2,1)S(1)} collective-permute-done((bf16[288,1152]{1,0:T(8,128)(2,1)}, bf16[288,1152]{1,0:T(8,128)(2,1)S(1)}, u32[]{:S(2)}, u32[]{:S(2)}) %collective-permute-start.71) | collective-permute-done | bytes 663584 | tf_op jit(solution)/shard_map/ppermute | solution.py:46
  651.5 19.8 %collective-permute-done.83 = bf16[288,2304]{1,0:T(8,128)(2,1)S(1)} collective-permute-done((bf16[288,2304]{1,0:T(8,128)(2,1)S(1)}, bf16[288,2304]{1,0:T(8,128)(2,1)S(1)}, u32[]{:S(2)}, u32[]{:S(2)}) %collective-permute-start.83) | collective-permute-done | bytes 1327136 | tf_op jit(solution)/shard_map/ppermute | solution.py:46
  676.8 8.5 adam_units.3
  731.3 19.6 %collective-permute-done.78 = bf16[2,1,512,256]{3,2,1,0:T(8,128)(2,1)} collective-permute-done((bf16[2,1,512,256]{3,2,1,0:T(8,128)(2,1)}, bf16[2,1,512,256]{3,2,1,0:T(8,128)(2,1)}, u32[]{:S(2)}, u32[]{:S(2)}) %collective-permute-start.78) | collective-permute-done | bytes 524320 | tf_op jit(solution)/shard_map/ppermute | solution.py:46
  757.3 7.0 convolution_convert_fusion.2
  776.2 7.8 collective-permute-done.88
  785.3 11.5 %collective-permute-done.85 = bf16[288,1024]{1,0:T(8,128)(2,1)} collective-permute-done((bf16[288,1024]{1,0:T(8,128)(2,1)S(1)}, bf16[288,1024]{1,0:T(8,128)(2,1)}, u32[]{:S(2)}, u32[]{:S(2)}) %collective-permute-start.85) | collective-permute-done | bytes 589856 | tf_op jit(solution)/shard_map/ppermute | solution.py:46
  798.1 5.3 convolution_convert_fusion.6
  811.4 10.1 %collective-permute-done.86 = bf16[288,1024]{1,0:T(8,128)(2,1)S(1)} collective-permute-done((bf16[288,1024]{1,0:T(8,128)(2,1)S(1)}, bf16[288,1024]{1,0:T(8,128)(2,1)S(1)}, u32[]{:S(2)}, u32[]{:S(2)}) %collective-permute-start.86) | collective-permute-done | bytes 589856 | tf_op jit(solution)/shard_map/ppermute | solution.py:46
  834.4 17.3 %adam_units.2 = (f32[2,288,2304]{2,1,0:T(8,128)}, f32[2,288,2304]{2,1,0:T(8,128)}, f32[2,288,2304]{2,1,0:T(8,128)}, f32[2,288,2304]{2,1,0:T(8,128)}) custom-call(s32[1]{0:T(128)} %bitcast.23.own_ref, f32[288,2304]{1,0:T(8,128)S(1)} %convert_add_fusion.refs_0_, bf16[288,2304]{1,0:T(8,128)(2,1)S(1)} %collective-permute-done.108.refs_1_, ...), custom_call_target="tpu_custom_call" | custom-call | bytes 39813120 | tf_op jit(solution)/shard_map/adam_units/pallas_call | solution.py:508
  860.0 8.6 collective-permute-done.91
  868.6 15.3 %collective-permute-start.106 = (bf16[64,2304]{1,0:T(8,128)(2,1)S(1)}, bf16[64,2304]{1,0:T(8,128)(2,1)S(1)}, u32[]{:S(2)}, u32[]{:S(2)}) collective-permute-start(bf16[64,2304]{1,0:T(8,128)(2,1)S(1)} %get-tuple-element.330), channel_id=1, source_target_pairs={{0,4},{12,8},{1,5},{13,9},{2,6},{14,10},{3,7},{15,11},{16,20},{28,... | collective-permute-start | bytes 884744 | tf_op jit(solution)/shard_map/ppermute | solution.py:46
  886.3 4.9 collective-permute-done.106
  892.7 5.0 collective-permute-done.94
  921.7 4.9 collective-permute-done.98
  (700 shorter events, 385.8 us)
Async XLA Ops:
  30.4 29.6 %collective-permute-start.10 = (bf16[288,1024]{1,0:T(8,128)(2,1)S(1)}, bf16[288,1024]{1,0:T(8,128)(2,1)S(1)}, u32[]{:S(2)}, u32[]{:S(2)}) collective-permute-start(bf16[288,1024]{1,0:T(8,128)(2,1)S(1)} %join_rows.1.refs_0_), channel_id=1, source_target_pairs={{0,8},{4,12},{8,0},{12,4},{1,9},{5,13},{9,1},{13,5},{2,10},{6,14},... | collective-permute-start | bytes 1769480 | tf_op jit(solution)/shard_map/ppermute | solution.py:46
  37.1 60.5 %collective-permute-start.2 = (bf16[256,2304]{1,0:T(8,128)(2,1)}, bf16[256,2304]{1,0:T(8,128)(2,1)}, u32[]{:S(2)}, u32[]{:S(2)}) collective-permute-start(bf16[256,2304]{1,0:T(8,128)(2,1)} %pad_maximum_fusion.2), channel_id=1, source_target_pairs={{0,1},{1,0},{2,3},{3,2},{4,5},{5,4},{6,7},{7,6},{8,9},{9,8},{10,11... | collective-permute-start | bytes 3538952 | tf_op jit(solution)/shard_map/ppermute | solution.py:68
  38.3 44.6 %collective-permute-start.9 = (bf16[288,1024]{1,0:T(8,128)(2,1)S(1)}, bf16[288,1024]{1,0:T(8,128)(2,1)}, u32[]{:S(2)}, u32[]{:S(2)}) collective-permute-start(bf16[288,1024]{1,0:T(8,128)(2,1)S(1)} %collective-permute-done.8.refs_4_), channel_id=1, source_target_pairs={{0,16},{4,20},{8,24},{16,0},{20,4},{24,8},{1,17},{5,21},{9,25},{17... | collective-permute-start | bytes 1769480 | tf_op jit(solution)/shard_map/ppermute | solution.py:46
  63.3 30.4 %collective-permute-start.11 = (bf16[288,1024]{1,0:T(8,128)(2,1)S(1)}, bf16[288,1024]{1,0:T(8,128)(2,1)}, u32[]{:S(2)}, u32[]{:S(2)}) collective-permute-start(bf16[288,1024]{1,0:T(8,128)(2,1)S(1)} %collective-permute-done.10.refs_6_), channel_id=1, source_target_pairs={{0,16},{4,20},{8,24},{12,28},{16,0},{20,4},{24,8},{28,12},{1,17},{... | collective-permute-start | bytes 1769480 | tf_op jit(solution)/shard_map/ppermute | solution.py:46
  93.7 42.9 %collective-permute-start.24 = (bf16[64,2304]{1,0:T(8,128)(2,1)S(1)}, bf16[64,2304]{1,0:T(8,128)(2,1)S(1)}, u32[]{:S(2)}, u32[]{:S(2)}) collective-permute-start(bf16[64,2304]{1,0:T(8,128)(2,1)S(1)} %convert_element_type.496.refs_0_), channel_id=1, source_target_pairs={{0,16},{4,20},{8,24},{12,28},{16,0},{20,4},{24,8},{28,12},{1,17},{... | collective-permute-start | bytes 884744 | tf_op jit(solution)/shard_map/ppermute | solution.py:46
  110.0 68.7 %collective-permute-start.21 = (bf16[288,2304]{1,0:T(8,128)(2,1)}, bf16[288,2304]{1,0:T(8,128)(2,1)}, u32[]{:S(2)}, u32[]{:S(2)}) collective-permute-start(bf16[288,2304]{1,0:T(8,128)(2,1)} %get-tuple-element.209.refs_0_), channel_id=1, source_target_pairs={{0,8},{4,12},{8,0},{12,4},{1,9},{5,13},{9,1},{13,5},{2,10},{6,14},... | collective-permute-start | bytes 3981320 | tf_op jit(solution)/shard_map/ppermute | solution.py:46
  134.3 44.3 %collective-permute-start.20 = (bf16[2,1,512,256]{3,2,1,0:T(8,128)(2,1)}, bf16[2,1,512,256]{3,2,1,0:T(8,128)(2,1)}, u32[]{:S(2)}, u32[]{:S(2)}) collective-permute-start(bf16[2,1,512,256]{3,2,1,0:T(8,128)(2,1)} %pad_maximum_fusion.11), channel_id=1, source_target_pairs={{4,0},{8,4},{12,8},{5,1},{9,5},{13,9},{6,2},{10,6},{14,10},{7,3},{... | collective-permute-start | bytes 1572872 | tf_op jit(solution)/shard_map/ppermute | solution.py:46
  141.5 99.6 %collective-permute-start.37 = (bf16[288,2304]{1,0:T(8,128)(2,1)}, bf16[288,2304]{1,0:T(8,128)(2,1)}, u32[]{:S(2)}, u32[]{:S(2)}) collective-permute-start(bf16[288,2304]{1,0:T(8,128)(2,1)} %get-tuple-element.226), channel_id=1, source_target_pairs={{0,4},{4,0},{8,12},{12,8},{1,5},{5,1},{9,13},{13,9},{2,6},{6,2},{1... | collective-permute-start | bytes 3981320 | tf_op jit(solution)/shard_map/ppermute | solution.py:46
  147.0 34.2 %collective-permute-start.26 = (bf16[64,2304]{1,0:T(8,128)(2,1)S(1)}, bf16[64,2304]{1,0:T(8,128)(2,1)S(1)}, u32[]{:S(2)}, u32[]{:S(2)}) collective-permute-start(bf16[64,2304]{1,0:T(8,128)(2,1)S(1)} %copy-done.15), channel_id=1, source_target_pairs={{0,16},{4,20},{8,24},{12,28},{16,0},{20,4},{24,8},{28,12},{1,17},{... | collective-permute-start | bytes 884744 | tf_op jit(solution)/shard_map/ppermute | solution.py:46
  151.1 30.1 %collective-permute-start.27 = (bf16[64,2304]{1,0:T(8,128)(2,1)S(1)}, bf16[64,2304]{1,0:T(8,128)(2,1)S(1)}, u32[]{:S(2)}, u32[]{:S(2)}) collective-permute-start(bf16[64,2304]{1,0:T(8,128)(2,1)S(1)} %collective-permute-done.18.refs_8_), channel_id=1, source_target_pairs={{0,16},{12,28},{16,0},{28,12},{1,17},{13,29},{17,1},{29,13},{2,18}... | collective-permute-start | bytes 884744 | tf_op jit(solution)/shard_map/ppermute | solution.py:46
  206.7 34.4 %collective-permute-start.36 = (bf16[288,2304]{1,0:T(8,128)(2,1)}, bf16[288,2304]{1,0:T(8,128)(2,1)}, u32[]{:S(2)}, u32[]{:S(2)}) collective-permute-start(bf16[288,2304]{1,0:T(8,128)(2,1)} %collective-permute-done.21.refs_2_), channel_id=1, source_target_pairs={{0,16},{4,20},{8,24},{12,28},{16,0},{20,4},{24,8},{28,12},{1,17},{... | collective-permute-start | bytes 3981320 | tf_op jit(solution)/shard_map/ppermute | solution.py:46
  240.2 32.2 %collective-permute-start.35 = (bf16[288,2304]{1,0:T(8,128)(2,1)}, bf16[288,2304]{1,0:T(8,128)(2,1)}, u32[]{:S(2)}, u32[]{:S(2)}) collective-permute-start(bf16[288,2304]{1,0:T(8,128)(2,1)} %get-tuple-element.209.refs_0_), channel_id=1, source_target_pairs={{0,16},{4,20},{8,24},{12,28},{16,0},{20,4},{24,8},{28,12},{1,17},{... | collective-permute-start | bytes 3981320 | tf_op jit(solution)/shard_map/ppermute | solution.py:46
  241.1 60.0 %collective-permute-start.39 = (bf16[288,2304]{1,0:T(8,128)(2,1)}, bf16[288,2304]{1,0:T(8,128)(2,1)}, u32[]{:S(2)}, u32[]{:S(2)}) collective-permute-start(bf16[288,2304]{1,0:T(8,128)(2,1)} %collective-permute-done.37.refs_4_), channel_id=1, source_target_pairs={{0,8},{4,12},{8,0},{12,4},{1,9},{5,13},{9,1},{13,5},{2,10},{6,14},... | collective-permute-start | bytes 3981320 | tf_op jit(solution)/shard_map/ppermute | solution.py:46
  241.1 60.0 %collective-permute-start.40 = (bf16[288,1152]{1,0:T(8,128)(2,1)S(1)}, bf16[288,1152]{1,0:T(8,128)(2,1)}, u32[]{:S(2)}, u32[]{:S(2)}) collective-permute-start(bf16[288,1152]{1,0:T(8,128)(2,1)S(1)} %get-tuple-element.235.refs_0_), channel_id=1, source_target_pairs={{0,16},{4,20},{8,24},{12,28},{16,0},{20,4},{24,8},{28,12},{1,17},{... | collective-permute-start | bytes 1990664 | tf_op jit(solution)/shard_map/ppermute | solution.py:46
  246.1 56.1 %collective-permute-start.32 = (bf16[128,2304]{1,0:T(8,128)(2,1)}, bf16[128,2304]{1,0:T(8,128)(2,1)}, u32[]{:S(2)}, u32[]{:S(2)}) collective-permute-start(bf16[128,2304]{1,0:T(8,128)(2,1)} %slice.453), channel_id=1, source_target_pairs={{0,2},{1,3},{2,0},{3,1},{4,6},{5,7},{6,4},{7,5},{8,10},{9,11},{10,... | collective-permute-start | bytes 1769480 | tf_op jit(solution)/shard_map/ppermute | solution.py:46
  247.6 61.1 %collective-permute-start.42 = (bf16[288,1152]{1,0:T(8,128)(2,1)}, bf16[288,1152]{1,0:T(8,128)(2,1)}, u32[]{:S(2)}, u32[]{:S(2)}) collective-permute-start(bf16[288,1152]{1,0:T(8,128)(2,1)} %get-tuple-element.233), channel_id=1, source_target_pairs={{0,4},{4,0},{8,12},{12,8},{1,5},{5,1},{9,13},{13,9},{2,6},{6,2},{1... | collective-permute-start | bytes 1990664 | tf_op jit(solution)/shard_map/ppermute | solution.py:46
  272.5 42.6 %collective-permute-start.38 = (bf16[288,2304]{1,0:T(8,128)(2,1)}, bf16[288,2304]{1,0:T(8,128)(2,1)S(1)}, u32[]{:S(2)}, u32[]{:S(2)}) collective-permute-start(bf16[288,2304]{1,0:T(8,128)(2,1)} %collective-permute-done.37.refs_4_), channel_id=1, source_target_pairs={{0,16},{4,20},{8,24},{12,28},{16,0},{20,4},{24,8},{28,12},{1,17},{... | collective-permute-start | bytes 3981320 | tf_op jit(solution)/shard_map/ppermute | solution.py:46
  301.1 66.1 %collective-permute-start.41 = (bf16[288,2304]{1,0:T(8,128)(2,1)}, bf16[288,2304]{1,0:T(8,128)(2,1)S(1)}, u32[]{:S(2)}, u32[]{:S(2)}) collective-permute-start(bf16[288,2304]{1,0:T(8,128)(2,1)} %collective-permute-done.39.refs_6_), channel_id=1, source_target_pairs={{0,16},{4,20},{8,24},{12,28},{16,0},{20,4},{24,8},{28,12},{1,17},{... | collective-permute-start | bytes 3981320 | tf_op jit(solution)/shard_map/ppermute | solution.py:46
  308.8 44.2 %collective-permute-start.44 = (bf16[288,1152]{1,0:T(8,128)(2,1)S(1)}, bf16[288,1152]{1,0:T(8,128)(2,1)}, u32[]{:S(2)}, u32[]{:S(2)}) collective-permute-start(bf16[288,1152]{1,0:T(8,128)(2,1)S(1)} %get-tuple-element.235.refs_0_), channel_id=1, source_target_pairs={{0,8},{4,12},{8,0},{12,4},{1,9},{5,13},{9,1},{13,5},{2,10},{6,14},... | collective-permute-start | bytes 1990664 | tf_op jit(solution)/shard_map/ppermute | solution.py:46
  315.0 42.2 %collective-permute-start.43 = (bf16[288,1152]{1,0:T(8,128)(2,1)}, bf16[288,1152]{1,0:T(8,128)(2,1)S(1)}, u32[]{:S(2)}, u32[]{:S(2)}) collective-permute-start(bf16[288,1152]{1,0:T(8,128)(2,1)} %collective-permute-done.42.refs_2_), channel_id=1, source_target_pairs={{0,16},{4,20},{8,24},{12,28},{16,0},{20,4},{24,8},{28,12},{1,17},{... | collective-permute-start | bytes 1990664 | tf_op jit(solution)/shard_map/ppermute | solution.py:46
  315.9 51.3 %collective-permute-start.46 = (bf16[288,1152]{1,0:T(8,128)(2,1)}, bf16[288,1152]{1,0:T(8,128)(2,1)}, u32[]{:S(2)}, u32[]{:S(2)}) collective-permute-start(bf16[288,1152]{1,0:T(8,128)(2,1)} %collective-permute-done.42.refs_2_), channel_id=1, source_target_pairs={{0,8},{4,12},{8,0},{12,4},{1,9},{5,13},{9,1},{13,5},{2,10},{6,14},... | collective-permute-start | bytes 1990664 | tf_op jit(solution)/shard_map/ppermute | solution.py:46
  322.3 46.6 %collective-permute-start.49 = (bf16[128,2304]{1,0:T(8,128)(2,1)S(1)}, bf16[128,2304]{1,0:T(8,128)(2,1)}, u32[]{:S(2)}, u32[]{:S(2)}) collective-permute-start(bf16[128,2304]{1,0:T(8,128)(2,1)S(1)} %get-tuple-element.223), channel_id=1, source_target_pairs={{0,4},{4,0},{8,12},{12,8},{1,5},{5,1},{9,13},{13,9},{2,6},{6,2},{1... | collective-permute-start | bytes 1769480 | tf_op jit(solution)/shard_map/ppermute | solution.py:46
  353.0 43.4 %collective-permute-start.34 = (bf16[256,2304]{1,0:T(8,128)(2,1)}, bf16[256,2304]{1,0:T(8,128)(2,1)}, u32[]{:S(2)}, u32[]{:S(2)}) collective-permute-start(bf16[256,2304]{1,0:T(8,128)(2,1)} %pad_maximum_fusion.3), channel_id=1, source_target_pairs={{0,1},{1,0},{2,3},{3,2},{4,5},{5,4},{6,7},{7,6},{8,9},{9,8},{10,11... | collective-permute-start | bytes 3538952 | tf_op jit(solution)/shard_map/ppermute | solution.py:68
  547.5 31.2 %collective-permute-start.68 = (bf16[288,1152]{1,0:T(8,128)(2,1)S(1)}, bf16[288,1152]{1,0:T(8,128)(2,1)}, u32[]{:S(2)}, u32[]{:S(2)}) collective-permute-start(bf16[288,1152]{1,0:T(8,128)(2,1)S(1)} %get-tuple-element.258), channel_id=1, source_target_pairs={{0,16},{16,0},{1,17},{17,1},{2,18},{18,2},{3,19},{19,3},{4,20},{20... | collective-permute-start | bytes 1990664 | tf_op jit(solution)/shard_map/ppermute | solution.py:46
  549.1 30.5 %collective-permute-start.62 = (bf16[128,2304]{1,0:T(8,128)(2,1)S(1)}, bf16[128,2304]{1,0:T(8,128)(2,1)}, u32[]{:S(2)}, u32[]{:S(2)}) collective-permute-start(bf16[128,2304]{1,0:T(8,128)(2,1)S(1)} %slice.450), channel_id=1, source_target_pairs={{0,2},{1,3},{2,0},{3,1},{4,6},{5,7},{6,4},{7,5},{8,10},{9,11},{10,... | collective-permute-start | bytes 1769480 | tf_op jit(solution)/shard_map/ppermute | solution.py:46
  566.6 52.9 %collective-permute-start.82 = (bf16[288,1152]{1,0:T(8,128)(2,1)S(1)}, bf16[288,1152]{1,0:T(8,128)(2,1)}, u32[]{:S(2)}, u32[]{:S(2)}) collective-permute-start(bf16[288,1152]{1,0:T(8,128)(2,1)S(1)} %get-tuple-element.282), channel_id=1, source_target_pairs={{0,16},{16,0},{1,17},{17,1},{2,18},{18,2},{3,19},{19,3},{4,20},{20... | collective-permute-start | bytes 1990664 | tf_op jit(solution)/shard_map/ppermute | solution.py:46
  567.5 52.1 %collective-permute-start.76 = (bf16[288,1152]{1,0:T(8,128)(2,1)}, bf16[288,1152]{1,0:T(8,128)(2,1)}, u32[]{:S(2)}, u32[]{:S(2)}) collective-permute-start(bf16[288,1152]{1,0:T(8,128)(2,1)} %add_convert_fusion.4), channel_id=1, source_target_pairs={{0,8},{4,12},{8,0},{12,4},{1,9},{5,13},{9,1},{13,5},{2,10},{6,14},... | collective-permute-start | bytes 1990664 | tf_op jit(solution)/shard_map/ppermute | solution.py:46
  578.8 32.1 %collective-permute-start.69 = (bf16[288,1152]{1,0:T(8,128)(2,1)S(1)}, bf16[288,1152]{1,0:T(8,128)(2,1)}, u32[]{:S(2)}, u32[]{:S(2)}) collective-permute-start(bf16[288,1152]{1,0:T(8,128)(2,1)S(1)} %get-tuple-element.259), channel_id=1, source_target_pairs={{0,16},{16,0},{1,17},{17,1},{2,18},{18,2},{3,19},{19,3},{4,20},{20... | collective-permute-start | bytes 1990664 | tf_op jit(solution)/shard_map/ppermute | solution.py:46
  610.9 36.6 %collective-permute-start.70 = (bf16[288,2304]{1,0:T(8,128)(2,1)S(1)}, bf16[288,2304]{1,0:T(8,128)(2,1)S(1)}, u32[]{:S(2)}, u32[]{:S(2)}) collective-permute-start(bf16[288,2304]{1,0:T(8,128)(2,1)S(1)} %get-tuple-element.260), channel_id=1, source_target_pairs={{0,16},{16,0},{1,17},{17,1},{2,18},{18,2},{3,19},{19,3},{4,20},{20... | collective-permute-start | bytes 3981320 | tf_op jit(solution)/shard_map/ppermute | solution.py:46
  612.2 31.8 %collective-permute-start.71 = (bf16[288,1152]{1,0:T(8,128)(2,1)}, bf16[288,1152]{1,0:T(8,128)(2,1)S(1)}, u32[]{:S(2)}, u32[]{:S(2)}) collective-permute-start(bf16[288,1152]{1,0:T(8,128)(2,1)} %add_convert_fusion.5), channel_id=1, source_target_pairs={{0,8},{4,12},{8,0},{12,4},{1,9},{5,13},{9,1},{13,5},{2,10},{6,14},... | collective-permute-start | bytes 1990664 | tf_op jit(solution)/shard_map/ppermute | solution.py:46
  622.1 49.2 %collective-permute-start.83 = (bf16[288,2304]{1,0:T(8,128)(2,1)S(1)}, bf16[288,2304]{1,0:T(8,128)(2,1)S(1)}, u32[]{:S(2)}, u32[]{:S(2)}) collective-permute-start(bf16[288,2304]{1,0:T(8,128)(2,1)S(1)} %get-tuple-element.283), channel_id=1, source_target_pairs={{0,16},{16,0},{1,17},{17,1},{2,18},{18,2},{3,19},{19,3},{4,20},{20... | collective-permute-start | bytes 3981320 | tf_op jit(solution)/shard_map/ppermute | solution.py:46
  647.4 37.9 %collective-permute-start.67 = (bf16[256,2304]{1,0:T(8,128)(2,1)}, bf16[256,2304]{1,0:T(8,128)(2,1)}, u32[]{:S(2)}, u32[]{:S(2)}) collective-permute-start(bf16[256,2304]{1,0:T(8,128)(2,1)} %pad_maximum_fusion.7), channel_id=1, source_target_pairs={{0,1},{1,0},{2,3},{3,2},{4,5},{5,4},{6,7},{7,6},{8,9},{9,8},{10,11... | collective-permute-start | bytes 3538952 | tf_op jit(solution)/shard_map/ppermute | solution.py:68
  648.8 119.0 %collective-permute-start.87 = (bf16[288,2304]{1,0:T(8,128)(2,1)}, bf16[288,2304]{1,0:T(8,128)(2,1)}, u32[]{:S(2)}, u32[]{:S(2)}) collective-permute-start(bf16[288,2304]{1,0:T(8,128)(2,1)} %get-tuple-element.290), channel_id=1, source_target_pairs={{0,16},{16,0},{1,17},{17,1},{2,18},{18,2},{3,19},{19,3},{4,20},{20... | collective-permute-start | bytes 3981320 | tf_op jit(solution)/shard_map/ppermute | solution.py:46
  649.6 61.0 %collective-permute-start.72 = (bf16[288,2304]{1,0:T(8,128)(2,1)}, bf16[288,2304]{1,0:T(8,128)(2,1)}, u32[]{:S(2)}, u32[]{:S(2)}) collective-permute-start(bf16[288,2304]{1,0:T(8,128)(2,1)} %add_convert_fusion.2), channel_id=1, source_target_pairs={{0,8},{4,12},{8,0},{12,4},{1,9},{5,13},{9,1},{13,5},{2,10},{6,14},... | collective-permute-start | bytes 3981320 | tf_op jit(solution)/shard_map/ppermute | solution.py:46
  671.4 96.4 %collective-permute-start.84 = (bf16[288,2304]{1,0:T(8,128)(2,1)}, bf16[288,2304]{1,0:T(8,128)(2,1)}, u32[]{:S(2)}, u32[]{:S(2)}) collective-permute-start(bf16[288,2304]{1,0:T(8,128)(2,1)} %get-tuple-element.284), channel_id=1, source_target_pairs={{0,16},{16,0},{1,17},{17,1},{2,18},{18,2},{3,19},{19,3},{4,20},{20... | collective-permute-start | bytes 3981320 | tf_op jit(solution)/shard_map/ppermute | solution.py:46
  719.7 31.2 %collective-permute-start.78 = (bf16[2,1,512,256]{3,2,1,0:T(8,128)(2,1)}, bf16[2,1,512,256]{3,2,1,0:T(8,128)(2,1)}, u32[]{:S(2)}, u32[]{:S(2)}) collective-permute-start(bf16[2,1,512,256]{3,2,1,0:T(8,128)(2,1)} %fusion.99), channel_id=1, source_target_pairs={{0,8},{4,12},{8,0},{12,4},{1,9},{5,13},{9,1},{13,5},{2,10},{6,14},... | collective-permute-start | bytes 1572872 | tf_op jit(solution)/shard_map/ppermute | solution.py:46
  730.5 38.7 %collective-permute-start.96 = (bf16[2,64,2304]{2,1,0:T(8,128)(2,1)}, bf16[2,64,2304]{2,1,0:T(8,128)(2,1)S(1)}, u32[]{:S(2)}, u32[]{:S(2)}) collective-permute-start(bf16[2,64,2304]{2,1,0:T(8,128)(2,1)} %get-tuple-element.306), channel_id=1, source_target_pairs={{0,3},{1,2},{2,1},{3,0},{4,7},{5,6},{6,5},{7,4},{8,11},{9,10},{10,... | collective-permute-start | bytes 1769480 | tf_op jit(solution)/shard_map/ppermute | solution.py:46
  730.6 42.7 %collective-permute-start.80 = (bf16[2,64,2304]{2,1,0:T(8,128)(2,1)}, bf16[2,64,2304]{2,1,0:T(8,128)(2,1)S(1)}, u32[]{:S(2)}, u32[]{:S(2)}) collective-permute-start(bf16[2,64,2304]{2,1,0:T(8,128)(2,1)} %get-tuple-element.274), channel_id=1, source_target_pairs={{0,2},{1,3},{2,0},{3,1},{4,6},{5,7},{6,4},{7,5},{8,10},{9,11},{10,... | collective-permute-start | bytes 1769480 | tf_op jit(solution)/shard_map/ppermute | solution.py:46
  767.8 57.2 %collective-permute-start.89 = (bf16[288,2304]{1,0:T(8,128)(2,1)}, bf16[288,2304]{1,0:T(8,128)(2,1)}, u32[]{:S(2)}, u32[]{:S(2)}) collective-permute-start(bf16[288,2304]{1,0:T(8,128)(2,1)} %add_convert_fusion.1), channel_id=1, source_target_pairs={{0,8},{4,12},{8,0},{12,4},{1,9},{5,13},{9,1},{13,5},{2,10},{6,14},... | collective-permute-start | bytes 3981320 | tf_op jit(solution)/shard_map/ppermute | solution.py:46
  773.3 59.5 %collective-permute-start.108 = (bf16[288,2304]{1,0:T(8,128)(2,1)}, bf16[288,2304]{1,0:T(8,128)(2,1)S(1)}, u32[]{:S(2)}, u32[]{:S(2)}) collective-permute-start(bf16[288,2304]{1,0:T(8,128)(2,1)} %add_convert_fusion), channel_id=1, source_target_pairs={{0,4},{4,0},{8,12},{12,8},{1,5},{5,1},{9,13},{13,9},{2,6},{6,2},{1... | collective-permute-start | bytes 3981320 | tf_op jit(solution)/shard_map/ppermute | solution.py:46
  803.5 80.4 %collective-permute-start.79 = (bf16[256,2304]{1,0:T(8,128)(2,1)S(1)}, bf16[256,2304]{1,0:T(8,128)(2,1)S(1)}, u32[]{:S(2)}, u32[]{:S(2)}) collective-permute-start(bf16[256,2304]{1,0:T(8,128)(2,1)S(1)} %slice.309), channel_id=1, source_target_pairs={{0,1},{1,0},{2,3},{3,2},{4,5},{5,4},{6,7},{7,6},{8,9},{9,8},{10,11... | collective-permute-start | bytes 3538952 | tf_op jit(solution)/shard_map/ppermute | solution.py:68
  809.3 42.4 %collective-permute-start.93 = (bf16[288,1024]{1,0:T(8,128)(2,1)S(1)}, bf16[288,1024]{1,0:T(8,128)(2,1)}, u32[]{:S(2)}, u32[]{:S(2)}) collective-permute-start(bf16[288,1024]{1,0:T(8,128)(2,1)S(1)} %get-tuple-element.300), channel_id=1, source_target_pairs={{0,4},{12,8},{1,5},{13,9},{2,6},{14,10},{3,7},{15,11},{16,20},{28,... | collective-permute-start | bytes 1769480 | tf_op jit(solution)/shard_map/ppermute | solution.py:46
  821.6 33.1 %collective-permute-start.102 = (bf16[64,2304]{1,0:T(8,128)(2,1)S(1)}, bf16[64,2304]{1,0:T(8,128)(2,1)S(1)}, u32[]{:S(2)}, u32[]{:S(2)}) collective-permute-start(bf16[64,2304]{1,0:T(8,128)(2,1)S(1)} %get-tuple-element.323), channel_id=1, source_target_pairs={{0,16},{16,0},{1,17},{17,1},{2,18},{18,2},{3,19},{19,3},{4,20},{20... | collective-permute-start | bytes 884744 | tf_op jit(solution)/shard_map/ppermute | solution.py:46
  824.9 31.8 %collective-permute-start.100 = (bf16[64,2304]{1,0:T(8,128)(2,1)S(1)}, bf16[64,2304]{1,0:T(8,128)(2,1)}, u32[]{:S(2)}, u32[]{:S(2)}) collective-permute-start(bf16[64,2304]{1,0:T(8,128)(2,1)S(1)} %get-tuple-element.319), channel_id=1, source_target_pairs={{0,16},{16,0},{1,17},{17,1},{2,18},{18,2},{3,19},{19,3},{4,20},{20... | collective-permute-start | bytes 884744 | tf_op jit(solution)/shard_map/ppermute | solution.py:46
  854.6 43.1 %collective-permute-start.94 = (bf16[288,1024]{1,0:T(8,128)(2,1)S(1)}, bf16[288,1024]{1,0:T(8,128)(2,1)S(1)}, u32[]{:S(2)}, u32[]{:S(2)}) collective-permute-start(bf16[288,1024]{1,0:T(8,128)(2,1)S(1)} %add_convert_fusion.6), channel_id=1, source_target_pairs={{0,8},{4,12},{8,0},{12,4},{1,9},{5,13},{9,1},{13,5},{2,10},{6,14},... | collective-permute-start | bytes 1769480 | tf_op jit(solution)/shard_map/ppermute | solution.py:46
  885.0 46.5 %collective-permute-start.101 = (bf16[64,2304]{1,0:T(8,128)(2,1)}, bf16[64,2304]{1,0:T(8,128)(2,1)}, u32[]{:S(2)}, u32[]{:S(2)}) collective-permute-start(bf16[64,2304]{1,0:T(8,128)(2,1)} %get-tuple-element.320), channel_id=1, source_target_pairs={{0,16},{16,0},{1,17},{17,1},{2,18},{18,2},{3,19},{19,3},{4,20},{20... | collective-permute-start | bytes 884744 | tf_op jit(solution)/shard_map/ppermute | solution.py:46
  892.0 39.5 %collective-permute-start.107 = (bf16[64,2304]{1,0:T(8,128)(2,1)}, bf16[64,2304]{1,0:T(8,128)(2,1)}, u32[]{:S(2)}, u32[]{:S(2)}) collective-permute-start(bf16[64,2304]{1,0:T(8,128)(2,1)} %add_convert_fusion.10), channel_id=1, source_target_pairs={{0,8},{4,12},{8,0},{12,4},{1,9},{5,13},{9,1},{13,5},{2,10},{6,14},... | collective-permute-start | bytes 884744 | tf_op jit(solution)/shard_map/ppermute | solution.py:46
  900.5 31.1 %collective-permute-start.103 = (bf16[64,2304]{1,0:T(8,128)(2,1)}, bf16[64,2304]{1,0:T(8,128)(2,1)}, u32[]{:S(2)}, u32[]{:S(2)}) collective-permute-start(bf16[64,2304]{1,0:T(8,128)(2,1)} %get-tuple-element.325), channel_id=1, source_target_pairs={{0,4},{4,8},{8,12},{1,5},{5,9},{9,13},{2,6},{6,10},{10,14},{3,7},{... | collective-permute-start | bytes 884744 | tf_op jit(solution)/shard_map/ppermute | solution.py:46
  (224 other events, 3121.7 us)
